TPU v7x, 32 devices: a whole 2x2x4 slice. The times are simulated.
32 devices in a mesh: row: 4 (over y, x), head: 8 (over z, core).
Axes of the slice: x: 2, y: 2, z: 4, core: 2. Of those that a mesh axis runs over, the one named last changes fastest.
Arguments:
- tokens: bfloat16 [8192, 2048], P(('row', 'head')), may hold values from -6 to 6
- in_weight: bfloat16 [2048, 8512], P(('row', 'head')), may hold values from -0.125 to 0.125
- norm_gain: bfloat16 [2048], P(('row', 'head')), may hold values from 0.5 to 1.5
- out_weight: bfloat16 [4096, 2048], P(('row', 'head')), may hold values from -0.09375 to 0.09375
- gate_gain: bfloat16 [4096], P(('row', 'head')), may hold values from 0.5 to 1.5
- conv_weight: float32 [4, 4352], replicated, may hold values from -3 to 3
- conv_bias: float32 [4352], replicated, may hold values from -3 to 3
- dt_bias: float32 [64], replicated, may hold values from -7 to -1
- a_log: float32 [64], replicated, may hold values from -1 to 2.5
- skip_gain: float32 [64], replicated, may hold values from 0.5 to 1.5
- boundary: int32 [4, 2048], P('row'), may hold values 0 or 1
- fill: int32 [4], P('row'), may hold values from 1024 to 2048
- cotangent: bfloat16 [8192, 2048], P(('row', 'head')), may hold values from -6 to 6
Outputs:
- output: bfloat16 [8192, 2048], P(('row', 'head'))
- input_grad: bfloat16 [8192, 2048], P(('row', 'head'))
- in_weight_grad: float32 [2048, 8512], P(('row', 'head'))
- norm_gain_grad: float32 [2048], P(('row', 'head'))
- out_weight_grad: float32 [4096, 2048], P(('row', 'head'))
- gate_gain_grad: float32 [4096], P(('row', 'head'))
- conv_weight_grad: float32 [4, 4352], replicated
- conv_bias_grad: float32 [4352], replicated
- dt_bias_grad: float32 [64], replicated
- a_log_grad: float32 [64], replicated
- skip_gain_grad: float32 [64], replicated
All inputs are finite; a program needn't handle non-finite values. No bound on the sum of `boundary` on one device may be relied on, other than what follows from the above.
Results may differ from a plain program's by a relative error of at most 0.011.
Values may be sent and summed in bfloat16 or wider, within the bound.
No kernel may reach another device: no remote copies, remote signals or barrier semaphores. Data moves between devices by JAX's collectives and lax.ppermute only.
A program may use at most 384 MiB of HBM per device.

v0:
```python
from functools import partial

import jax
import jax.numpy as jnp
from jax import lax
from jax.sharding import PartitionSpec as P

HEADS = 64
HDIM = 64
NSTATE = 128
SPAN = 256
DIN = 4096


epsilon = 1e-05
highest = lax.Precision.HIGHEST


def row_norm(values):
    return values * lax.rsqrt(jnp.mean(values * values, axis=-1, keepdims=True) + epsilon)


def gate_piece(mixed_heads, gate_values):
    return row_norm(mixed_heads * jax.nn.silu(gate_values))


def conv_piece(raw_values, tap_weight, tap_bias, segments):
    tap_count = tap_weight.shape[0]
    result = tap_bias + tap_weight[0] * raw_values
    for offset in range(1, tap_count):
        shifted = jnp.pad(raw_values, ((0, 0), (offset, 0), (0, 0)))[:, :-offset]
        shifted_seg = jnp.pad(segments, ((0, 0), (offset, 0)), constant_values=-1)[:, :-offset]
        usable = (shifted_seg == segments).astype(raw_values.dtype)
        result = result + tap_weight[offset] * shifted * usable[:, :, None]
    return jax.nn.silu(result)


def block_step(decay_rate, memory, inputs):
    values, step_sizes, keys_in, queries, segments, previous = inputs
    length = step_sizes.shape[1]
    log_decay = jnp.cumsum(step_sizes * decay_rate, axis=1)
    causal = jnp.arange(length)[:, None] >= jnp.arange(length)[None, :]
    linked = jnp.logical_and(segments[:, :, None] == segments[:, None, :], causal[None])[..., None]
    spread = log_decay[:, :, None, :] - log_decay[:, None, :, :]
    decays = jnp.where(linked, jnp.exp(jnp.where(linked, spread, 0.0)), 0.0)
    scores = jnp.einsum("rtn,run->rtu", queries, keys_in, precision=highest)
    scaled_values = values * step_sizes[..., None]
    within = jnp.einsum(
        "rtuh,ruhp->rthp", decays * scores[..., None], scaled_values, precision=highest
    )
    carried = (segments == previous[:, None]).astype(log_decay.dtype)
    reading = jnp.einsum("rtn,rhpn->rthp", queries, memory, precision=highest)
    across = reading * (jnp.exp(log_decay) * carried[..., None])[..., None]
    ending = (segments == segments[:, -1:]).astype(log_decay.dtype)
    to_end = jnp.exp(log_decay[:, -1:, :] - log_decay) * ending[..., None]
    local_state = jnp.einsum(
        "ruh,ruhp,run->rhpn", to_end, scaled_values, keys_in, precision=highest
    )
    survive = (
        jnp.exp(log_decay[:, -1, :])
        * (segments[:, -1] == previous).astype(log_decay.dtype)[:, None]
    )
    return (survive[:, :, None, None] * memory + local_state, within + across)


def ssd_scan(values, step_sizes, decay_rate, keys_in, queries, segments, span_len):
    row_count, seq_len, head_count, head_dim = values.shape
    block_count = seq_len // span_len

    def blocks(tensor):
        return jnp.moveaxis(
            tensor.reshape((row_count, block_count, span_len) + tensor.shape[2:]), 1, 0
        )

    last_ids = segments.reshape(row_count, block_count, span_len)[:, :, -1]
    previous = jnp.concatenate([jnp.full((row_count, 1), -1, jnp.int32), last_ids[:, :-1]], axis=1)
    stepper = jax.checkpoint(partial(block_step, decay_rate))
    memory = jnp.zeros((row_count, head_count, head_dim, keys_in.shape[-1]), values.dtype)
    last_memory, outputs = lax.scan(
        stepper,
        memory,
        (
            blocks(values),
            blocks(step_sizes),
            blocks(keys_in),
            blocks(queries),
            blocks(segments),
            jnp.moveaxis(previous, 1, 0),
        ),
    )
    return jnp.moveaxis(outputs, 0, 1).reshape(row_count, seq_len, head_count, head_dim)


def ssd_piece(
    conv_values,
    raw_steps,
    step_bias,
    decay_log,
    skip_heads,
    segments,
    fill_mask,
    width,
    state_size,
    span_len,
):
    row_count, seq_len, head_count = raw_steps.shape
    head_dim = width // head_count
    values = conv_values[..., :width].reshape(row_count, seq_len, head_count, head_dim)
    keys_in = conv_values[..., width : width + state_size]
    queries = conv_values[..., width + state_size :]
    step_sizes = jax.nn.softplus(raw_steps + step_bias)
    decay_rate = -jnp.exp(decay_log)
    core = ssd_scan(values, step_sizes, decay_rate, keys_in, queries, segments, span_len)
    mixed = (core + skip_heads[:, None] * values) * fill_mask[:, :, None, None]
    return mixed.reshape(row_count, seq_len, width)


def shards(
    tokens,
    in_weight,
    norm_gain,
    out_weight,
    gate_gain,
    conv_weight,
    conv_bias,
    dt_bias,
    a_log,
    skip_gain,
    boundary,
    fill,
    cotangent,
):
    contract = (((1,), (1,)), ((), ()))
    transpose = (((0,), (0,)), ((), ()))
    activations = tokens.astype(jnp.float32)
    normed, norm_back = jax.vjp(row_norm, activations)
    weight_rows = lax.all_gather(in_weight, ("row", "head"), axis=0, tiled=True)
    gain_rows = lax.all_gather(norm_gain, ("row", "head"), axis=0, tiled=True)
    columns = normed
    scaled = (columns * gain_rows.astype(jnp.float32)).astype(jnp.bfloat16)
    running = jnp.dot(scaled, weight_rows, preferred_element_type=jnp.float32)
    projected = running
    projected_in = scaled
    gate_values = projected[:, :DIN]
    value_send = projected[:, DIN : 2 * DIN].astype(jnp.bfloat16)
    matrix_send = projected[:, 2 * DIN : 2 * DIN + 2 * NSTATE].astype(jnp.bfloat16)
    step_send = projected[:, 2 * DIN + 2 * NSTATE :].astype(jnp.bfloat16)
    value_heads, step_heads = (
        lax.all_to_all(value_send, "head", split_axis=1, concat_axis=0, tiled=True),
        lax.all_to_all(step_send, "head", split_axis=1, concat_axis=0, tiled=True),
    )
    matrix_rows = lax.all_gather(matrix_send, "head", axis=0, tiled=True)
    row_count, seq_len = boundary.shape
    segments = jnp.cumsum(boundary, axis=1)
    fill_mask = (jnp.arange(seq_len)[None, :] < fill[:, None]).astype(jnp.float32)
    head_index = lax.axis_index("head")
    head_local = HEADS // lax.axis_size("head")
    width = head_local * HDIM
    local_weight = jnp.concatenate(
        [lax.dynamic_slice_in_dim(conv_weight, head_index * width, width, 1), conv_weight[:, DIN:]],
        axis=1,
    )
    local_bias = jnp.concatenate(
        [lax.dynamic_slice_in_dim(conv_bias, head_index * width, width, 0), conv_bias[DIN:]], axis=0
    )
    local_step = lax.dynamic_slice_in_dim(dt_bias, head_index * head_local, head_local, 0)
    local_decay = lax.dynamic_slice_in_dim(a_log, head_index * head_local, head_local, 0)
    local_skip = lax.dynamic_slice_in_dim(skip_gain, head_index * head_local, head_local, 0)
    conv_raw = jnp.concatenate(
        [value_heads.astype(jnp.float32), matrix_rows.astype(jnp.float32)], axis=1
    ).reshape(row_count, seq_len, width + 2 * NSTATE)
    conv_out, conv_back = jax.vjp(
        partial(conv_piece, segments=segments), conv_raw, local_weight, local_bias
    )
    conv_values = conv_out.astype(jnp.bfloat16).astype(jnp.float32)
    raw_steps = step_heads.astype(jnp.float32).reshape(row_count, seq_len, head_local)
    mixed, ssd_back = jax.vjp(
        partial(
            ssd_piece,
            segments=segments,
            fill_mask=fill_mask,
            width=width,
            state_size=NSTATE,
            span_len=SPAN,
        ),
        conv_values,
        raw_steps,
        local_step,
        local_decay,
        local_skip,
    )
    mixed_send = mixed.reshape(row_count * seq_len, width).astype(jnp.bfloat16)
    mixed_tokens = lax.all_to_all(mixed_send, "head", split_axis=0, concat_axis=1, tiled=True)
    gated, gate_back = jax.vjp(gate_piece, mixed_tokens.astype(jnp.float32), gate_values)
    weight_rows = lax.all_gather(out_weight, ("row", "head"), axis=0, tiled=True)
    gain_rows = lax.all_gather(gate_gain, ("row", "head"), axis=0, tiled=True)
    columns = gated
    scaled = (columns * gain_rows.astype(jnp.float32)).astype(jnp.bfloat16)
    running = jnp.dot(scaled, weight_rows, preferred_element_type=jnp.float32)
    output = (activations + running).astype(jnp.bfloat16)
    weight_rows, gain_rows = lax.all_gather(
        (out_weight, gate_gain), ("row", "head"), axis=0, tiled=True
    )
    partial_grad = lax.dot_general(
        cotangent, weight_rows, contract, preferred_element_type=jnp.float32
    )
    stacked = jnp.stack([partial_grad, partial_grad * gain_rows.astype(jnp.float32)])
    grad_out_in = stacked[0]
    grad_gated = stacked[1]
    columns = scaled
    out_weight_grad = lax.psum_scatter(
        lax.dot_general(columns, cotangent, transpose, preferred_element_type=jnp.float32),
        ("row", "head"),
        scatter_dimension=0,
        tiled=True,
    )
    gate_gain_grad = jnp.sum(grad_out_in * gated, axis=0)
    grad_mixed, grad_gate_values = gate_back(grad_gated)
    grad_heads = lax.all_to_all(
        grad_mixed.astype(jnp.bfloat16), "head", split_axis=1, concat_axis=0, tiled=True
    )
    grad_conv_values, grad_raw_steps, grad_step, grad_decay, grad_skip = ssd_back(
        grad_heads.astype(jnp.float32).reshape(row_count, seq_len, width)
    )
    grad_conv_raw, grad_weight_local, grad_bias_local = conv_back(grad_conv_values)
    grad_conv_raw = grad_conv_raw.reshape(row_count * seq_len, width + 2 * NSTATE)
    value_back = grad_conv_raw[:, :width].astype(jnp.bfloat16)
    step_back = grad_raw_steps.reshape(row_count * seq_len, head_local).astype(jnp.bfloat16)
    grad_value_tok, grad_step_tok = (
        lax.all_to_all(value_back, "head", split_axis=0, concat_axis=1, tiled=True),
        lax.all_to_all(step_back, "head", split_axis=0, concat_axis=1, tiled=True),
    )
    grad_matrix_tok = lax.psum_scatter(
        grad_conv_raw[:, width:], "head", scatter_dimension=0, tiled=True
    ).astype(jnp.bfloat16)
    grad_projected = jnp.concatenate(
        [grad_gate_values.astype(jnp.bfloat16), grad_value_tok, grad_matrix_tok, grad_step_tok],
        axis=1,
    )
    columns = projected_in
    in_weight_grad = lax.psum_scatter(
        lax.dot_general(columns, grad_projected, transpose, preferred_element_type=jnp.float32),
        ("row", "head"),
        scatter_dimension=0,
        tiled=True,
    )
    weight_rows, gain_rows = lax.all_gather(
        (in_weight, norm_gain), ("row", "head"), axis=0, tiled=True
    )
    partial_grad = lax.dot_general(
        grad_projected, weight_rows, contract, preferred_element_type=jnp.float32
    )
    stacked_in = jnp.stack([partial_grad, partial_grad * gain_rows.astype(jnp.float32)])
    grad_in = stacked_in[0]
    grad_normed = stacked_in[1]
    norm_gain_grad = jnp.sum(grad_in * normed, axis=0)
    (grad_tokens,) = norm_back(grad_normed)
    input_grad = (cotangent.astype(jnp.float32) + grad_tokens).astype(jnp.bfloat16)
    norm_owned, gate_owned = (
        lax.psum_scatter(norm_gain_grad, ("row", "head"), scatter_dimension=0, tiled=True),
        lax.psum_scatter(gate_gain_grad, ("row", "head"), scatter_dimension=0, tiled=True),
    )
    conv_grad = jnp.zeros(conv_weight.shape, jnp.float32)
    conv_grad = lax.dynamic_update_slice_in_dim(
        conv_grad, grad_weight_local[:, :width], head_index * width, 1
    )
    conv_grad = lax.dynamic_update_slice_in_dim(conv_grad, grad_weight_local[:, width:], DIN, 1)
    bias_grad = jnp.zeros(conv_bias.shape, jnp.float32)
    bias_grad = lax.dynamic_update_slice_in_dim(
        bias_grad, grad_bias_local[:width], head_index * width, 0
    )
    bias_grad = lax.dynamic_update_slice_in_dim(bias_grad, grad_bias_local[width:], DIN, 0)
    step_grad = lax.dynamic_update_slice_in_dim(
        jnp.zeros((HEADS,), jnp.float32), grad_step, head_index * head_local, 0
    )
    decay_grad = lax.dynamic_update_slice_in_dim(
        jnp.zeros((HEADS,), jnp.float32), grad_decay, head_index * head_local, 0
    )
    skip_grad = lax.dynamic_update_slice_in_dim(
        jnp.zeros((HEADS,), jnp.float32), grad_skip, head_index * head_local, 0
    )
    summed = lax.psum((conv_grad, bias_grad, step_grad, decay_grad, skip_grad), ("row", "head"))
    return (
        output,
        input_grad,
        in_weight_grad,
        norm_owned,
        out_weight_grad,
        gate_owned,
        summed[0],
        summed[1],
        summed[2],
        summed[3],
        summed[4],
    )


def solution(mesh):
    return jax.shard_map(
        shards,
        mesh=mesh,
        in_specs=(
            P(("row", "head"), None),
            P(("row", "head"), None),
            P(("row", "head")),
            P(("row", "head"), None),
            P(("row", "head")),
            P(),
            P(),
            P(),
            P(),
            P(),
            P("row", None),
            P("row"),
            P(("row", "head"), None),
        ),
        out_specs=(
            P(("row", "head"), None),
            P(("row", "head"), None),
            P(("row", "head"), None),
            P(("row", "head")),
            P(("row", "head"), None),
            P(("row", "head")),
            P(),
            P(),
            P(),
            P(),
            P(),
        ),
        check_vma=False,
    )
```

profile of v0, /device:TPU:0, one launch (start us, length us, event | category | flops | bytes accessed | tf_op | source)
XLA Modules:
  0.0 2301.4 jit_solution(7869668411101427993)
XLA Ops:
  8.8 43.9 %all-reduce.18 = bf16[2048]{0:T(1024)(128)(2,1)S(1)} all-reduce(bf16[2048]{0:T(1024)(128)(2,1)S(1)} %dynamic-update-slice), channel_id=1, replica_groups=mesh['row'=4,'head'=8] {'row','head'}, use_global_device_ids=true, to_apply=%add.18 | all-reduce | flops 2048 | bytes 8192
  54.9 162.2 %all-gather.5.cloned.1.call-done = bf16[2048,8512]{1,0:T(8,128)(2,1)} async-done(((bf16[64,8512]{1,0:T(8,128)(2,1)}), bf16[2048,8512]{1,0:T(8,128)(2,1)}) %all-gather.5.cloned.1.call-update) | async-done | bytes 34865168 | tf_op jit(solution)/shard_map/all_gather | solution.py:137
  217.1 22.1 fusion.184
  269.0 48.1 %all-to-all-done.1 = bf16[256,8,512]{0,2,1:T(8,128)(2,1)} async-done(((bf16[256,8,512]{0,2,1:T(8,128)(2,1)}), bf16[256,8,512]{0,2,1:T(8,128)(2,1)}, u32[]{:S(2)}, u32[]{:S(2)}) %all-to-all-start.1) | async-done | bytes 2097184 | tf_op jit(solution)/shard_map/all_to_all | solution.py:149
  354.4 119.3 %while.42 = (s32[]{:T(128)}, f32[1,8,64,128]{3,2,1,0:T(8,128)S(1)}, f32[8,1,256,8,64]{2,4,3,1,0:T(8,128)}, f32[8,1,8,64,128]{4,3,2,1,0:T(8,128)}, f32[8,1,256,8]...) while((s32[]{:T(128)}, f32[1,8,64,128]{3,2,1,0:T(8,128)S(1)}, ...), condition=%wide.region_6.7_spmd.clone, body=%wide.region_3.6_spmd.clone.sunk | while | flops 909519872 | bytes 5282278 | solution.py:79
  483.9 77.9 %all-gather = bf16[32,1,128]{2,1,0:T(2,128)(2,1)S(1)} all-gather(bf16[1,1,128]{2,1,0:T(2,128)(2,1)S(1)} %bitcast.726), channel_id=1, replica_groups=mesh['row'=4,'head'=8] {'row','head'}, dimensions={0}, use_global_device_ids=true | all-gather | bytes 8448 | tf_op jit(solution)/shard_map/all_gather | solution.py:196
  565.3 11.3 multiply_reduce_fusion.7
  587.1 48.8 %all-to-all-done.3 = bf16[256,8,512]{0,2,1:T(8,128)(2,1)S(1)} async-done(((bf16[256,8,512]{0,2,1:T(8,128)(2,1)}), bf16[256,8,512]{0,2,1:T(8,128)(2,1)S(1)}, u32[]{:S(2)}, u32[]{:S(2)}) %all-to-all-start.3) | async-done | bytes 2097184 | tf_op jit(solution)/shard_map/all_to_all | solution.py:219
  645.2 316.9 %while.43 = (s32[]{:T(128)}, f32[8]{0:T(128)S(1)}, f32[1,8,64,128]{3,2,1,0:T(8,128)S(1)}, f32[8,1,256,8,64]{2,0,4,3,1:T(8,128)}, f32[8,1,256,8]{2,3,1,0:T(8,128)...) while((s32[]{:T(128)}, f32[8]{0:T(128)S(1)}, ...), condition=%wide.region_22.23_spmd.clone, body=%wide.region_9.22_spmd.clone.sunk | while | flops 2124850176 | bytes 18511416 | solution.py:79
  665.1 12.7 dynamic_update_slice.104
  704.7 12.7 dynamic_update_slice.104
  744.2 12.7 dynamic_update_slice.104
  783.8 12.7 dynamic_update_slice.104
  823.3 12.7 dynamic_update_slice.104
  862.8 12.7 dynamic_update_slice.104
  902.4 12.7 dynamic_update_slice.104
  941.9 12.7 dynamic_update_slice.104
  1016.2 13.5 fusion.189
  1049.5 45.1 %all-to-all-done.4 = bf16[8,256,512]{1,2,0:T(8,128)(2,1)} async-done(((bf16[8,256,512]{1,2,0:T(8,128)(2,1)}), bf16[8,256,512]{1,2,0:T(8,128)(2,1)}, u32[]{:S(2)}, u32[]{:S(2)}) %all-to-all-start.4) | async-done | bytes 2097184 | tf_op jit(solution)/shard_map/all_to_all | solution.py:230
  1094.6 26.7 %fusion.150 = f32[2048,8512]{1,0:T(8,128)} fusion(bf16[256,64]{0,1:T(8,128)(2,1)S(1)} %bitcast.703, bf16[256,256]{0,1:T(8,128)(2,1)S(1)} %convert_element_type.230, bf16[256,4096]{0,1:T(8,128)(2,1)} %bitcast.34, bf16[256,4096]{0,1:T(8,128)(2,1)} %get-tuple-element.840, bf16[256,2048]{1,0:T(8,128)(2,1)S(1)} %copy-done.5, f32[2048]{0:T(1024)S(1)} %copy-done.13, ...), kind=kOutput, calls=%fused_computation.250 | convolution fusion | flops 8945008640 | bytes 75146240 | tf_op jit(solution)/shard_map/dot_general | solution.py:242
  1132.1 26.9 %fusion.145 = (f32[2048]{0:T(1024)S(1)}, f32[256]{0:T(256)S(1)}, f32[256,2048]{1,0:T(8,128)}) fusion(bf16[256,2048]{1,0:T(8,128)(2,1)S(1)} %copy-done.5, f32[256]{0:T(256)S(1)} %copy-done.17, f32[2048]{0:T(1024)S(1)} %copy-done.13, bf16[2048,8512]{1,0:T(8,128)(2,1)} %all-gather.5.cloned.1.call-done, bf16[256,64]{0,1:T(8,128)(2,1)S(1)} %bitcast.704, ...), kind=kOutput, calls=%fused_computation.242 | convolution fusion | flops 8946579456 | bytes 42387456 | tf_op jit(solution)/shard_map/dot_general | solution.py:250
  1159.0 38.2 %all-reduce.21 = (f32[2048]{0:T(1024)S(1)}, f32[4096]{0:T(1024)S(1)}, f32[4352]{0:T(1024)}, f32[64]{0:T(128)}, f32[64]{0:T(128)}, /*index=5*/f32[64]{0:T(128)}) all-reduce(f32[2048]{0:T(1024)S(1)} %get-tuple-element.751, f32[4096]{0:T(1024)S(1)} %copy-done.19, ...), channel_id=4, replica_groups=mesh['row'=4,'head'=8] {'row','head'}, use_global_device_ids=true, to_apply=%region_27.28.clone | all-reduce | flops 10688 | bytes 85504
  1201.6 349.4 %reduce-scatter.8.cloned.1.call-done = f32[128,2048]{1,0:T(8,128)} async-done(((f32[4096,2048]{1,0:T(8,128)}), f32[128,2048]{1,0:T(8,128)}) %reduce-scatter.8.cloned.1.call-update) | async-done | bytes 1048592 | tf_op jit(solution)/shard_map/reduce_scatter | solution.py:211
  1551.1 741.5 %reduce-scatter.6.cloned.1.call-done = f32[64,8512]{1,0:T(8,128)} async-done(((f32[2048,8512]{1,0:T(8,128)}), f32[64,8512]{1,0:T(8,128)}) %reduce-scatter.6.cloned.1.call-update) | async-done | bytes 2179088 | tf_op jit(solution)/shard_map/reduce_scatter | solution.py:241
  (743 shorter events, 504.6 us)
Async XLA Ops:
  7.2 209.9 %all-gather.5.cloned.1.call-start = ((), (), s32[]{:S(2)}) async-start(), calls=%async_computation.9 | async-start | bytes 36225024 | tf_op jit(solution)/shard_map/all_gather | solution.py:137
  7.9 258.0 %all-gather.7.cloned.1.call-start = ((), (), s32[]{:S(2)}) async-start(), calls=%async_computation.10 | async-start | bytes 1179648 | tf_op jit(solution)/shard_map/all_gather | solution.py:152
  52.8 186.4 %copy-start.12 = (f32[2048]{0:T(1024)}, f32[2048]{0:T(1024)S(1)}, u32[]{:S(2)}) copy-start(f32[2048]{0:T(1024)S(1)} %convert_element_type.204) | copy-start | bytes 24580
  54.9 184.3 %copy-start.16 = (f32[256]{0:T(256)}, f32[256]{0:T(256)S(1)}, u32[]{:S(2)}) copy-start(f32[256]{0:T(256)S(1)} %fusion.174) | copy-start | bytes 3076
  242.1 9.2 all-to-all-start
  251.3 65.8 %all-to-all-start.1 = ((bf16[256,8,512]{0,2,1:T(8,128)(2,1)}), bf16[256,8,512]{0,2,1:T(8,128)(2,1)}, u32[]{:S(2)}, u32[]{:S(2)}) async-start(bf16[256,8,512]{0,2,1:T(8,128)(2,1)} %bitcast.10), calls=%async_computation.1 | async-start | bytes 4194304 | tf_op jit(solution)/shard_map/all_to_all | solution.py:149
  255.7 309.6 %all-gather.9.cloned.1.call-start = ((), (), s32[]{:S(2)}) async-start(), calls=%async_computation.11 | async-start | bytes 17301504 | tf_op jit(solution)/shard_map/all_gather | solution.py:195
  258.1 61.5 %copy-start.24 = (f32[8]{0:T(128)}, f32[8]{0:T(128)S(1)}, u32[]{:S(2)}) copy-start(f32[8]{0:T(128)S(1)} %dynamic_slice.129) | copy-start | bytes 100
  269.0 62.5 %copy-start.4 = (f32[2048,256]{0,1:T(8,128)}, f32[2048,256]{0,1:T(8,128)S(1)}, u32[]{:S(2)}) copy-start(f32[2048,256]{0,1:T(8,128)S(1)} %get-tuple-element.855) | copy-start | bytes 6291460
  480.1 81.6 %all-to-all-start.2 = ((bf16[8,256,512]{1,2,0:T(8,128)(2,1)}), bf16[8,256,512]{1,2,0:T(8,128)(2,1)S(1)}, u32[]{:S(2)}, u32[]{:S(2)}) async-start(bf16[8,256,512]{1,2,0:T(8,128)(2,1)} %fusion.138), calls=%async_computation.2 | async-start | bytes 4194304 | tf_op jit(solution)/shard_map/all_to_all | solution.py:193
  483.8 81.5 %copy-start.8 = (bf16[256,2048]{1,0:T(8,128)(2,1)S(1)}, bf16[256,2048]{1,0:T(8,128)(2,1)}, u32[]{:S(2)}) copy-start(bf16[256,2048]{1,0:T(8,128)(2,1)} %param.29) | copy-start | bytes 3145732
  583.3 52.6 %all-to-all-start.3 = ((bf16[256,8,512]{0,2,1:T(8,128)(2,1)}), bf16[256,8,512]{0,2,1:T(8,128)(2,1)S(1)}, u32[]{:S(2)}, u32[]{:S(2)}) async-start(bf16[256,8,512]{0,2,1:T(8,128)(2,1)} %bitcast.686), calls=%async_computation.3 | async-start | bytes 4194304 | tf_op jit(solution)/shard_map/all_to_all | solution.py:219
  586.9 461.6 %reduce-scatter.4.cloned.1.call-start = ((), (), s32[]{:S(2)}) async-start(), calls=%async_computation.12 | async-start | bytes 2359296 | tf_op jit(solution)/shard_map/reduce_scatter | solution.py:233
  1015.3 186.3 %all-reduce.24.cloned.1.call-start = ((), (), s32[]{:S(2)}) async-start(), calls=%async_computation.15 | async-start | bytes 139264 | tf_op jit(solution)/shard_map/psum | solution.py:282
  1016.2 534.9 %reduce-scatter.8.cloned.1.call-start = ((), (), s32[]{:S(2)}) async-start(), calls=%async_computation.14 | async-start | bytes 34603008 | tf_op jit(solution)/shard_map/reduce_scatter | solution.py:211
  1031.3 9.3 all-to-all-start.5
  1037.2 57.4 %copy-start.5 = (bf16[256,2048]{1,0:T(8,128)(2,1)S(1)}, bf16[256,2048]{1,0:T(8,128)(2,1)}, u32[]{:S(2)}) copy-start(bf16[256,2048]{1,0:T(8,128)(2,1)} %param.17) | copy-start | bytes 3145732
  1037.2 57.4 %copy-start.13 = (f32[2048]{0:T(1024)S(1)}, f32[2048]{0:T(1024)}, u32[]{:S(2)}) copy-start(f32[2048]{0:T(1024)} %copy-done.12) | copy-start | bytes 24580
  1037.2 57.4 %copy-start.17 = (f32[256]{0:T(256)S(1)}, f32[256]{0:T(256)}, u32[]{:S(2)}) copy-start(f32[256]{0:T(256)} %copy-done.16) | copy-start | bytes 3076
  1040.6 54.0 %all-to-all-start.4 = ((bf16[8,256,512]{1,2,0:T(8,128)(2,1)}), bf16[8,256,512]{1,2,0:T(8,128)(2,1)}, u32[]{:S(2)}, u32[]{:S(2)}) async-start(bf16[8,256,512]{1,2,0:T(8,128)(2,1)} %bitcast.687), calls=%async_computation.4 | async-start | bytes 4194304 | tf_op jit(solution)/shard_map/all_to_all | solution.py:230
  1044.9 1247.7 %reduce-scatter.6.cloned.1.call-start = ((), (), s32[]{:S(2)}) async-start(), calls=%async_computation.13 | async-start | bytes 72450048 | tf_op jit(solution)/shard_map/reduce_scatter | solution.py:241
  1132.1 26.9 %copy-start.19 = (f32[4096]{0:T(1024)S(1)}, f32[4096]{0:T(1024)}, u32[]{:S(2)}) copy-start(f32[4096]{0:T(1024)} %get-tuple-element.744) | copy-start | bytes 49156
  1132.1 66.3 %copy-start.22 = (f32[256]{0:T(256)S(1)}, f32[256]{0:T(256)}, u32[]{:S(2)}) copy-start(f32[256]{0:T(256)} %copy-done.21) | copy-start | bytes 3076
  1132.1 66.3 %copy-start.10 = (bf16[256,2048]{1,0:T(8,128)(2,1)S(1)}, bf16[256,2048]{1,0:T(8,128)(2,1)}, u32[]{:S(2)}) copy-start(bf16[256,2048]{1,0:T(8,128)(2,1)} %param.29) | copy-start | bytes 3145732
  (25 other events, 184.2 us)
Sparse Core Ops, SparseCore 0:
  10.9 206.1 all-gather.4
  240.9 24.9 all-gather.6
  268.9 132.8 all-gather.8
  1015.4 33.0 reduce-scatter.3
  1054.5 130.4 all-reduce.23
  1187.7 363.3 reduce-scatter.7
  1554.0 738.5 reduce-scatter.5
where the time goes:
time: 2320 us; the launch traced here: 2300 us
  waiting for transfers between devices  1410 us (61%)
  matrix products  262 us (11%)
  local copies, waits for them, and re-layouts  259 us (11%)
  blocking collectives  160 us (7%)
  other arithmetic  147 us (6%)
  loops' own time  23.4 us (1%)
    reduce_scatter x1, waiting for transfers between devices, shards(): lax.psum_scatter(lax.dot_general(columns, grad_projected, transpose, pref...  742 us
    reduce_scatter x1, waiting for transfers between devices, shards(): lax.psum_scatter(lax.dot_general(columns, cotangent, transpose, preferred...  349 us
    all_gather x1, waiting for transfers between devices, shards(): weight_rows = lax.all_gather(in_weight, ('row', 'head'), axis=0, tiled=True)  162 us
    dynamic_update_slice x32, local copies, waits for them, and re-layouts, ssd_scan(): lax.scan(stepper, memory, (blocks(values), blocks(step_sizes), blocks(key...  139 us
    unnamed x2, blocking collectives  82.1 us
    all_gather x1, blocking collectives, shards(): gain_rows = lax.all_gather(gate_gain, ('row', 'head'), axis=0, tiled=True)  77.9 us
    dot_general x24, matrix products, block_step(): jnp.einsum('rtuh,ruhp->rthp', decays * scores[..., None], scaled_values,...  74.5 us
    all_to_all x1, waiting for transfers between devices, shards(): lax.all_to_all(grad_mixed.astype(jnp.bfloat16), 'head', split_axis=1, con...  48.8 us
  transfers between devices with their start and end apart: 13, of which 10 were waited for; matrix products, arithmetic and copies ran while one was open for 11% of the time, Pallas kernels for 0%

commit v1 on v0

v1 whole, which is shorter than its diff:
```python
import jax
import jax.numpy as jnp
from jax import lax
from jax.experimental import pallas as pl
from jax.experimental.pallas import tpu as pltpu
from jax.sharding import PartitionSpec as P

HEADS = 64
HDIM = 64
NSTATE = 128
SPAN = 256
DIN = 4096
TAPS = 4
LANES = 128
epsilon = 1e-05

f32 = jnp.float32
bf16 = jnp.bfloat16

NN = (((1,), (0,)), ((), ()))
NT = (((1,), (1,)), ((), ()))
TN = (((0,), (0,)), ((), ()))
CROSS = (((0,), (1,)), ((), ()))


def mm(a, b, dims, out=f32):
    return lax.dot_general(a, b, dims, preferred_element_type=f32).astype(out)


def sigmoid(v):
    return 0.5 * jnp.tanh(0.5 * v) + 0.5


def seen(info, count):
    here = info[0:1, LANES : LANES + SPAN]
    return (info[0:1, LANES - count : LANES + SPAN - count] == here).astype(f32)


def shifts(info, row, sign):
    source = lax.broadcasted_iota(jnp.int32, (SPAN + LANES, SPAN), 0)
    target = lax.broadcasted_iota(jnp.int32, (SPAN + LANES, SPAN), 1)
    edge = 4 * row + 4 if sign == 1 else 4 * row - SPAN
    parts = []
    for k in range(1, TAPS):
        wanted = target - sign * k
        outside = wanted < 0 if sign == 1 else wanted >= SPAN
        wanted = jnp.where(outside, SPAN + edge + wanted, wanted)
        parts.append(jnp.where(source == wanted, seen(info, sign * k), 0.0).astype(bf16))
    return jnp.concatenate(parts, axis=1)


def twice(tile):
    return jnp.concatenate([tile, tile], axis=1)


def tap(taps, k):
    return jnp.broadcast_to(taps[:, k : k + 1], (taps.shape[0], SPAN))


def conv_kernel(
    raw_ref, halo_ref, info_ref, step_ref, log_ref, taps_ref, conv_ref, slope_ref, state_ref, wx_ref
):
    info = info_ref[0]
    before = shifts(info, pl.program_id(0), 1)
    here = info[0:1, LANES : LANES + SPAN]
    ending = (here == here[:, SPAN - 1 : SPAN]).astype(f32)
    logs = log_ref[...]
    weight = jnp.exp(logs[:, SPAN - 1 : SPAN] - logs) * step_ref[...] * ending
    heads = weight.shape[0]
    width = heads * HDIM
    for part in range(conv_ref.shape[0] // LANES):
        rows = pl.ds(part * LANES, LANES)
        raw = raw_ref[rows, :]
        shifted = mm(jnp.concatenate([raw, halo_ref[rows, :]], axis=1), before, NN)
        taps = taps_ref[rows, :]
        pre = tap(taps, TAPS) + tap(taps, 0) * raw.astype(f32)
        for k in range(1, TAPS):
            pre = pre + tap(taps, k) * shifted[:, (k - 1) * SPAN : k * SPAN]
        sig = sigmoid(pre)
        out = pre * sig
        conv_ref[rows, :] = out.astype(bf16)
        slope_ref[rows, :] = (sig + out * (1.0 - sig)).astype(bf16)
        if part * LANES < width:
            out = out.astype(bf16).astype(f32)
            for h in range(part * LANES // HDIM, (part + 1) * LANES // HDIM):
                at = h * HDIM - part * LANES
                scaled = out[at : at + HDIM] * weight[h : h + 1]
                wx_ref[pl.ds(h * HDIM, HDIM), :] = scaled.astype(bf16)
    keys = conv_ref[width : width + NSTATE, :]
    state_ref[0] = mm(wx_ref[...], keys, NT, bf16)


def link_bias(info, info_col):
    here = info[0:1, LANES : LANES + SPAN]
    u = lax.broadcasted_iota(jnp.int32, (SPAN, LANES), 0)
    t = lax.broadcasted_iota(jnp.int32, (SPAN, LANES), 1)
    same0 = info_col[:LANES] == here[:, :LANES]
    same1 = info_col == here[:, LANES:]
    first = jnp.where(jnp.logical_and(same0, u[:LANES] <= t[:LANES]), 0.0, -1e30)
    second = jnp.where(jnp.logical_and(same1, u <= t + LANES), 0.0, -1e30)
    return first, second


def within_kernel(conv_ref, info_ref, log_ref, shifted_ref, out_ref):
    info = info_ref[0]
    heads = log_ref.shape[0]
    width = heads * HDIM
    info_col = jnp.transpose(info[:, LANES : LANES + SPAN])[:, 0:1]
    bias0, bias1 = link_bias(info, info_col)
    keys = conv_ref[width : width + NSTATE, :]
    queries = conv_ref[width + NSTATE : width + 2 * NSTATE, :]
    score0 = mm(keys[:, :LANES], queries[:, :LANES], TN)
    score1 = mm(keys, queries[:, LANES:], TN)
    logs = log_ref[...]
    source = jnp.transpose(shifted_ref[...])
    for h in range(heads):
        rows = pl.ds(h * HDIM, HDIM)
        col = source[:, h : h + 1]
        m0 = jnp.exp(logs[h : h + 1, :LANES] - col[:LANES] + bias0) * score0
        m1 = jnp.exp(logs[h : h + 1, LANES:] - col + bias1) * score1
        x = conv_ref[rows, :]
        out_ref[rows, :LANES] = mm(x[:, :LANES], m0.astype(bf16), NN)
        out_ref[rows, LANES:] = mm(x, m1.astype(bf16), NN)


def carried_decay(info, logs):
    here = info[0:1, LANES : LANES + SPAN]
    carried = (here == info[0:1, LANES - 1 : LANES]).astype(f32)
    return jnp.exp(logs) * carried


def mix_kernel(
    conv_ref, info_ref, log_ref, state_ref, within_ref, gate_ref, grad_ref, skip_ref,
    gain_ref, mixed_ref, sums_ref,
):
    info = info_ref[0]
    heads = log_ref.shape[0]
    width = heads * HDIM
    decay = carried_decay(info, log_ref[...])
    fill = info[1:2, LANES : LANES + SPAN]
    queries = conv_ref[width + NSTATE : width + 2 * NSTATE, :]
    reading = mm(state_ref[0], queries, NN)
    square = jnp.zeros((HDIM, SPAN), f32)
    cross = jnp.zeros((HDIM, SPAN), f32)
    for h in range(heads):
        rows = pl.ds(h * HDIM, HDIM)
        x = conv_ref[rows, :].astype(f32)
        core = within_ref[rows, :] + decay[h : h + 1] * reading[h * HDIM : (h + 1) * HDIM]
        mixed = ((core + skip_ref[h : h + 1, 0:1] * x) * fill).astype(bf16)
        mixed_ref[rows, :] = mixed
        z = gate_ref[rows, :]
        gated = mixed.astype(f32) * (z * sigmoid(z))
        square = square + gated * gated
        cross = cross + gated * (grad_ref[rows, :] * twice(gain_ref[rows, :]))
    sums_ref[0:1, :] = jnp.sum(square, axis=0, keepdims=True)
    sums_ref[1:2, :] = jnp.sum(cross, axis=0, keepdims=True)
    sums_ref[2:8, :] = jnp.zeros((6, SPAN), f32)


def gate_kernel(
    matrix_ref, info_ref, log_ref, mixed_ref, gate_ref, grad_ref, sums_ref, gain_ref,
    hat_ref, dmixed_ref, dgate_ref, state_ref, ey_ref,
):
    info = info_ref[0]
    heads = log_ref.shape[0]
    decay = carried_decay(info, log_ref[...])
    fill = info[1:2, LANES : LANES + SPAN]
    inverse = lax.rsqrt(sums_ref[0:1, :] * (1.0 / DIN) + epsilon)
    along = inverse * inverse * sums_ref[1:2, :] * (1.0 / DIN)
    for h in range(heads):
        rows = pl.ds(h * HDIM, HDIM)
        z = gate_ref[rows, :]
        mixed = mixed_ref[rows, :].astype(f32)
        sig = sigmoid(z)
        silu = z * sig
        gated = mixed * silu
        gain = twice(gain_ref[rows, :])
        hat_ref[rows, :] = (gated * inverse * gain).astype(bf16)
        grad = inverse * (grad_ref[rows, :] * gain - gated * along)
        dgate_ref[rows, :] = (grad * mixed * (sig * (1.0 + z * (1.0 - sig)))).astype(bf16)
        dy = ((grad * silu).astype(bf16).astype(f32) * fill)
        dmixed_ref[rows, :] = dy.astype(bf16)
        ey_ref[rows, :] = (dy * decay[h : h + 1]).astype(bf16)
    queries = matrix_ref[NSTATE:, :]
    state_ref[0] = mm(ey_ref[...], queries, NT, bf16)


def within_back_kernel(
    conv_ref, info_ref, log_ref, shifted_ref, dy_ref, state_ref,
    dx_ref, dbc_ref, rows_ref, ey_ref, ds0_ref, ds1_ref,
):
    info = info_ref[0]
    heads = log_ref.shape[0]
    width = heads * HDIM
    info_col = jnp.transpose(info[:, LANES : LANES + SPAN])[:, 0:1]
    bias0, bias1 = link_bias(info, info_col)
    keys = conv_ref[width : width + NSTATE, :]
    queries = conv_ref[width + NSTATE : width + 2 * NSTATE, :]
    score0 = mm(keys[:, :LANES], queries[:, :LANES], TN)
    score1 = mm(keys, queries[:, LANES:], TN)
    logs = log_ref[...]
    source = jnp.transpose(shifted_ref[...])
    decay = carried_decay(info, logs)
    state = state_ref[0]
    reading = mm(state, queries, NN)
    for h in range(heads):
        rows = pl.ds(h * HDIM, HDIM)
        col = source[:, h : h + 1]
        d0 = jnp.exp(logs[h : h + 1, :LANES] - col[:LANES] + bias0)
        d1 = jnp.exp(logs[h : h + 1, LANES:] - col + bias1)
        m0 = (d0 * score0).astype(bf16)
        m1 = (d1 * score1).astype(bf16)
        x = conv_ref[rows, :]
        dy = dy_ref[rows, :]
        y0 = mm(x[:, :LANES], m0, NN)
        y1 = mm(x, m1, NN)
        dxa = mm(dy[:, :LANES], m0, NT)
        dxb = mm(dy[:, LANES:], m1, NT)
        g0 = mm(x[:, :LANES], dy[:, :LANES], TN) * d0
        g1 = mm(x, dy[:, LANES:], TN) * d1
        if h == 0:
            ds0_ref[...] = g0
            ds1_ref[...] = g1
        else:
            ds0_ref[...] += g0
            ds1_ref[...] += g1
        dx = jnp.concatenate([dxa + dxb[:, :LANES], dxb[:, LANES:]], axis=1)
        dx_ref[rows, :] = dx
        xf = x.astype(f32)
        dyf = dy.astype(f32)
        ey = dyf * decay[h : h + 1]
        ey_ref[rows, :] = ey.astype(bf16)
        inner = jnp.sum(xf * dx, axis=0, keepdims=True)
        y = jnp.concatenate([y0, y1], axis=1)
        across = reading[h * HDIM : (h + 1) * HDIM]
        outer = jnp.sum(dyf * y + ey * across, axis=0, keepdims=True)
        rows_ref[h : h + 1, :] = outer - inner
        rows_ref[heads + h : heads + h + 1, :] = inner
        rows_ref[2 * heads + h : 2 * heads + h + 1, :] = jnp.sum(dyf * xf, axis=0, keepdims=True)
    ds0 = ds0_ref[...].astype(bf16)
    ds1 = ds1_ref[...].astype(bf16)
    dkeys_b = mm(queries[:, LANES:], ds1, NT)
    dkeys_a = mm(queries[:, :LANES], ds0, NT)
    dbc_ref[:NSTATE, :LANES] = dkeys_a + dkeys_b[:, :LANES]
    dbc_ref[:NSTATE, LANES:] = dkeys_b[:, LANES:]
    dq_state = mm(state, ey_ref[...], TN)
    dbc_ref[NSTATE:, :LANES] = mm(keys[:, :LANES], ds0, NN) + dq_state[:, :LANES]
    dbc_ref[NSTATE:, LANES:] = mm(keys, ds1, NN) + dq_state[:, LANES:]


def state_back_kernel(
    conv_ref, slope_ref, info_ref, log_ref, step_ref, sig_ref, dy_ref, dx_ref, dbc_ref,
    rows_ref, dstate_ref, state_ref, par_ref,
    g_ref, dstep_ref, starts_ref, wx_ref,
):
    row = pl.program_id(0)
    info = info_ref[0]
    heads = log_ref.shape[0]
    width = heads * HDIM
    here = info[0:1, LANES : LANES + SPAN]
    ending = (here == here[:, SPAN - 1 : SPAN]).astype(f32)
    logs = log_ref[...]
    step = step_ref[...]
    last = logs[:, SPAN - 1 : SPAN]
    weight = jnp.exp(last - logs) * step * ending
    keep = jnp.exp(last) * (here[:, SPAN - 1 : SPAN] == info[0:1, LANES - 1 : LANES]).astype(f32)
    keys = conv_ref[width : width + NSTATE, :]
    dstate = dstate_ref[0]
    along = mm(dstate, keys, NN)
    inner_rows = []
    tail_rows = []
    for h in range(heads):
        rows = pl.ds(h * HDIM, HDIM)
        x = conv_ref[rows, :].astype(f32)
        w = weight[h : h + 1]
        wv = w * along[h * HDIM : (h + 1) * HDIM]
        wx_ref[rows, :] = (w * x).astype(bf16)
        inner_rows.append(jnp.sum(x * wv, axis=0, keepdims=True))
        product = dstate[h * HDIM : (h + 1) * HDIM].astype(f32) * state_ref[
            0, h * HDIM : (h + 1) * HDIM, :
        ].astype(f32)
        tail_rows.append(jnp.sum(jnp.sum(product, axis=0, keepdims=True), axis=1, keepdims=True))
        dx = dx_ref[rows, :] + wv + par_ref[h : h + 1, 0:1] * dy_ref[rows, :].astype(f32)
        g = dx * slope_ref[rows, :].astype(f32)
        g_ref[rows, :] = g.astype(bf16)

    inner = jnp.concatenate(inner_rows, axis=0)
    tail = jnp.concatenate(tail_rows, axis=0) * keep + jnp.sum(inner, axis=1, keepdims=True)
    dlog = rows_ref[0:heads, :] - inner
    t = lax.broadcasted_iota(jnp.int32, (SPAN, SPAN), 0)
    u = lax.broadcasted_iota(jnp.int32, (SPAN, SPAN), 1)
    later = (t >= u).astype(f32)
    dstepped = lax.dot_general(
        dlog, later, NN, precision=lax.Precision.HIGHEST, preferred_element_type=f32
    ) + tail
    rate = par_ref[:, 1:2]
    total = rows_ref[heads : 2 * heads, :] + inner
    sig = sig_ref[...]
    ratio = jnp.where(step > 1e-30, sig / jnp.maximum(step, 1e-30), 1.0)
    dstep_ref[0:heads, :] = total * ratio + rate * dstepped * sig
    dstep_ref[heads : 2 * heads, :] = dstepped * step * rate
    dkeys = dbc_ref[:NSTATE, :] + mm(dstate, wx_ref[...], TN)
    for start, grad in ((width, dkeys), (width + NSTATE, dbc_ref[NSTATE:, :])):
        rows = pl.ds(start, NSTATE)
        g_ref[rows, :] = (grad * slope_ref[rows, :].astype(f32)).astype(bf16)
    lane = lax.broadcasted_iota(jnp.int32, starts_ref.shape, 1)
    ours = jnp.logical_and(lane >= 4 * row, lane < 4 * row + 4)
    kept = jnp.where(row == 0, 0.0, starts_ref[...].astype(f32))
    fresh = pltpu.roll(g_ref[:, :LANES].astype(f32), 4 * row, 1)
    starts_ref[...] = jnp.where(ours, fresh, kept).astype(bf16)


def conv_back_kernel(
    raw_ref, halo_ref, g_ref, later_ref, info_ref, taps_ref, draw_ref, dtaps_ref
):
    row = pl.program_id(0)
    info = info_ref[0]
    before, after_ = shifts(info, row, 1), shifts(info, row, -1)
    size = min(LANES, raw_ref.shape[0])
    for part in range(raw_ref.shape[0] // size):
        rows = pl.ds(part * size, size)
        raw, low = raw_ref[rows, :], g_ref[rows, :]
        g = low.astype(f32)
        shifted = mm(jnp.concatenate([raw, halo_ref[rows, :]], axis=1), before, NN)
        ahead = mm(jnp.concatenate([low, later_ref[rows, :]], axis=1), after_, NN)
        taps = taps_ref[rows, :]
        draw = tap(taps, 0) * g
        products = [g * raw.astype(f32)]
        for k in range(1, TAPS):
            lanes = slice((k - 1) * SPAN, k * SPAN)
            draw = draw + tap(taps, k) * ahead[:, lanes]
            products.append(g * shifted[:, lanes])
        products.append(g)
        draw_ref[rows, :] = draw.astype(bf16)
        for k, product in enumerate(products):
            kept = jnp.where(row == 0, 0.0, dtaps_ref[k, rows, :])
            dtaps_ref[k, rows, :] = kept + product[:, :LANES] + product[:, LANES:]


def token_spec(channels):
    return pl.BlockSpec((channels, SPAN), lambda k, c: (0, k))


def part_spec(shape, start, by_token=False):
    lead = (0,) * (len(shape) - 2)
    return pl.BlockSpec(shape, lambda k, c: lead + (start(c), k if by_token else 0))


def fixed_spec(shape):
    return pl.BlockSpec(shape, lambda k, c: (0,) * len(shape))


def cell_spec(shape):
    return pl.BlockSpec((1,) + shape, lambda k, c: (k, 0, 0))


def call(kernel, rows, operands, in_specs, outs, out_specs, scratch=(), name=None, place=None):
    used = place is not None
    place = place if used else jnp.zeros((1,), jnp.int32)
    return pl.pallas_call(
        kernel if used else lambda place_ref, *refs: kernel(*refs),
        grid_spec=pltpu.PrefetchScalarGridSpec(
            num_scalar_prefetch=1,
            grid=(rows,),
            in_specs=in_specs,
            out_specs=out_specs,
            scratch_shapes=list(scratch),
        ),
        out_shape=outs,
        compiler_params=pltpu.CompilerParams(vmem_limit_bytes=50 * 1024 * 1024),
        cost_estimate=pl.CostEstimate(flops=0, bytes_accessed=0, transcendentals=0),
        name=name,
    )(place, *operands)


def finish_kernel(gate_ref, main_ref, tail_ref, weight_ref, grad_ref, sums_ref):
    total = jnp.zeros(sums_ref.shape, f32)
    ranks, _, width = gate_ref.shape
    matrix = slice(width, width + 2 * NSTATE)
    parts = [(gate_ref[q].astype(f32), q * width) for q in range(ranks)]
    parts += [(main_ref[q, :, :width].astype(f32), (ranks + q) * width) for q in range(ranks)]
    parts += [(sum(main_ref[q, :, matrix].astype(f32) for q in range(ranks)), 2 * ranks * width)]
    parts += [(tail_ref[...].astype(f32), 2 * ranks * width + 2 * NSTATE)]
    for value, start in parts:
        size = value.shape[1]
        grad_ref[:, start : start + size] = value
        product = value * weight_ref[:, start : start + size].astype(f32)
        whole = size // LANES * LANES
        for i in range(0, whole, LANES):
            total = total + product[:, i : i + LANES]
        if whole < size:
            rest = jnp.zeros((product.shape[0], LANES - size + whole), f32)
            total = total + jnp.concatenate([product[:, whole:], rest], axis=1)
    sums_ref[...] = total


def finish(gate_rows, main_rows, tail, weight):
    span_rows = weight.shape[0]
    return pl.pallas_call(
        finish_kernel,
        out_shape=[
            jax.ShapeDtypeStruct(weight.shape, f32),
            jax.ShapeDtypeStruct((span_rows, LANES), f32),
        ],
        compiler_params=pltpu.CompilerParams(vmem_limit_bytes=50 * 1024 * 1024),
        name="finish",
    )(gate_rows, main_rows, tail, weight)


def tie(*values):
    return lax.optimization_barrier(values)


def after(value, *others):
    return tie(value, *others)[0]


def shards(
    tokens, in_weight, norm_gain, out_weight, gate_gain, conv_weight, conv_bias, dt_bias, a_log,
    skip_gain, boundary, fill, cotangent,
):
    rows = lax.axis_size("row")
    head_axis = lax.axis_size("head")
    devices = rows * head_axis
    local, width_in = tokens.shape
    seq = boundary.shape[1]
    spans = seq // SPAN
    planes = spans // 2
    groups = head_axis // spans
    assert rows == 4 and local == SPAN and boundary.shape[0] == groups
    heads = HEADS // rows
    width = heads * HDIM
    span_rows = in_weight.shape[0]
    out_rows = out_weight.shape[0]
    count = rows * SPAN
    half = width_in // 2
    channels = width + 2 * NSTATE

    row = lax.axis_index("row")
    head = lax.axis_index("head")
    core = head % 2
    span = head % spans
    plane = span // 2
    group = head // spans
    first = core == 0

    def across_rows(a, mask):
        return lax.ppermute(a, "row", [(i, i ^ mask) for i in range(rows)])

    def over_heads(a, pairs):
        return lax.ppermute(a, "head", pairs)

    def device(g, p, c):
        return (g * planes + p) * 2 + c

    every = [(g, p, c) for g in range(groups) for p in range(planes) for c in range(2)]
    siblings = [(device(g, p, c), device(g, p, 1 - c)) for g, p, c in every]
    ring_up = [(device(g, p, c), device(g, (p + 1) % planes, c)) for g, p, c in every]
    ring_down = [(b, a) for a, b in ring_up]
    next_span = [(g * spans + b, g * spans + b + 1) for g in range(groups) for b in range(spans - 1)]
    last_span = [(b, a) for a, b in next_span]
    same_place = [
        [device(g, p, c) for g in range(groups)] for p in range(planes) for c in range(2)
    ]

    def hop_up(p):
        return [(device(g, p, c), device(g, p + 1, c)) for g in range(groups) for c in range(2)]

    def hop_down(p):
        return [(b, a) for a, b in hop_up(p)]

    def sibling(a):
        return over_heads(a, siblings)

    def by_core(zero, one):
        return jnp.where(first, zero, one)

    def all_rows(a):
        return lax.all_to_all(
            jnp.broadcast_to(a[None], (rows,) + a.shape), "row", 0, 0, tiled=True
        )

    def gather_groups(a):
        if groups == 1:
            return a
        return lax.all_gather(a, "head", axis=0, axis_index_groups=same_place, tiled=True)

    def everywhere(a):
        return lax.all_to_all(
            jnp.broadcast_to(a[None], (devices,) + a.shape), ("row", "head"), 0, 0, tiled=True
        )

    def arranged(a):
        whole = a.reshape(a.shape[0], rows, head_axis, span_rows)
        return whole.transpose(0, 2, 1, 3).reshape(a.shape[0], width_in)

    def restored(a):
        whole = a.reshape(a.shape[0], head_axis, rows, span_rows)
        return whole.transpose(0, 2, 1, 3).reshape(a.shape[0], width_in)

    def column_part(cols):
        return lax.all_to_all(cols, "row", 0, 0, tiled=True).reshape(rows * span_rows, -1)

    def place_parts(whole, pieces):
        size = pieces[0][0].shape[0]
        for i, both in enumerate(pieces):
            for e, part in enumerate(both):
                at = (plane - i) % planes * 2 + (core ^ e)
                if groups == 1:
                    found = [(at, part)]
                else:
                    every_group = lax.all_gather(
                        part, "head", axis=0, axis_index_groups=same_place
                    )
                    found = [(g * spans + at, every_group[g]) for g in range(groups)]
                for place, one in found:
                    whole = lax.dynamic_update_slice(whole, one, (place * size, 0))
        return whole

    def up_ring(a):
        return over_heads(a, ring_up)

    value_cols = in_weight[:, DIN : 2 * DIN].reshape(span_rows, rows, width).transpose(1, 0, 2)
    matrix_cols = in_weight[:, 2 * DIN : 2 * DIN + 2 * NSTATE]
    matrix_cols = jnp.broadcast_to(matrix_cols[None], (rows, span_rows, 2 * NSTATE))
    main = [column_part(jnp.concatenate([value_cols, matrix_cols], axis=2))]
    out_rank = lax.all_gather(out_weight, "head", axis=0, tiled=True)

    gains = jnp.stack(
        [jnp.pad(g.astype(f32), (0, LANES - g.shape[0])) for g in (norm_gain, gate_gain)]
    )
    gains = everywhere(after(jnp.pad(gains, ((0, 6), (0, 0))), main[0]))
    main.append(up_ring(main[0]))
    gains, main[1] = tie(gains, main[1])
    all_norm_gain = gains[:, 0, :span_rows].reshape(1, width_in)
    rank_gain = gains[:, 1, :out_rows].reshape(rows, width)
    rank_gain = lax.dynamic_index_in_dim(rank_gain, row, 0, keepdims=False)
    rank_gain = jnp.broadcast_to(rank_gain[:, None], (width, LANES))

    activations = tokens.astype(f32)
    inverse = lax.rsqrt(jnp.mean(activations * activations, axis=-1, keepdims=True) + epsilon)
    normed = activations * inverse
    projected_in = arranged((normed * all_norm_gain).astype(bf16))
    projected_in, main[1] = tie(projected_in, main[1])
    cut = SPAN // 2
    from_x, from_y = across_rows(projected_in, 1), across_rows(projected_in, 2)
    gate_cols = after(in_weight[:, :DIN], gains)
    gate_parts = [column_part(gate_cols.reshape(span_rows, rows, width).transpose(1, 0, 2))]
    for _ in range(planes - 2):
        main.append(up_ring(main[-1]))
    from_x, from_y, gate_parts[0], main[-1] = tie(from_x, from_y, gate_parts[0], main[-1])

    x_far, y_far = across_rows(from_x[:cut], 2), across_rows(from_y[cut:], 1)
    steps_cols = after(in_weight[:, 2 * DIN + 2 * NSTATE :], main[-1]).T
    steps_cols = steps_cols.reshape(rows, 1, heads, span_rows)
    steps_cols = jnp.broadcast_to(steps_cols, (rows, head_axis, heads, span_rows))
    steps_cols = lax.all_to_all(
        steps_cols.reshape(devices, heads, span_rows), ("row", "head"), 0, 0, tiled=True
    )
    step_weight = steps_cols.reshape(rows, head_axis, heads, span_rows).transpose(2, 1, 0, 3)
    step_weight = step_weight.reshape(heads, width_in)
    gate_parts.append(up_ring(gate_parts[0]))
    x_far, y_far, step_weight, gate_parts[1] = tie(x_far, y_far, step_weight, gate_parts[1])
    main_weight = jnp.zeros((width_in, channels + heads), bf16)
    main_weight = place_parts(main_weight, [(part, sibling(part)) for part in main])
    main_weight = lax.dynamic_update_slice(main_weight, step_weight.T, (0, channels))

    plane_in = jnp.zeros((count + LANES, width_in), bf16)
    ends_in = jnp.zeros((rows, 4, width_in), bf16)
    for part, source, start in (
        (projected_in, row, 0), (from_x, row ^ 1, 0), (from_y, row ^ 2, 0),
        (x_far, row ^ 3, 0), (y_far, row ^ 3, cut),
    ):
        plane_in = lax.dynamic_update_slice(plane_in, part, (source * SPAN + start, 0))
        if start + part.shape[0] == SPAN:
            ends_in = lax.dynamic_update_slice(ends_in, part[-4:][None], (source, 0, 0))
    halo_in = over_heads(ends_in.reshape(4 * rows, width_in), next_span)
    extended_in = lax.dynamic_update_slice(plane_in, halo_in, (count + 0 * row, 0))
    plane_in = extended_in[:count]

    segments = jnp.cumsum(boundary, axis=1).astype(f32)
    used = (jnp.arange(seq)[None, :] < fill[:, None]).astype(f32)
    says = jnp.stack(
        [
            jnp.pad(segments, ((0, 0), (LANES, LANES)), constant_values=-1.0),
            jnp.pad(used, ((0, 0), (LANES, LANES))),
        ],
        axis=1,
    )
    says = lax.dynamic_slice(says, (group, 0, span * SPAN), (1, 2, SPAN + 2 * LANES))[0]
    info = all_rows(after(jnp.pad(says, ((0, 6), (0, 0))), steps_cols))

    plane_cot = all_rows(after(cotangent, info)).reshape(count, width_in)

    local_step = lax.dynamic_slice_in_dim(dt_bias, row * heads, heads, 0)
    local_rate = -jnp.exp(lax.dynamic_slice_in_dim(a_log, row * heads, heads, 0))
    local_skip = lax.dynamic_slice_in_dim(skip_gain, row * heads, heads, 0)
    raw_steps = mm(step_weight, plane_in, NT, bf16).astype(f32)
    shifted_steps = raw_steps + local_step[:, None]
    steps = jax.nn.softplus(shifted_steps)
    step_slope = jax.nn.sigmoid(shifted_steps)
    earlier = jnp.triu(jnp.ones((SPAN, SPAN), f32))
    logs = lax.dot_general(
        (steps * local_rate[:, None]).reshape(heads * rows, SPAN), earlier, NN,
        precision=lax.Precision.HIGHEST, preferred_element_type=f32,
    ).reshape(heads, count)
    shifted_logs = logs - jnp.log(steps)
    params = jnp.pad(jnp.stack([local_skip, local_rate], axis=1), ((0, 0), (0, LANES - 2)))
    ends = logs.reshape(heads, rows, SPAN)[:, :, -1].T
    seg_ids = info[:, 0]
    unbroken = (seg_ids[:, LANES - 1] == seg_ids[:, LANES + SPAN - 1]).astype(f32)
    keep = jnp.exp(ends) * unbroken[:, None]
    keep_other = sibling(jnp.pad(keep, ((0, 0), (0, LANES - heads))))[:, :heads]
    keep, keep_other = keep[:, :, None, None], keep_other[:, :, None, None]
    keep_plane = keep * keep_other

    all_taps = jnp.concatenate([conv_weight, conv_bias[None]], axis=0)
    taps = jnp.concatenate(
        [lax.dynamic_slice_in_dim(all_taps, row * width, width, 1), all_taps[:, DIN:]], axis=1
    )
    taps = jnp.pad(taps.T, ((0, 0), (0, LANES - TAPS - 1)))

    raw = mm(main_weight[:, :channels], extended_in, CROSS, bf16)
    gate_parts.append(up_ring(gate_parts[1]))
    raw, gate_parts[2] = tie(raw, gate_parts[2])
    halo_spec = pl.BlockSpec((channels, LANES), lambda k, c: (0, count // LANES))
    shape = jax.ShapeDtypeStruct
    info_spec = cell_spec(info.shape[1:])
    state_spec = cell_spec((width, NSTATE))
    states = shape((rows, width, NSTATE), bf16)
    by_head = (rows, heads, HDIM, NSTATE)
    row_spec = token_spec(heads)
    wide = token_spec(width)
    tall = token_spec(channels)
    low_wide = shape((width, count), bf16)
    conv, slope, local_state = call(
        conv_kernel, rows, (raw, raw, info, steps, logs, taps),
        [tall, halo_spec, info_spec, row_spec, row_spec, fixed_spec(taps.shape)],
        [shape((channels, count), bf16), shape((channels, count), bf16), states],
        [tall, tall, state_spec],
        [pltpu.VMEM((width, SPAN), bf16)], name="conv",
    )

    for _ in range(planes - 3):
        gate_parts.append(up_ring(gate_parts[-1]))
    local_state, gate_parts[-1] = tie(local_state, gate_parts[-1])
    gate_weight = place_parts(
        jnp.zeros((width_in, width), bf16), [(part, sibling(part)) for part in gate_parts]
    )

    def pass_states(mine, hops, beside, near):
        other = sibling(mine)
        is_near = core == near

        def own_heads(a):
            return lax.dynamic_slice_in_dim(a, core * (heads // 2), heads // 2, 1).astype(f32)

        total = own_heads(jnp.where(is_near, other, mine)) + own_heads(
            jnp.where(is_near, keep_other, keep)
        ) * own_heads(jnp.where(is_near, mine, other))
        keep_half = own_heads(keep_plane)
        got = jnp.zeros((), f32)
        passed = []
        for hop, others in zip(hops, beside):
            running = after((total + keep_half * got).astype(bf16), *others)
            got = got + over_heads(running, hop).astype(f32)
            passed.append(got)
        got = got.astype(bf16)
        rest = sibling(got)
        whole = by_core(
            jnp.concatenate([got, rest], axis=1), jnp.concatenate([rest, got], axis=1)
        )
        through = (other.astype(f32) + keep_other * whole.astype(f32)).astype(bf16)
        return jnp.where(is_near, whole, through).reshape(states.shape), passed

    within = call(
        within_kernel, rows, (conv, info, logs, shifted_logs),
        [tall, info_spec, row_spec, row_spec],
        shape((width, count), f32), wide, name="within",
    )
    gate = mm(gate_weight, plane_in, CROSS)
    grad_hat = mm(out_rank, plane_cot, NT, bf16)

    state_in, _ = pass_states(
        local_state.reshape(by_head), [hop_up(p) for p in range(planes - 1)],
        [(), (within,), (gate, plane_cot)] + [()] * (planes - 4), 0,
    )

    mixed, sums = call(
        mix_kernel, rows, (conv, info, logs, state_in, within, gate, grad_hat, params, rank_gain),
        [tall, info_spec, row_spec, state_spec, wide, wide, wide, fixed_spec(params.shape),
         fixed_spec(rank_gain.shape)],
        [low_wide, shape((8, count), f32)], [wide, token_spec(8)], name="mix",
    )
    sums = sums + sum(across_rows(sums, m) for m in range(1, rows))

    gated_hat, dmixed, dgate, local_dstate = call(
        gate_kernel, rows, (conv, info, logs, mixed, gate, grad_hat, sums, rank_gain),
        [part_spec((2 * NSTATE, SPAN), lambda c: width // (2 * NSTATE), True), info_spec, row_spec,
         wide, wide, wide, token_spec(8), fixed_spec(rank_gain.shape)],
        [low_wide] * 3 + [states], [wide, wide, wide, state_spec],
        [pltpu.VMEM((width, SPAN), bf16)], name="gate",
    )

    def to_owner(partial_sum):
        got = lax.all_to_all(partial_sum.reshape(rows, SPAN, -1), "row", 0, 0, tiled=True)
        return jnp.sum(got.astype(f32), axis=0)

    def rows_product(grads):
        return mm(plane_in, grads, CROSS, bf16)

    def over_planes(product):
        return lax.psum_scatter(product, "head", scatter_dimension=0, tiled=True)

    def rows_to_owner(summed):
        return lax.all_to_all(summed.reshape(rows, span_rows, -1), "row", 0, 0, tiled=True)

    dgate_product = rows_product(dgate)
    dx, dmatrix, row_sums = call(
        within_back_kernel, rows, (conv, info, logs, shifted_logs, dmixed, state_in),
        [tall, info_spec, row_spec, row_spec, wide, state_spec],
        [shape((width, count), f32), shape((2 * NSTATE, count), f32), shape((3 * heads, count), f32)],
        [wide, token_spec(2 * NSTATE), token_spec(3 * heads)],
        [pltpu.VMEM((width, SPAN), bf16), pltpu.VMEM((LANES, LANES), f32),
         pltpu.VMEM((SPAN, LANES), f32)],
        name="within_back",
    )
    out_part = mm(gated_hat, out_rank, TN, bf16)
    dout = mm(gated_hat, plane_cot, NN, bf16)
    dstate_out, passed = pass_states(
        local_dstate.reshape(by_head), [hop_down(p) for p in reversed(range(planes - 1))],
        [(), (dgate_product, out_part), (dx,)] + [()] * (planes - 4), 1,
    )
    dgate_sum = over_planes(after(dgate_product, passed[1]))
    output = (activations + to_owner(out_part)).astype(bf16)
    gate_part = mm(dgate, gate_weight, CROSS, bf16)
    dstate_out = after(dstate_out, output, dout, gate_part)

    grad_conv, dsteps, grad_starts = call(
        state_back_kernel, rows,
        (conv, slope, info, logs, steps, step_slope, dmixed, dx, dmatrix, row_sums, dstate_out,
         state_in, params),
        [tall, tall, info_spec, row_spec, row_spec, row_spec, wide, wide, token_spec(2 * NSTATE),
         token_spec(3 * heads), state_spec, state_spec, fixed_spec(params.shape)],
        [shape((channels, count), bf16), shape((2 * heads, count), f32),
         shape((channels, LANES), bf16)],
        [tall, token_spec(2 * heads), fixed_spec((channels, LANES))],
        [pltpu.VMEM((width, SPAN), bf16)], name="state_back",
    )
    draw, dtaps = call(
        conv_back_kernel, rows,
        (raw, raw, grad_conv, over_heads(grad_starts, last_span), info, taps),
        [tall, halo_spec, tall, fixed_spec(grad_starts.shape), info_spec,
         fixed_spec(taps.shape)],
        [shape((channels, count), bf16), shape((TAPS + 1, channels, LANES), f32)],
        [tall, fixed_spec((TAPS + 1, channels, LANES))], name="conv_back",
    )

    dmain = jnp.concatenate([draw, dsteps[:heads].astype(bf16)], axis=0)
    dmain_product = rows_product(dmain)
    dmain_sum = over_planes(dmain_product)
    dgate_rows = rows_to_owner(dgate_sum)
    dmain_rows = rows_to_owner(after(dmain_sum, dgate_rows))
    dmain = after(dmain, dmain_product)
    grad_parts = []
    for lanes in (slice(0, half), slice(half, width_in)):
        part = mm(dmain, main_weight[lanes], CROSS) + gate_part[:, lanes].astype(f32)
        grad_parts.append(to_owner(part.astype(bf16)))
    grad_normed = restored(jnp.concatenate(grad_parts, axis=1)) * all_norm_gain
    grad_tokens = inverse * (
        grad_normed - normed * jnp.mean(grad_normed * normed, axis=-1, keepdims=True)
    )
    input_grad = (cotangent.astype(f32) + grad_tokens).astype(bf16)

    dout = after(dout, dgate_sum).reshape(groups, planes, 2, out_rows, width_in)
    dout_mine = by_core(dout[:, :, 0], dout[:, :, 1])
    dout_other = sibling(by_core(dout[:, :, 1], dout[:, :, 0]))

    def out_piece(i):
        at = (plane - i) % planes
        return sum(
            lax.dynamic_index_in_dim(a, at, 1, keepdims=False).astype(f32)
            for a in (dout_mine, dout_other)
        )

    running = out_piece(planes - 1)
    for i in reversed(range(planes - 1)):
        running = over_heads(running.astype(bf16), ring_down).astype(f32) + out_piece(i)
    if groups > 1:
        running = lax.psum_scatter(
            running, "head", scatter_dimension=0, axis_index_groups=same_place, tiled=True
        )
    out_weight_grad = running.reshape(out_rows, width_in)
    gate_gain_grad = jnp.sum(out_weight_grad * out_weight.astype(f32), axis=1) / gate_gain.astype(f32)

    tail = dmain_rows[..., channels:].transpose(1, 0, 2).reshape(span_rows, HEADS)
    in_weight_grad, norm_sums = finish(dgate_rows, dmain_rows, tail, in_weight)
    norm_gain_grad = jnp.sum(norm_sums, axis=1) / norm_gain.astype(f32)

    head_sums = jnp.sum(jnp.concatenate([dsteps, row_sums[2 * heads :]], axis=0), axis=1)
    taps_sum = jnp.sum(dtaps, axis=2)
    packed = after(jnp.concatenate([taps_sum.reshape(-1), head_sums]), *grad_parts)
    size = packed.shape[0]
    padded = -(-size // (8 * LANES)) * 8 * LANES
    packed = jnp.pad(packed, (0, padded - size)).reshape(padded // LANES, LANES)
    packed = jnp.broadcast_to(packed[None], (head_axis,) + packed.shape)
    packed = jnp.sum(lax.all_to_all(packed, "head", 0, 0, tiled=True), axis=0)
    total = all_rows(packed).reshape(rows, padded)
    taps_size = (TAPS + 1) * channels
    total_taps = total[:, :taps_size].reshape(rows, TAPS + 1, channels)
    all_taps_grad = jnp.concatenate(
        [
            total_taps[..., :width].transpose(1, 0, 2).reshape(TAPS + 1, DIN),
            jnp.sum(total_taps[..., width:], axis=0),
        ],
        axis=1,
    )
    total_heads = total[:, taps_size:size].reshape(rows, 3, heads)
    total_heads = total_heads.transpose(1, 0, 2).reshape(3, HEADS)
    return (
        output,
        input_grad,
        in_weight_grad,
        norm_gain_grad,
        out_weight_grad,
        gate_gain_grad,
        all_taps_grad[:TAPS],
        all_taps_grad[TAPS],
        total_heads[0],
        total_heads[1],
        total_heads[2],
    )


def solution(mesh):
    both = ("row", "head")
    return jax.shard_map(
        shards,
        mesh=mesh,
        in_specs=(
            P(both, None), P(both, None), P(both), P(both, None), P(both),
            P(), P(), P(), P(), P(),
            P("row", None), P("row"), P(both, None),
        ),
        out_specs=(
            P(both, None), P(both, None), P(both, None), P(both), P(both, None), P(both),
            P(), P(), P(), P(), P(),
        ),
        check_vma=False,
    )
```

time: 2320 us -> 587 us (0.25)
  waiting for transfers between devices: 1410 us -> 150 us
  matrix products: 262 us -> 88.9 us
  local copies, waits for them, and re-layouts: 259 us -> 91.4 us
  blocking collectives: 160 us -> 0 us
  other arithmetic: 147 us -> 52.5 us
  starting transfers between devices: 23 us -> 110 us
  Pallas kernels: 0 us -> 67.2 us
  loops' own time: 23.4 us -> 0 us
    reduce_scatter x3 -> x2, waiting for transfers between devices: 1090 us -> 0.02 us  [over_planes(): return lax.psum_scatter(product, 'head', scatter_dimension=0, tiled=True)]
    dot_general x118 -> x12, matrix products: 262 us -> 88.9 us  [the longest x11 88.6 us: mm(): return lax.dot_general(a, b, dims, preferred_element_type=f32).astype(out)]
    all_gather x3 -> x1, waiting for transfers between devices: 169 us -> 0.02 us  [shards(): out_rank = lax.all_gather(out_weight, 'head', axis=0, tiled=True)]
    dynamic_update_slice x37 -> x27, local copies, waits for them, and re-layouts: 140 us -> 40.3 us  [the longest x16 29 us: place_parts(): whole = lax.dynamic_update_slice(whole, one, (place * size, 0))]
    unnamed x2 -> x0, blocking collectives: 82.1 us -> none
    all_gather x1 -> x0, blocking collectives: 77.9 us -> none  [shards(): gain_rows = lax.all_gather(gate_gain, ('row', 'head'), axis=0, tiled=True)]
    ppermute x0 -> x38, waiting for transfers between devices: none -> 67.5 us  [the longest x31 63.7 us: over_heads(): return lax.ppermute(a, 'head', pairs)]
    pallas_call x0 -> x8, Pallas kernels: none -> 67.2 us  [the longest x7 65.6 us: call(): pl.pallas_call(kernel if used else lambda place_ref, *refs: kernel(*refs)...]
  transfers between devices with their start and end apart: 13 -> 54, of which waited for: 10 -> 19; matrix products, arithmetic and copies ran while one was open for 11% -> 37% of each run, Pallas kernels for 0% -> 9%
where the time goes in v1:
time: 587 us; the launch traced here: 576 us
  waiting for transfers between devices  150 us (26%)
  starting transfers between devices  110 us (19%)
  local copies, waits for them, and re-layouts  91.4 us (16%)
  matrix products  88.9 us (15%)
  Pallas kernels  67.2 us (11%)
  other arithmetic  52.5 us (9%)
  between operations  16.3 us (3%)
    dot_general x11, matrix products, mm(): return lax.dot_general(a, b, dims, preferred_element_type=f32).astype(out)  88.6 us
    pallas_call x7, Pallas kernels, call(): pl.pallas_call(kernel if used else lambda place_ref, *refs: kernel(*refs)...  65.6 us
    ppermute x31, waiting for transfers between devices, over_heads(): return lax.ppermute(a, 'head', pairs)  63.7 us
    ppermute x31, starting transfers between devices, over_heads(): return lax.ppermute(a, 'head', pairs)  43.5 us
    all_to_all x3, waiting for transfers between devices, to_owner(): lax.all_to_all(partial_sum.reshape(rows, SPAN, -1), 'row', 0, 0, tiled=True)  29.1 us
    dynamic_update_slice x16, local copies, waits for them, and re-layouts, place_parts(): whole = lax.dynamic_update_slice(whole, one, (place * size, 0))  29 us
    all_to_all x1, waiting for transfers between devices, everywhere(): lax.all_to_all(jnp.broadcast_to(a[None], (devices,) + a.shape), ('row', '...  25.2 us
    all_to_all x2, waiting for transfers between devices, column_part(): lax.all_to_all(cols, 'row', 0, 0, tiled=True).reshape(rows * span_rows, -1)  16.7 us
  transfers between devices with their start and end apart: 54, of which 19 were waited for; matrix products, arithmetic and copies ran while one was open for 37% of the time, Pallas kernels for 9%

profile of v1, /device:TPU:0, one launch (start us, length us, event | category | flops | bytes accessed | tf_op | source)
XLA Modules:
  0.0 576.3 jit_solution(14756739375997886305)
XLA Ops:
  19.8 7.8 %all-to-all-done = bf16[4,64,1280]{2,1,0:T(8,128)(2,1)} async-done(((bf16[4,64,1280]{2,1,0:T(8,128)(2,1)}), bf16[4,64,1280]{2,1,0:T(8,128)(2,1)}, u32[]{:S(2)}, u32[]{:S(2)}) %all-to-all-start) | async-done | bytes 655392 | tf_op jit(solution)/shard_map/all_to_all | solution.py:502
  40.0 25.2 %all-to-all-done.1 = f32[32,8,128]{2,1,0:T(8,128)S(1)} async-done(((f32[32,8,128]{2,1,0:T(8,128)}), f32[32,8,128]{2,1,0:T(8,128)S(1)}, u32[]{:S(2)}, u32[]{:S(2)}) %all-to-all-start.1) | async-done | bytes 131104 | tf_op jit(solution)/shard_map/all_to_all | solution.py:489
  68.9 7.7 %collective-permute-start.3 = (bf16[256,1280]{1,0:T(8,128)(2,1)}, bf16[256,1280]{1,0:T(8,128)(2,1)}, u32[]{:S(2)}, u32[]{:S(2)}) collective-permute-start(bf16[256,1280]{1,0:T(8,128)(2,1)} %copy-done.23), channel_id=1, source_target_pairs={{0,2},{1,3},{2,4},{3,5},{4,6},{5,7},{6,0},{7,1},{8,10},{9,11},{10,... | collective-permute-start | bytes 1966088 | tf_op jit(solution)/shard_map/ppermute | solution.py:451
  100.4 8.9 %all-to-all-done.2 = bf16[4,64,1024]{2,1,0:T(8,128)(2,1)} async-done(((bf16[4,64,1024]{2,1,0:T(8,128)(2,1)}), bf16[4,64,1024]{2,1,0:T(8,128)(2,1)}, u32[]{:S(2)}, u32[]{:S(2)}) %all-to-all-start.2) | async-done | bytes 524320 | tf_op jit(solution)/shard_map/all_to_all | solution.py:502
  168.6 12.3 %convolution_convert_fusion.1.refs_0_.refs_1_ = bf16[1280,1152]{1,0:T(8,128)(2,1)} fusion(bf16[1152,2048]{0,1:T(8,128)(2,1)} %dynamic_update_slice.99, bf16[2048,1296]{1,0:T(8,128)(2,1)} %constant_dynamic-update-slice_fusion.17), kind=kOutput, calls=%fused_computation.2 | convolution fusion | flops 6041272320 | bytes 12910592 | tf_op jit(solution)/shard_map/dot_general | solution.py:27
  180.8 10.2 %collective-permute-start.14 = (bf16[256,1024]{1,0:T(8,128)(2,1)}, bf16[256,1024]{1,0:T(8,128)(2,1)}, u32[]{:S(2)}, u32[]{:S(2)}) collective-permute-start(bf16[256,1024]{1,0:T(8,128)(2,1)} %collective-permute-done.13), channel_id=1, source_target_pairs={{0,2},{1,3},{2,4},{3,5},{4,6},{5,7},{6,0},{7,1},{8,10},{9,11},{10,... | collective-permute-start | bytes 1572872 | tf_op jit(solution)/shard_map/ppermute | solution.py:451
  192.8 10.4 %conv.1 = (bf16[1280,1024]{1,0:T(8,128)(2,1)}, bf16[1280,1024]{1,0:T(8,128)(2,1)}, bf16[4,1024,128]{2,1,0:T(8,128)(2,1)}) custom-call(s32[1]{0:T(128)} %constant.164.clone.1.place_ref, bf16[1280,1152]{1,0:T(8,128)(2,1)} %convolution_convert_fusion.1.refs_0_.refs_1_, bf16[1280,1152]{1,0:T(8,128)(2,1)} %convolution_convert_fusion.1.refs_0_.refs_1_, ...), custom_call_target="tpu_custom_call" | custom-call | tf_op jit(solution)/shard_map/conv/pallas_call | solution.py:360
  230.5 8.3 %fusion.10.refs_5_.refs_4_ = f32[1024,1024]{1,0:T(8,128)} fusion(bf16[2048,1024]{1,0:T(8,128)(2,1)} %constant_dynamic-update-slice_fusion, bf16[1152,2048]{0,1:T(8,128)(2,1)S(1)} %bitcast.160), kind=kOutput, calls=%fused_computation.24 | convolution fusion | flops 4294967296 | bytes 12582912 | tf_op jit(solution)/shard_map/dot_general | solution.py:27
  245.5 9.3 %convert_bitcast_fusion.refs_6_.refs_5_ = bf16[1024,1024]{1,0:T(8,128)(2,1)} fusion(bf16[1024,2048]{1,0:T(8,128)(2,1)} %bitcast.31, bf16[1024,2048]{1,0:T(8,128)(2,1)} %all-gather.2.cloned.1.call-done), kind=kOutput, calls=%fused_computation.40 | convolution fusion | flops 4296015872 | bytes 10485760 | tf_op jit(solution)/shard_map/dot_general | solution.py:27
  255.0 6.9 %mix.1 = (bf16[1024,1024]{1,0:T(8,128)(2,1)S(1)}, f32[8,1024]{1,0:T(8,128)S(1)}) custom-call(s32[1]{0:T(128)} %constant.164.clone.1.place_ref, bf16[1280,1024]{1,0:T(8,128)(2,1)} %get-tuple-element.78.refs_0_, f32[4,8,512]{2,1,0:T(8,128)S(1)} %all-to-all-done.4.refs_2_.refs_1_.refs_4_, f32[16,1024]{1,0:T(8,128)S(1)} %reshape.426.refs_4_.refs_2_.refs_3_, ...), custom_call_target="tpu_custom_call" | custom-call | tf_op jit(solution)/shard_map/mix/pallas_call | solution.py:360
  270.5 8.2 %gate.1 = (bf16[1024,1024]{1,0:T(8,128)(2,1)S(1)}, bf16[1024,1024]{1,0:T(8,128)(2,1)}, bf16[1024,1024]{1,0:T(8,128)(2,1)}, bf16[4,1024,128]{2,1,0:T(8,128)(2,1)S(1)}) custom-call(s32[1]{0:T(128)} %constant.164.clone.1.place_ref, bf16[1280,1024]{1,0:T(8,128)(2,1)} %get-tuple-element.78.refs_0_, f32[4,8,512]{2,1,0:T(8,128)S(1)} %all-to-all-done.4.refs_2_.refs_1_.refs_4_, ...), custom_call_target="tpu_custom_call" | custom-call | tf_op jit(solution)/shard_map/gate/pallas_call | solution.py:360
  280.0 9.4 %convolution_convert_fusion.4 = bf16[2048,1024]{1,0:T(8,128)(2,1)} fusion(bf16[1024,1024]{1,0:T(8,128)(2,1)} %get-tuple-element.95, bf16[1152,2048]{0,1:T(8,128)(2,1)} %dynamic_update_slice.99), kind=kOutput, calls=%fused_computation.10 | convolution fusion | flops 4297064448 | bytes 10485760 | tf_op jit(solution)/shard_map/dot_general | solution.py:27
  294.3 9.3 %convolution_convert_fusion.5 = bf16[1024,2048]{1,0:T(8,128)(2,1)} fusion(bf16[1024,1024]{1,0:T(8,128)(2,1)} %copy-done.9, bf16[1024,2048]{1,0:T(8,128)(2,1)} %all-gather.2.cloned.1.call-done), kind=kOutput, calls=%fused_computation.11 | convolution fusion | flops 4297064448 | bytes 10485760 | tf_op jit(solution)/shard_map/dot_general | solution.py:27
  308.7 12.3 %within_back.1 = (f32[1024,1024]{1,0:T(8,128)}, f32[256,1024]{1,0:T(8,128)S(1)}, f32[48,1024]{1,0:T(8,128)S(1)}) custom-call(s32[1]{0:T(128)} %constant.164.clone.1.place_ref, bf16[1280,1024]{1,0:T(8,128)(2,1)} %get-tuple-element.78.refs_0_, f32[4,8,512]{2,1,0:T(8,128)S(1)} %all-to-all-done.4.refs_2_.refs_1_.refs_4_, ...), custom_call_target="tpu_custom_call" | custom-call | tf_op jit(solution)/shard_map/within_back/pallas_call | solution.py:360
  323.3 8.4 %convolution_convert_fusion.2 = bf16[1024,2048]{1,0:T(8,128)(2,1)} fusion(bf16[1024,1024]{1,0:T(8,128)(2,1)S(1)} %copy-done.37, bf16[2048,1024]{1,0:T(8,128)(2,1)} %constant_dynamic-update-slice_fusion), kind=kOutput, calls=%fused_computation.8 | convolution fusion | flops 4297064448 | bytes 10485760 | tf_op jit(solution)/shard_map/dot_general | solution.py:27
  334.7 8.3 %convolution_convert_fusion.3 = bf16[1024,2048]{1,0:T(8,128)(2,1)} fusion(bf16[1024,1024]{1,0:T(8,128)(2,1)S(1)} %copy-done.10, bf16[1024,2048]{1,0:T(8,128)(2,1)} %bitcast.31), kind=kOutput, calls=%fused_computation.9 | convolution fusion | flops 4297064448 | bytes 10485760 | tf_op jit(solution)/shard_map/dot_general | solution.py:27
  343.0 43.6 %collective-permute-done.31 = bf16[4,8,64,128]{3,2,1,0:T(8,128)(2,1)S(1)} collective-permute-done((bf16[4,8,64,128]{3,2,1,0:T(8,128)(2,1)S(1)}, bf16[4,8,64,128]{3,2,1,0:T(8,128)(2,1)S(1)}, u32[]{:S(2)}, u32[]{:S(2)}) %collective-permute-start.31) | collective-permute-done | bytes 524320 | tf_op jit(solution)/shard_map/ppermute | solution.py:451
  396.1 8.5 %state_back.1 = (bf16[1280,1024]{1,0:T(8,128)(2,1)}, f32[32,1024]{1,0:T(8,128)S(1)}, bf16[1280,128]{1,0:T(8,128)(2,1)S(1)}) custom-call(s32[1]{0:T(128)} %constant.164.clone.1.place_ref, bf16[1280,1024]{1,0:T(8,128)(2,1)} %get-tuple-element.78.refs_0_, bf16[1280,1024]{1,0:T(8,128)(2,1)} %get-tuple-element.89.refs_1_, ...), custom_call_target="tpu_custom_call" | custom-call | tf_op jit(solution)/shard_map/state_back/pallas_call | solution.py:360
  408.2 13.9 %conv_back.1 = (bf16[1280,1024]{1,0:T(8,128)(2,1)S(1)}, f32[5,1280,128]{2,1,0:T(8,128)}) custom-call(s32[1]{0:T(128)} %constant.164.clone.1.place_ref, bf16[1280,1152]{1,0:T(8,128)(2,1)} %convolution_convert_fusion.1.refs_0_.refs_1_, bf16[1280,1152]{1,0:T(8,128)(2,1)} %convolution_convert_fusion.1.refs_0_.refs_1_, ...), custom_call_target="tpu_custom_call" | custom-call | tf_op jit(solution)/shard_map/conv_back/pallas_call | solution.py:360
  422.0 7.7 %convolution_convert_fusion = bf16[2048,1296]{0,1:T(8,128)(2,1)} fusion(bf16[1152,2048]{0,1:T(8,128)(2,1)S(1)} %bitcast.162, bf16[16,1024]{1,0:T(8,128)(2,1)S(1)} %slice.249, bf16[1280,1024]{1,0:T(8,128)(2,1)S(1)} %get-tuple-element.101), kind=kOutput, calls=%fused_computation.1 | convolution fusion | flops 5443780608 | bytes 12156928 | tf_op jit(solution)/shard_map/dot_general | solution.py:27
  432.0 7.5 %add_convert_fusion = bf16[1024,1024]{1,0:T(8,128)(2,1)} fusion(bf16[1024,2048]{1,0:T(8,128)(2,1)S(1)} %copy-done.45, bf16[1296,1024]{1,0:T(8,128)(2,1)S(1)} %pad_maximum_fusion, bf16[2048,1296]{1,0:T(8,128)(2,1)} %constant_dynamic-update-slice_fusion.17), kind=kOutput, calls=%fused_computation.5 | convolution fusion | flops 2721054720 | bytes 9732096 | tf_op jit(solution)/shard_map/dot_general | solution.py:27
  460.5 9.0 %all-to-all-done.8 = bf16[4,256,1024]{2,1,0:T(8,128)(2,1)} async-done(((bf16[4,256,1024]{2,1,0:T(8,128)(2,1)}), bf16[4,256,1024]{2,1,0:T(8,128)(2,1)}, u32[]{:S(2)}, u32[]{:S(2)}) %all-to-all-start.8) | async-done | bytes 2097184 | tf_op jit(solution)/shard_map/all_to_all | solution.py:706
  480.0 20.1 %all-to-all-done.7 = bf16[4,256,1024]{2,1,0:T(8,128)(2,1)} async-done(((bf16[4,256,1024]{2,1,0:T(8,128)(2,1)}), bf16[4,256,1024]{2,1,0:T(8,128)(2,1)}, u32[]{:S(2)}, u32[]{:S(2)}) %all-to-all-start.7) | async-done | bytes 2097184 | tf_op jit(solution)/shard_map/all_to_all | solution.py:706
  518.4 8.0 %all-to-all-done.11 = f32[8,56,128]{2,1,0:T(8,128)S(1)} async-done(((f32[8,56,128]{2,1,0:T(8,128)}), f32[8,56,128]{2,1,0:T(8,128)S(1)}, u32[]{:S(2)}, u32[]{:S(2)}) %all-to-all-start.11) | async-done | bytes 229408 | tf_op jit(solution)/shard_map/all_to_all | solution.py:807
  (390 shorter events, 278.7 us)
Async XLA Ops:
  7.3 238.2 %all-gather.2.cloned.1.call-start = ((), (), s32[]{:S(2)}) async-start(), calls=%async_computation.15 | async-start | bytes 4718592 | tf_op jit(solution)/shard_map/all_gather | solution.py:527
  27.6 37.5 %collective-permute-start.1 = (bf16[256,1280]{1,0:T(8,128)(2,1)}, bf16[256,1280]{1,0:T(8,128)(2,1)S(1)}, u32[]{:S(2)}, u32[]{:S(2)}) collective-permute-start(bf16[256,1280]{1,0:T(8,128)(2,1)} %bitcast.1), channel_id=1, source_target_pairs={{0,2},{1,3},{2,4},{3,5},{4,6},{5,7},{6,0},{7,1},{8,10},{9,11},{10,... | collective-permute-start | bytes 1966088 | tf_op jit(solution)/shard_map/ppermute | solution.py:451
  30.1 35.0 %all-to-all-start.1 = ((f32[32,8,128]{2,1,0:T(8,128)}), f32[32,8,128]{2,1,0:T(8,128)S(1)}, u32[]{:S(2)}, u32[]{:S(2)}) async-start(f32[32,8,128]{2,1,0:T(8,128)} %broadcast_in_dim.50), calls=%async_computation.1 | async-start | bytes 262144 | tf_op jit(solution)/shard_map/all_to_all | solution.py:489
  34.7 54.4 %collective-permute-start = (bf16[256,1280]{1,0:T(8,128)(2,1)}, bf16[256,1280]{1,0:T(8,128)(2,1)}, u32[]{:S(2)}, u32[]{:S(2)}) collective-permute-start(bf16[256,1280]{1,0:T(8,128)(2,1)} %bitcast.1), channel_id=1, source_target_pairs={{0,1},{1,0},{2,3},{3,2},{4,5},{5,4},{6,7},{7,6},{8,9},{9,8},{10,11... | collective-permute-start | bytes 1966088 | tf_op jit(solution)/shard_map/ppermute | solution.py:451
  68.9 27.4 %collective-permute-start.3 = (bf16[256,1280]{1,0:T(8,128)(2,1)}, bf16[256,1280]{1,0:T(8,128)(2,1)}, u32[]{:S(2)}, u32[]{:S(2)}) collective-permute-start(bf16[256,1280]{1,0:T(8,128)(2,1)} %copy-done.23), channel_id=1, source_target_pairs={{0,2},{1,3},{2,4},{3,5},{4,6},{5,7},{6,0},{7,1},{8,10},{9,11},{10,... | collective-permute-start | bytes 1966088 | tf_op jit(solution)/shard_map/ppermute | solution.py:451
  76.6 32.7 %collective-permute-start.6 = (bf16[256,2048]{0,1:T(8,128)(2,1)S(1)}, bf16[256,2048]{0,1:T(8,128)(2,1)S(1)}, u32[]{:S(2)}, u32[]{:S(2)}) collective-permute-start(bf16[256,2048]{0,1:T(8,128)(2,1)S(1)} %bitcast.153), channel_id=1, source_target_pairs={{0,16},{8,24},{16,0},{24,8},{1,17},{9,25},{17,1},{25,9},{2,18},{10... | collective-permute-start | bytes 3145736 | tf_op jit(solution)/shard_map/ppermute | solution.py:448
  78.3 31.1 %collective-permute-start.5 = (bf16[256,2048]{0,1:T(8,128)(2,1)S(1)}, bf16[256,2048]{0,1:T(8,128)(2,1)}, u32[]{:S(2)}, u32[]{:S(2)}) collective-permute-start(bf16[256,2048]{0,1:T(8,128)(2,1)S(1)} %bitcast.154), channel_id=1, source_target_pairs={{0,8},{8,0},{16,24},{24,16},{1,9},{9,1},{17,25},{25,17},{2,10},{10... | collective-permute-start | bytes 3145736 | tf_op jit(solution)/shard_map/ppermute | solution.py:448
  82.1 27.2 %all-to-all-start.2 = ((bf16[4,64,1024]{2,1,0:T(8,128)(2,1)}), bf16[4,64,1024]{2,1,0:T(8,128)(2,1)}, u32[]{:S(2)}, u32[]{:S(2)}) async-start(bf16[4,64,1024]{2,1,0:T(8,128)(2,1)} %copy.103), calls=%async_computation.2 | async-start | bytes 1048576 | tf_op jit(solution)/shard_map/all_to_all | solution.py:502
  96.4 34.0 %collective-permute-start.4 = (bf16[256,1280]{1,0:T(8,128)(2,1)}, bf16[256,1280]{1,0:T(8,128)(2,1)}, u32[]{:S(2)}, u32[]{:S(2)}) collective-permute-start(bf16[256,1280]{1,0:T(8,128)(2,1)} %collective-permute-done.3), channel_id=1, source_target_pairs={{0,1},{1,0},{2,3},{3,2},{4,5},{5,4},{6,7},{7,6},{8,9},{9,8},{10,11... | collective-permute-start | bytes 1966088 | tf_op jit(solution)/shard_map/ppermute | solution.py:451
  114.7 90.0 %collective-permute-start.19 = (bf16[256,1024]{1,0:T(8,128)(2,1)}, bf16[256,1024]{1,0:T(8,128)(2,1)}, u32[]{:S(2)}, u32[]{:S(2)}) collective-permute-start(bf16[256,1024]{1,0:T(8,128)(2,1)} %bitcast.8), channel_id=1, source_target_pairs={{0,1},{1,0},{2,3},{3,2},{4,5},{5,4},{6,7},{7,6},{8,9},{9,8},{10,11... | collective-permute-start | bytes 1572872 | tf_op jit(solution)/shard_map/ppermute | solution.py:451
  114.7 39.2 %collective-permute-start.11 = (bf16[256,1024]{1,0:T(8,128)(2,1)}, bf16[256,1024]{1,0:T(8,128)(2,1)}, u32[]{:S(2)}, u32[]{:S(2)}) collective-permute-start(bf16[256,1024]{1,0:T(8,128)(2,1)} %bitcast.8), channel_id=1, source_target_pairs={{0,2},{1,3},{2,4},{3,5},{4,6},{5,7},{6,0},{7,1},{8,10},{9,11},{10,... | collective-permute-start | bytes 1572872 | tf_op jit(solution)/shard_map/ppermute | solution.py:451
  119.6 46.1 %collective-permute-start.8 = (bf16[256,1280]{1,0:T(8,128)(2,1)}, bf16[256,1280]{1,0:T(8,128)(2,1)}, u32[]{:S(2)}, u32[]{:S(2)}) collective-permute-start(bf16[256,1280]{1,0:T(8,128)(2,1)} %collective-permute-done.7), channel_id=1, source_target_pairs={{0,1},{1,0},{2,3},{3,2},{4,5},{5,4},{6,7},{7,6},{8,9},{9,8},{10,11... | collective-permute-start | bytes 1966088 | tf_op jit(solution)/shard_map/ppermute | solution.py:451
  124.9 28.9 %collective-permute-start.10 = (bf16[128,2048]{0,1:T(8,128)(2,1)}, bf16[128,2048]{0,1:T(8,128)(2,1)S(1)}, u32[]{:S(2)}, u32[]{:S(2)}) collective-permute-start(bf16[128,2048]{0,1:T(8,128)(2,1)} %slice.131), channel_id=1, source_target_pairs={{0,8},{8,0},{16,24},{24,16},{1,9},{9,1},{17,25},{25,17},{2,10},{10... | collective-permute-start | bytes 1572872 | tf_op jit(solution)/shard_map/ppermute | solution.py:448
  148.7 90.5 %all-to-all-start.5 = ((bf16[4,256,2048]{2,1,0:T(8,128)(2,1)}), bf16[4,256,2048]{2,1,0:T(8,128)(2,1)}, u32[]{:S(2)}, u32[]{:S(2)}) async-start(bf16[4,256,2048]{2,1,0:T(8,128)(2,1)} %broadcast_in_dim.113), calls=%async_computation.5 | async-start | bytes 8388608 | tf_op jit(solution)/shard_map/all_to_all | solution.py:479
  153.6 290.7 %reduce-scatter.3.cloned.1.call-start = ((), (), s32[]{:S(2)}) async-start(), calls=%async_computation.16 | async-start | bytes 4718592 | tf_op jit(solution)/shard_map/reduce_scatter | solution.py:713
  153.9 62.7 %collective-permute-start.20 = (bf16[256,1024]{1,0:T(8,128)(2,1)}, bf16[256,1024]{1,0:T(8,128)(2,1)}, u32[]{:S(2)}, u32[]{:S(2)}) collective-permute-start(bf16[256,1024]{1,0:T(8,128)(2,1)} %collective-permute-done.11), channel_id=1, source_target_pairs={{0,1},{1,0},{2,3},{3,2},{4,5},{5,4},{6,7},{7,6},{8,9},{9,8},{10,11... | collective-permute-start | bytes 1572872 | tf_op jit(solution)/shard_map/ppermute | solution.py:451
  153.9 26.9 %collective-permute-start.13 = (bf16[256,1024]{1,0:T(8,128)(2,1)}, bf16[256,1024]{1,0:T(8,128)(2,1)}, u32[]{:S(2)}, u32[]{:S(2)}) collective-permute-start(bf16[256,1024]{1,0:T(8,128)(2,1)} %collective-permute-done.11), channel_id=1, source_target_pairs={{0,2},{1,3},{2,4},{3,5},{4,6},{5,7},{6,0},{7,1},{8,10},{9,11},{10,... | collective-permute-start | bytes 1572872 | tf_op jit(solution)/shard_map/ppermute | solution.py:451
  292.7 28.3 %collective-permute-start.29 = (bf16[4,8,64,128]{3,2,1,0:T(8,128)(2,1)}, bf16[4,8,64,128]{3,2,1,0:T(8,128)(2,1)}, u32[]{:S(2)}, u32[]{:S(2)}) collective-permute-start(bf16[4,8,64,128]{3,2,1,0:T(8,128)(2,1)} %get-tuple-element.138), channel_id=1, source_target_pairs={{6,4},{7,5},{14,12},{15,13},{22,20},{23,21},{30,28},{31,29}} | collective-permute-start | bytes 1572872 | tf_op jit(solution)/shard_map/ppermute | solution.py:451
  303.7 85.0 %all-to-all-start.6 = ((bf16[4,256,2048]{2,1,0:T(8,128)(2,1)}), bf16[4,256,2048]{2,1,0:T(8,128)(2,1)}, u32[]{:S(2)}, u32[]{:S(2)}) async-start(bf16[4,256,2048]{2,1,0:T(8,128)(2,1)} %bitcast.164), calls=%async_computation.6 | async-start | bytes 8388608 | tf_op jit(solution)/shard_map/all_to_all | solution.py:706
  308.6 243.0 %reduce-scatter.5.cloned.1.call-start = ((), (), s32[]{:S(2)}) async-start(), calls=%async_computation.17 | async-start | bytes 5971968 | tf_op jit(solution)/shard_map/reduce_scatter | solution.py:713
  333.2 53.4 %collective-permute-start.31 = (bf16[4,8,64,128]{3,2,1,0:T(8,128)(2,1)S(1)}, bf16[4,8,64,128]{3,2,1,0:T(8,128)(2,1)S(1)}, u32[]{:S(2)}, u32[]{:S(2)}) collective-permute-start(bf16[4,8,64,128]{3,2,1,0:T(8,128)(2,1)S(1)} %add_convert_fusion.5), channel_id=1, source_target_pairs={{2,0},{3,1},{10,8},{11,9},{18,16},{19,17},{26,24},{27,25}} | collective-permute-start | bytes 1572872 | tf_op jit(solution)/shard_map/ppermute | solution.py:451
  439.5 30.0 %all-to-all-start.8 = ((bf16[4,256,1024]{2,1,0:T(8,128)(2,1)}), bf16[4,256,1024]{2,1,0:T(8,128)(2,1)}, u32[]{:S(2)}, u32[]{:S(2)}) async-start(bf16[4,256,1024]{2,1,0:T(8,128)(2,1)} %bitcast.41), calls=%async_computation.8 | async-start | bytes 4194304 | tf_op jit(solution)/shard_map/all_to_all | solution.py:706
  448.3 55.4 %collective-permute-start.34 = (bf16[1,4,128,2048]{3,2,1,0:T(8,128)(2,1)}, bf16[1,4,128,2048]{3,2,1,0:T(8,128)(2,1)}, u32[]{:S(2)}, u32[]{:S(2)}) collective-permute-start(bf16[1,4,128,2048]{3,2,1,0:T(8,128)(2,1)} %get-tuple-element.147), channel_id=1, source_target_pairs={{0,1},{1,0},{2,3},{3,2},{4,5},{5,4},{6,7},{7,6},{8,9},{9,8},{10,11... | collective-permute-start | bytes 6291464 | tf_op jit(solution)/shard_map/ppermute | solution.py:451
  469.5 30.6 %all-to-all-start.7 = ((bf16[4,256,1024]{2,1,0:T(8,128)(2,1)}), bf16[4,256,1024]{2,1,0:T(8,128)(2,1)}, u32[]{:S(2)}, u32[]{:S(2)}) async-start(bf16[4,256,1024]{2,1,0:T(8,128)(2,1)} %bitcast.167), calls=%async_computation.7 | async-start | bytes 4194304 | tf_op jit(solution)/shard_map/all_to_all | solution.py:706
  (84 other events, 1319.8 us)
Sparse Core Ops, SparseCore 0:
  9.7 66.4 all-gather.1
  289.5 77.1 reduce-scatter.2
  429.9 63.4 reduce-scatter.4

commit v2 on v1

--- a/solution.py
+++ b/solution.py
@@ -373,18 +373,25 @@
     )(place, *operands)
 
 
-def finish_kernel(gate_ref, main_ref, tail_ref, weight_ref, grad_ref, sums_ref):
-    total = jnp.zeros(sums_ref.shape, f32)
-    ranks, _, width = gate_ref.shape
+def finish_kernel(
+    place_ref, *refs
+):
+    *gate_refs, main_ref, tail_ref, weight_ref, grad_ref, sums_ref = refs
+    ranks, _, columns = main_ref.shape
+    width = gate_refs[0].shape[1]
     matrix = slice(width, width + 2 * NSTATE)
-    parts = [(gate_ref[q].astype(f32), q * width) for q in range(ranks)]
+    parts = [
+        (ref[...].astype(f32), pl.multiple_of(jnp.bitwise_xor(place_ref[0], k) * width, LANES))
+        for k, ref in enumerate(gate_refs)
+    ]
     parts += [(main_ref[q, :, :width].astype(f32), (ranks + q) * width) for q in range(ranks)]
     parts += [(sum(main_ref[q, :, matrix].astype(f32) for q in range(ranks)), 2 * ranks * width)]
     parts += [(tail_ref[...].astype(f32), 2 * ranks * width + 2 * NSTATE)]
+    total = jnp.zeros(sums_ref.shape, f32)
     for value, start in parts:
         size = value.shape[1]
-        grad_ref[:, start : start + size] = value
-        product = value * weight_ref[:, start : start + size].astype(f32)
+        grad_ref[:, pl.ds(start, size)] = value
+        product = value * weight_ref[:, pl.ds(start, size)].astype(f32)
         whole = size // LANES * LANES
         for i in range(0, whole, LANES):
             total = total + product[:, i : i + LANES]
@@ -394,25 +401,32 @@
     sums_ref[...] = total
 
 
-def finish(gate_rows, main_rows, tail, weight):
-    span_rows = weight.shape[0]
-    return pl.pallas_call(
-        finish_kernel,
-        out_shape=[
-            jax.ShapeDtypeStruct(weight.shape, f32),
-            jax.ShapeDtypeStruct((span_rows, LANES), f32),
-        ],
-        compiler_params=pltpu.CompilerParams(vmem_limit_bytes=50 * 1024 * 1024),
-        name="finish",
-    )(gate_rows, main_rows, tail, weight)
+def finish(place, gate_rows, main_rows, tail, weight):
+    operands = (*gate_rows, main_rows, tail, weight)
+    outs = [
+        jax.ShapeDtypeStruct(weight.shape, f32),
+        jax.ShapeDtypeStruct((weight.shape[0], LANES), f32),
+    ]
+    return call(
+        finish_kernel, 1, operands, [fixed_spec(a.shape) for a in operands],
+        outs, [fixed_spec(o.shape) for o in outs], name="finish", place=place,
+    )
 
 
 def tie(*values):
     return lax.optimization_barrier(values)
 
 
-def after(value, *others):
-    return tie(value, *others)[0]
+class Clock:
+    def __init__(self):
+        self.last = ()
+
+    def now(self, *values):
+        out = tie(*values, *self.last)[: len(values)]
+        return out if len(out) > 1 else out[0]
+
+    def until(self, *values):
+        self.last = values
 
 
 def shards(
@@ -444,6 +458,9 @@
     group = head // spans
     first = core == 0
 
+    clock = Clock()
+    now, until = clock.now, clock.until
+
     def across_rows(a, mask):
         return lax.ppermute(a, "row", [(i, i ^ mask) for i in range(rows)])
 
@@ -501,9 +518,15 @@
     def column_part(cols):
         return lax.all_to_all(cols, "row", 0, 0, tiled=True).reshape(rows * span_rows, -1)
 
-    def place_parts(whole, pieces):
+    def zeros(size, *since):
+        zero = tie(jnp.zeros((), bf16), *since)[0]
+        return jnp.broadcast_to(zero, size)
+
+    def place_parts(whole, pieces, since=()):
         size = pieces[0][0].shape[0]
         for i, both in enumerate(pieces):
+            if i < len(since):
+                whole = tie(whole, since[i])[0]
             for e, part in enumerate(both):
                 at = (plane - i) % planes * 2 + (core ^ e)
                 if groups == 1:
@@ -524,73 +547,94 @@
     matrix_cols = in_weight[:, 2 * DIN : 2 * DIN + 2 * NSTATE]
     matrix_cols = jnp.broadcast_to(matrix_cols[None], (rows, span_rows, 2 * NSTATE))
     main = [column_part(jnp.concatenate([value_cols, matrix_cols], axis=2))]
-    out_rank = lax.all_gather(out_weight, "head", axis=0, tiled=True)
-
-    gains = jnp.stack(
-        [jnp.pad(g.astype(f32), (0, LANES - g.shape[0])) for g in (norm_gain, gate_gain)]
-    )
-    gains = everywhere(after(jnp.pad(gains, ((0, 6), (0, 0))), main[0]))
-    main.append(up_ring(main[0]))
-    gains, main[1] = tie(gains, main[1])
-    all_norm_gain = gains[:, 0, :span_rows].reshape(1, width_in)
-    rank_gain = gains[:, 1, :out_rows].reshape(rows, width)
-    rank_gain = lax.dynamic_index_in_dim(rank_gain, row, 0, keepdims=False)
+    out_parts = [out_weight, up_ring(out_weight)]
+    gate_cols = tie(in_weight[:, :DIN], main[0])[0]
+    gate_parts = [column_part(gate_cols.reshape(span_rows, rows, width).transpose(1, 0, 2))]
+    until(main[0], out_parts[1], gate_parts[0])
+
+    segments = jnp.cumsum(boundary, axis=1)
+    used = (jnp.arange(seq)[None, :] < fill[:, None]).astype(jnp.int32)
+    edge = ((0, 0), (LANES, LANES))
+    says = [
+        jnp.pad(part, edge, constant_values=value)
+        for part, value in ((segments // LANES, -1), (segments % LANES, 0), (used, 0))
+    ]
+    says = jnp.stack(says, axis=1).astype(bf16)
+    reach = SPAN + 2 * LANES
+    says = jnp.stack(
+        [
+            says[h // spans, :, h % spans * SPAN : h % spans * SPAN + reach]
+            for h in range(head_axis)
+        ]
+    ).reshape(1, head_axis, -1, LANES)
+    steps_cols = in_weight[:, 2 * DIN + 2 * NSTATE :].T.reshape(rows, 1, heads, span_rows)
+    both_gains = [jnp.pad(g, (0, LANES - g.shape[0])) for g in (norm_gain, gate_gain)]
+    table = [
+        jnp.pad(steps_cols, ((0, 0), (0, 0), (0, 0), (0, LANES - span_rows))),
+        jnp.stack(both_gains).reshape(1, 1, 2, LANES),
+        says,
+    ]
+    table = jnp.concatenate(
+        [jnp.broadcast_to(t, (rows, head_axis) + t.shape[2:]) for t in table], axis=2
+    )
+    table = jnp.pad(table, ((0, 0), (0, 0), (0, -table.shape[2] % 16), (0, 0)))
+    table = now(table.reshape((devices,) + table.shape[2:]))
+    table = lax.all_to_all(table, ("row", "head"), 0, 0, tiled=True)
+    main.append(up_ring(now(main[0])))
+    main_others = [sibling(now(main[0]))]
+    until(table, main[1], main_others[0])
+    table = table.reshape((rows, head_axis) + table.shape[1:])
+    step_weight = table[:, :, :heads, :span_rows].transpose(2, 1, 0, 3).reshape(heads, width_in)
+    all_norm_gain = table[:, :, heads, :span_rows].reshape(1, width_in).astype(f32)
+    rank_gain = table[:, :, heads + 1, :out_rows].reshape(rows, width)
+    rank_gain = lax.dynamic_index_in_dim(rank_gain, row, 0, keepdims=False).astype(f32)
     rank_gain = jnp.broadcast_to(rank_gain[:, None], (width, LANES))
+    info = table[:, 0, heads + 2 : heads + 2 + 3 * reach // LANES].astype(f32)
+    info = info.reshape(rows, 3, reach)
+    info = jnp.stack([info[:, 0] * LANES + info[:, 1], info[:, 2]], axis=1)
+    info = jnp.pad(info, ((0, 0), (0, 6), (0, 0)))
 
     activations = tokens.astype(f32)
     inverse = lax.rsqrt(jnp.mean(activations * activations, axis=-1, keepdims=True) + epsilon)
     normed = activations * inverse
-    projected_in = arranged((normed * all_norm_gain).astype(bf16))
-    projected_in, main[1] = tie(projected_in, main[1])
+    projected_in = arranged((normed * now(all_norm_gain)).astype(bf16))
+    gain_arranged = arranged(all_norm_gain)
+    main.append(up_ring(now(main[1])))
+    main_others.append(sibling(now(main[1])))
     cut = SPAN // 2
     from_x, from_y = across_rows(projected_in, 1), across_rows(projected_in, 2)
-    gate_cols = after(in_weight[:, :DIN], gains)
-    gate_parts = [column_part(gate_cols.reshape(span_rows, rows, width).transpose(1, 0, 2))]
-    for _ in range(planes - 2):
-        main.append(up_ring(main[-1]))
-    from_x, from_y, gate_parts[0], main[-1] = tie(from_x, from_y, gate_parts[0], main[-1])
-
-    x_far, y_far = across_rows(from_x[:cut], 2), across_rows(from_y[cut:], 1)
-    steps_cols = after(in_weight[:, 2 * DIN + 2 * NSTATE :], main[-1]).T
-    steps_cols = steps_cols.reshape(rows, 1, heads, span_rows)
-    steps_cols = jnp.broadcast_to(steps_cols, (rows, head_axis, heads, span_rows))
-    steps_cols = lax.all_to_all(
-        steps_cols.reshape(devices, heads, span_rows), ("row", "head"), 0, 0, tiled=True
-    )
-    step_weight = steps_cols.reshape(rows, head_axis, heads, span_rows).transpose(2, 1, 0, 3)
-    step_weight = step_weight.reshape(heads, width_in)
-    gate_parts.append(up_ring(gate_parts[0]))
-    x_far, y_far, step_weight, gate_parts[1] = tie(x_far, y_far, step_weight, gate_parts[1])
-    main_weight = jnp.zeros((width_in, channels + heads), bf16)
-    main_weight = place_parts(main_weight, [(part, sibling(part)) for part in main])
+    out_parts.append(up_ring(now(out_parts[1])))
+    until(from_x, from_y, main[-1], main_others[-1], out_parts[-1])
+
+    far_x, far_y = now(from_x[:cut], from_y[cut:])
+    x_far, y_far = across_rows(far_x, 2), across_rows(far_y, 1)
+    for _ in range(planes - 3):
+        main_others.append(sibling(now(main[-1])))
+        main.append(up_ring(now(main[-1])))
+    until(x_far, y_far, main[-1], main_others[-1])
+    main_others.append(sibling(now(main[-1])))
+    main_weight = zeros((width_in, channels + heads), main[1])
+    main_weight = place_parts(
+        main_weight, list(zip(main, main_others)), [main[1], main[2]]
+    )
     main_weight = lax.dynamic_update_slice(main_weight, step_weight.T, (0, channels))
 
-    plane_in = jnp.zeros((count + LANES, width_in), bf16)
-    ends_in = jnp.zeros((rows, 4, width_in), bf16)
-    for part, source, start in (
-        (projected_in, row, 0), (from_x, row ^ 1, 0), (from_y, row ^ 2, 0),
-        (x_far, row ^ 3, 0), (y_far, row ^ 3, cut),
-    ):
-        plane_in = lax.dynamic_update_slice(plane_in, part, (source * SPAN + start, 0))
-        if start + part.shape[0] == SPAN:
-            ends_in = lax.dynamic_update_slice(ends_in, part[-4:][None], (source, 0, 0))
+    def of_plane(since, mine, x, y, far_of_x, far_of_y):
+        whole = zeros((count, width_in), since)
+        ends = jnp.zeros((rows, 4, width_in), bf16)
+        for part, source, start in (
+            (mine, row, 0), (x, row ^ 1, 0), (y, row ^ 2, 0),
+            (far_of_x, row ^ 3, 0), (far_of_y, row ^ 3, cut),
+        ):
+            whole = lax.dynamic_update_slice(whole, part, (source * SPAN + start, 0))
+            if start + part.shape[0] == SPAN:
+                ends = lax.dynamic_update_slice(ends, part[-4:][None], (source, 0, 0))
+        return whole, ends
+
+    plane_in, ends_in = of_plane(main[2], projected_in, from_x, from_y, x_far, y_far)
     halo_in = over_heads(ends_in.reshape(4 * rows, width_in), next_span)
-    extended_in = lax.dynamic_update_slice(plane_in, halo_in, (count + 0 * row, 0))
-    plane_in = extended_in[:count]
-
-    segments = jnp.cumsum(boundary, axis=1).astype(f32)
-    used = (jnp.arange(seq)[None, :] < fill[:, None]).astype(f32)
-    says = jnp.stack(
-        [
-            jnp.pad(segments, ((0, 0), (LANES, LANES)), constant_values=-1.0),
-            jnp.pad(used, ((0, 0), (LANES, LANES))),
-        ],
-        axis=1,
-    )
-    says = lax.dynamic_slice(says, (group, 0, span * SPAN), (1, 2, SPAN + 2 * LANES))[0]
-    info = all_rows(after(jnp.pad(says, ((0, 6), (0, 0))), steps_cols))
-
-    plane_cot = all_rows(after(cotangent, info)).reshape(count, width_in)
+    gate_parts.append(up_ring(now(gate_parts[0])))
+    cot_x, cot_y = across_rows(now(cotangent), 1), across_rows(now(cotangent), 2)
 
     local_step = lax.dynamic_slice_in_dim(dt_bias, row * heads, heads, 0)
     local_rate = -jnp.exp(lax.dynamic_slice_in_dim(a_log, row * heads, heads, 0))
@@ -620,10 +664,12 @@
     )
     taps = jnp.pad(taps.T, ((0, 0), (0, LANES - TAPS - 1)))
 
-    raw = mm(main_weight[:, :channels], extended_in, CROSS, bf16)
-    gate_parts.append(up_ring(gate_parts[1]))
-    raw, gate_parts[2] = tie(raw, gate_parts[2])
-    halo_spec = pl.BlockSpec((channels, LANES), lambda k, c: (0, count // LANES))
+    raw = mm(main_weight[:, :channels], plane_in, CROSS, bf16)
+    halo = mm(main_weight[:, :channels], halo_in, CROSS, bf16)
+    until(raw, halo_in, gate_parts[1])
+    gate_parts.append(up_ring(now(gate_parts[1])))
+    halo_in = jnp.pad(now(halo_in), ((0, LANES - 4 * rows), (0, 0)))
+    halo = mm(main_weight[:, :channels], halo_in, CROSS, bf16)
     shape = jax.ShapeDtypeStruct
     info_spec = cell_spec(info.shape[1:])
     state_spec = cell_spec((width, NSTATE))
@@ -634,22 +680,16 @@
     tall = token_spec(channels)
     low_wide = shape((width, count), bf16)
     conv, slope, local_state = call(
-        conv_kernel, rows, (raw, raw, info, steps, logs, taps),
-        [tall, halo_spec, info_spec, row_spec, row_spec, fixed_spec(taps.shape)],
+        conv_kernel, rows, (raw, halo, info, steps, logs, taps),
+        [tall, fixed_spec(halo.shape), info_spec, row_spec, row_spec, fixed_spec(taps.shape)],
         [shape((channels, count), bf16), shape((channels, count), bf16), states],
         [tall, tall, state_spec],
         [pltpu.VMEM((width, SPAN), bf16)], name="conv",
     )
 
-    for _ in range(planes - 3):
-        gate_parts.append(up_ring(gate_parts[-1]))
-    local_state, gate_parts[-1] = tie(local_state, gate_parts[-1])
-    gate_weight = place_parts(
-        jnp.zeros((width_in, width), bf16), [(part, sibling(part)) for part in gate_parts]
-    )
-
-    def pass_states(mine, hops, beside, near):
-        other = sibling(mine)
+    until(local_state, gate_parts[2], cot_x, cot_y)
+
+    def pass_states(mine, hops, beside, near, other):
         is_near = core == near
 
         def own_heads(a):
@@ -660,31 +700,63 @@
         ) * own_heads(jnp.where(is_near, mine, other))
         keep_half = own_heads(keep_plane)
         got = jnp.zeros((), f32)
-        passed = []
-        for hop, others in zip(hops, beside):
-            running = after((total + keep_half * got).astype(bf16), *others)
-            got = got + over_heads(running, hop).astype(f32)
-            passed.append(got)
-        got = got.astype(bf16)
+        for hop, step in zip(hops, beside):
+            running = now((total + keep_half * got).astype(bf16))
+            until(running)
+            passed = over_heads(running, hop)
+            until(passed, *step())
+            got = got + passed.astype(f32)
+        got = now(got.astype(bf16))
         rest = sibling(got)
         whole = by_core(
             jnp.concatenate([got, rest], axis=1), jnp.concatenate([rest, got], axis=1)
         )
         through = (other.astype(f32) + keep_other * whole.astype(f32)).astype(bf16)
-        return jnp.where(is_near, whole, through).reshape(states.shape), passed
-
-    within = call(
-        within_kernel, rows, (conv, info, logs, shifted_logs),
-        [tall, info_spec, row_spec, row_spec],
-        shape((width, count), f32), wide, name="within",
-    )
-    gate = mm(gate_weight, plane_in, CROSS)
-    grad_hat = mm(out_rank, plane_cot, NT, bf16)
-
-    state_in, _ = pass_states(
-        local_state.reshape(by_head), [hop_up(p) for p in range(planes - 1)],
-        [(), (within,), (gate, plane_cot)] + [()] * (planes - 4), 0,
-    )
+        return jnp.where(is_near, whole, through).reshape(states.shape)
+
+    seen = {}
+
+    def within_step():
+        seen["within"] = call(
+            within_kernel, rows, (conv, info, logs, now(shifted_logs)),
+            [tall, info_spec, row_spec, row_spec],
+            shape((width, count), f32), wide, name="within",
+        )
+        for _ in range(planes - 3):
+            gate_parts.append(up_ring(now(gate_parts[-1])))
+        seen["far"] = across_rows(now(cot_x[:cut]), 2), across_rows(now(cot_y[cut:]), 1)
+        return (seen["within"], gate_parts[-1]) + seen["far"]
+
+    def gate_step():
+        others = [sibling(now(part)) for part in gate_parts]
+        gate_weight = place_parts(
+            zeros((width_in, width), others[0]), list(zip(gate_parts, others))
+        )
+        seen["gate_weight"] = gate_weight
+        seen["gate"] = mm(gate_weight, now(plane_in), CROSS)
+        for _ in range(planes - 3):
+            out_parts.append(up_ring(now(out_parts[-1])))
+        return seen["gate"], out_parts[-1]
+
+    def hat_step():
+        far = now(*seen["far"])
+        seen["cot"], _ = of_plane(far[0], cotangent, cot_x, cot_y, *far)
+        out_others = [sibling(now(part)) for part in out_parts]
+        seen["out_rank"] = place_parts(
+            zeros((width, width_in), far[0]), list(zip(out_parts, out_others))
+        )
+        seen["hat"] = mm(seen["out_rank"], seen["cot"], NT, bf16)
+        return (seen["hat"],)
+
+    local_state = local_state.reshape(by_head)
+    other_state = sibling(now(local_state))
+    until(other_state)
+    state_in = pass_states(
+        local_state, [hop_up(p) for p in range(planes - 1)], [within_step, gate_step, hat_step], 0,
+        other_state,
+    )
+    within, gate, grad_hat = seen["within"], seen["gate"], seen["hat"]
+    gate_weight, plane_cot, out_rank = seen["gate_weight"], seen["cot"], seen["out_rank"]
 
     mixed, sums = call(
         mix_kernel, rows, (conv, info, logs, state_in, within, gate, grad_hat, params, rank_gain),
@@ -712,29 +784,41 @@
     def over_planes(product):
         return lax.psum_scatter(product, "head", scatter_dimension=0, tiled=True)
 
-    def rows_to_owner(summed):
-        return lax.all_to_all(summed.reshape(rows, span_rows, -1), "row", 0, 0, tiled=True)
-
-    dgate_product = rows_product(dgate)
-    dx, dmatrix, row_sums = call(
-        within_back_kernel, rows, (conv, info, logs, shifted_logs, dmixed, state_in),
-        [tall, info_spec, row_spec, row_spec, wide, state_spec],
-        [shape((width, count), f32), shape((2 * NSTATE, count), f32), shape((3 * heads, count), f32)],
-        [wide, token_spec(2 * NSTATE), token_spec(3 * heads)],
-        [pltpu.VMEM((width, SPAN), bf16), pltpu.VMEM((LANES, LANES), f32),
-         pltpu.VMEM((SPAN, LANES), f32)],
-        name="within_back",
-    )
-    out_part = mm(gated_hat, out_rank, TN, bf16)
-    dout = mm(gated_hat, plane_cot, NN, bf16)
-    dstate_out, passed = pass_states(
-        local_dstate.reshape(by_head), [hop_down(p) for p in reversed(range(planes - 1))],
-        [(), (dgate_product, out_part), (dx,)] + [()] * (planes - 4), 1,
-    )
-    dgate_sum = over_planes(after(dgate_product, passed[1]))
-    output = (activations + to_owner(out_part)).astype(bf16)
-    gate_part = mm(dgate, gate_weight, CROSS, bf16)
-    dstate_out = after(dstate_out, output, dout, gate_part)
+    def dgate_step():
+        seen["dgate"] = rows_product(now(dgate))
+        out = mm(now(gated_hat), out_rank, TN, bf16)
+        seen["out"] = lax.psum_scatter(out, "row", scatter_dimension=0, tiled=True)
+        return seen["dgate"], out
+
+    def within_back_step():
+        seen["back"] = call(
+            within_back_kernel, rows, (conv, info, logs, shifted_logs, now(dmixed), state_in),
+            [tall, info_spec, row_spec, row_spec, wide, state_spec],
+            [shape((width, count), f32), shape((2 * NSTATE, count), f32),
+             shape((3 * heads, count), f32)],
+            [wide, token_spec(2 * NSTATE), token_spec(3 * heads)],
+            [pltpu.VMEM((width, SPAN), bf16), pltpu.VMEM((LANES, LANES), f32),
+             pltpu.VMEM((SPAN, LANES), f32)],
+            name="within_back",
+        )
+        return seen["back"][:1]
+
+    def out_step():
+        seen["dgate_sum"] = over_planes(now(seen["dgate"]))
+        seen["dout"] = mm(now(gated_hat), plane_cot, NN, bf16)
+        seen["gate_part"] = mm(now(dgate), gate_weight, CROSS, bf16)
+        seen["own"] = arranged(now(normed)), arranged(now(cotangent))
+        return (seen["dout"], seen["gate_part"]) + seen["own"]
+
+    local_dstate = local_dstate.reshape(by_head)
+    other_dstate = sibling(local_dstate)
+    until(other_dstate)
+    dstate_out = pass_states(
+        local_dstate, [hop_down(p) for p in reversed(range(planes - 1))],
+        [dgate_step, within_back_step, out_step], 1, other_dstate,
+    )
+    dx, dmatrix, row_sums = seen["back"]
+    output = (activations + seen["out"].astype(f32)).astype(bf16)
 
     grad_conv, dsteps, grad_starts = call(
         state_back_kernel, rows,
@@ -747,34 +831,13 @@
         [tall, token_spec(2 * heads), fixed_spec((channels, LANES))],
         [pltpu.VMEM((width, SPAN), bf16)], name="state_back",
     )
-    draw, dtaps = call(
-        conv_back_kernel, rows,
-        (raw, raw, grad_conv, over_heads(grad_starts, last_span), info, taps),
-        [tall, halo_spec, tall, fixed_spec(grad_starts.shape), info_spec,
-         fixed_spec(taps.shape)],
-        [shape((channels, count), bf16), shape((TAPS + 1, channels, LANES), f32)],
-        [tall, fixed_spec((TAPS + 1, channels, LANES))], name="conv_back",
-    )
-
-    dmain = jnp.concatenate([draw, dsteps[:heads].astype(bf16)], axis=0)
-    dmain_product = rows_product(dmain)
-    dmain_sum = over_planes(dmain_product)
-    dgate_rows = rows_to_owner(dgate_sum)
-    dmain_rows = rows_to_owner(after(dmain_sum, dgate_rows))
-    dmain = after(dmain, dmain_product)
-    grad_parts = []
-    for lanes in (slice(0, half), slice(half, width_in)):
-        part = mm(dmain, main_weight[lanes], CROSS) + gate_part[:, lanes].astype(f32)
-        grad_parts.append(to_owner(part.astype(bf16)))
-    grad_normed = restored(jnp.concatenate(grad_parts, axis=1)) * all_norm_gain
-    grad_tokens = inverse * (
-        grad_normed - normed * jnp.mean(grad_normed * normed, axis=-1, keepdims=True)
-    )
-    input_grad = (cotangent.astype(f32) + grad_tokens).astype(bf16)
-
-    dout = after(dout, dgate_sum).reshape(groups, planes, 2, out_rows, width_in)
+    until(grad_starts)
+
+    dout = now(seen["dout"]).reshape(groups, planes, 2, out_rows, width_in)
     dout_mine = by_core(dout[:, :, 0], dout[:, :, 1])
     dout_other = sibling(by_core(dout[:, :, 1], dout[:, :, 0]))
+    next_starts = over_heads(now(grad_starts), last_span)
+    until(next_starts, dout_other)
 
     def out_piece(i):
         at = (plane - i) % planes
@@ -783,9 +846,67 @@
             for a in (dout_mine, dout_other)
         )
 
+    def head_exchange(dtaps):
+        taps_sum = jnp.sum(dtaps, axis=2).reshape(-1)
+        head_sums = jnp.sum(jnp.concatenate([dsteps, row_sums[2 * heads :]], axis=0), axis=1)
+        packed = jnp.concatenate([taps_sum, head_sums])
+        padded = -(-packed.shape[0] // (8 * LANES)) * 8 * LANES
+        packed = jnp.pad(packed, (0, padded - packed.shape[0])).reshape(padded // LANES, LANES)
+        packed = jnp.broadcast_to(packed[None], (head_axis,) + packed.shape)
+        return lax.all_to_all(packed, "head", 0, 0, tiled=True)
+
+    def conv_back_step():
+        seen["draw"], seen["dtaps"] = call(
+            conv_back_kernel, rows, (raw, halo, now(grad_conv), next_starts, info, taps),
+            [tall, fixed_spec(halo.shape), tall, fixed_spec(grad_starts.shape), info_spec,
+             fixed_spec(taps.shape)],
+            [shape((channels, count), bf16), shape((TAPS + 1, channels, LANES), f32)],
+            [tall, fixed_spec((TAPS + 1, channels, LANES))], name="conv_back",
+        )
+        return (seen["draw"],)
+
+    def second_half_step():
+        got = to_owner(seen["part"])
+        seen["part"] = grad_part(1)
+        return got, seen["part"]
+
+    def last_step():
+        got = to_owner(now(seen["part"]))
+        seen["others"] = [across_rows(now(params), m) for m in range(1, rows)]
+        return [got] + seen["others"]
+
+    def grad_part(i):
+        lanes = slice(i * half, (i + 1) * half)
+        part = mm(now(seen["dmain"]), main_weight[lanes], CROSS)
+        return (part + seen["gate_part"][:, lanes].astype(f32)).astype(bf16)
+
+    grad_parts = []
     running = out_piece(planes - 1)
-    for i in reversed(range(planes - 1)):
-        running = over_heads(running.astype(bf16), ring_down).astype(f32) + out_piece(i)
+    for i, step in zip(
+        reversed(range(planes - 1)), (conv_back_step, second_half_step, last_step)
+    ):
+        passed = over_heads(now(running.astype(bf16)), ring_down)
+        found = step()
+        until(passed, *found)
+        running = passed.astype(f32) + out_piece(i)
+        if step is not conv_back_step:
+            grad_parts.append(found[0])
+            continue
+        dmain = jnp.concatenate([now(seen["draw"]), dsteps[:heads].astype(bf16)], axis=0)
+        product = rows_product(dmain)
+        dmain_sum = over_planes(tie(product, seen["dgate_sum"])[0])
+        params = head_exchange(now(seen["dtaps"]))
+        until(product, params)
+        seen["dmain"] = dmain
+        seen["part"] = grad_part(0)
+        sums = now(seen["dgate_sum"]).reshape(rows, span_rows, -1)
+        gate_rows = [
+            lax.dynamic_index_in_dim(sums, row ^ m, 0, keepdims=False) for m in range(rows)
+        ]
+        gate_rows[1:] = [across_rows(part, m) for m, part in enumerate(gate_rows) if m]
+        params = jnp.sum(now(params), axis=0)
+        until(seen["part"], *gate_rows)
+        seen["part"] = now(seen["part"])
     if groups > 1:
         running = lax.psum_scatter(
             running, "head", scatter_dimension=0, axis_index_groups=same_place, tiled=True
@@ -793,20 +914,26 @@
     out_weight_grad = running.reshape(out_rows, width_in)
     gate_gain_grad = jnp.sum(out_weight_grad * out_weight.astype(f32), axis=1) / gate_gain.astype(f32)
 
+    dmain_rows = lax.all_to_all(dmain_sum.reshape(rows, span_rows, -1), "row", 0, 0, tiled=True)
+    every = jnp.zeros((rows, params.size), f32)
+    for m, part in enumerate([params] + seen["others"]):
+        every = lax.dynamic_update_slice(every, part.reshape(1, -1), (row ^ m, 0))
+    total = every
+
+    normed_arranged, cot_arranged = seen["own"]
+    grad_normed = jnp.concatenate(grad_parts, axis=1) * gain_arranged
+    grad_tokens = inverse * (
+        grad_normed
+        - normed_arranged * jnp.mean(grad_normed * normed_arranged, axis=-1, keepdims=True)
+    )
+    input_grad = restored((cot_arranged.astype(f32) + grad_tokens).astype(bf16))
+
     tail = dmain_rows[..., channels:].transpose(1, 0, 2).reshape(span_rows, HEADS)
-    in_weight_grad, norm_sums = finish(dgate_rows, dmain_rows, tail, in_weight)
+    place = jnp.reshape(row, (1,)).astype(jnp.int32)
+    in_weight_grad, norm_sums = finish(place, gate_rows, dmain_rows, tail, in_weight)
     norm_gain_grad = jnp.sum(norm_sums, axis=1) / norm_gain.astype(f32)
 
-    head_sums = jnp.sum(jnp.concatenate([dsteps, row_sums[2 * heads :]], axis=0), axis=1)
-    taps_sum = jnp.sum(dtaps, axis=2)
-    packed = after(jnp.concatenate([taps_sum.reshape(-1), head_sums]), *grad_parts)
-    size = packed.shape[0]
-    padded = -(-size // (8 * LANES)) * 8 * LANES
-    packed = jnp.pad(packed, (0, padded - size)).reshape(padded // LANES, LANES)
-    packed = jnp.broadcast_to(packed[None], (head_axis,) + packed.shape)
-    packed = jnp.sum(lax.all_to_all(packed, "head", 0, 0, tiled=True), axis=0)
-    total = all_rows(packed).reshape(rows, padded)
-    taps_size = (TAPS + 1) * channels
+    taps_size, size = (TAPS + 1) * channels, (TAPS + 1) * channels + 3 * heads
     total_taps = total[:, :taps_size].reshape(rows, TAPS + 1, channels)
     all_taps_grad = jnp.concatenate(
         [

time: 587 us -> 544 us (0.927)
  starting transfers between devices: 110 us -> 86.3 us
  local copies, waits for them, and re-layouts: 91.4 us -> 81.6 us
  waiting for transfers between devices: 150 us -> 143 us
    all_to_all x3 -> x2, waiting for transfers between devices: 29.1 us -> 8.93 us  [to_owner(): lax.all_to_all(partial_sum.reshape(rows, SPAN, -1), 'row', 0, 0, tiled=True)]
    all_to_all x8 -> x3, starting transfers between devices: 33.4 us -> 14.8 us  [the longest x1 7.29 us: head_exchange(): return lax.all_to_all(packed, 'head', 0, 0, tiled=True)]
    ppermute x31 -> x38, waiting for transfers between devices: 63.7 us -> 79.9 us  [over_heads(): return lax.ppermute(a, 'head', pairs)]
    all_to_all x8 -> x3, waiting for transfers between devices: 35.4 us -> 22.7 us  [the longest x1 20 us: shards(): table = lax.all_to_all(table, ('row', 'head'), 0, 0, tiled=True)]
    ppermute x7 -> x17, waiting for transfers between devices: 3.82 us -> 15.7 us  [across_rows(): return lax.ppermute(a, 'row', [(i, i ^ mask) for i in range(rows)])]
    ppermute x7 -> x17, starting transfers between devices: 10 us -> 17.9 us  [across_rows(): return lax.ppermute(a, 'row', [(i, i ^ mask) for i in range(rows)])]
    dynamic_update_slice x16 -> x24, local copies, waits for them, and re-layouts: 29 us -> 21.2 us  [place_parts(): whole = lax.dynamic_update_slice(whole, one, (place * size, 0))]
    ppermute x31 -> x38, starting transfers between devices: 43.5 us -> 36.3 us  [over_heads(): return lax.ppermute(a, 'head', pairs)]
  transfers between devices with their start and end apart: 54 -> 65, of which waited for: 19 -> 26; matrix products, arithmetic and copies ran while one was open for 37% -> 38% of each run, Pallas kernels for 9% -> 9%
where the time goes in v2:
time: 544 us; the launch traced here: 534 us
  waiting for transfers between devices  143 us (26%)
  matrix products  89.4 us (16%)
  starting transfers between devices  86.3 us (16%)
  local copies, waits for them, and re-layouts  81.6 us (15%)
  Pallas kernels  67.3 us (12%)
  other arithmetic  49.1 us (9%)
  between operations  16.9 us (3%)
    dot_general x12, matrix products, mm(): return lax.dot_general(a, b, dims, preferred_element_type=f32).astype(out)  89.1 us
    ppermute x38, waiting for transfers between devices, over_heads(): return lax.ppermute(a, 'head', pairs)  79.9 us
    pallas_call x8, Pallas kernels, call(): pl.pallas_call(kernel if used else lambda place_ref, *refs: kernel(*refs)...  67.3 us
    ppermute x38, starting transfers between devices, over_heads(): return lax.ppermute(a, 'head', pairs)  36.3 us
    dynamic_update_slice x24, local copies, waits for them, and re-layouts, place_parts(): whole = lax.dynamic_update_slice(whole, one, (place * size, 0))  21.2 us
    all_to_all x1, waiting for transfers between devices, shards(): table = lax.all_to_all(table, ('row', 'head'), 0, 0, tiled=True)  20 us
    ppermute x17, starting transfers between devices, across_rows(): return lax.ppermute(a, 'row', [(i, i ^ mask) for i in range(rows)])  17.9 us
    ppermute x17, waiting for transfers between devices, across_rows(): return lax.ppermute(a, 'row', [(i, i ^ mask) for i in range(rows)])  15.7 us
  transfers between devices with their start and end apart: 65, of which 26 were waited for; matrix products, arithmetic and copies ran while one was open for 38% of the time, Pallas kernels for 9%

profile of v2, /device:TPU:0, one launch (start us, length us, event | category | flops | bytes accessed | tf_op | source)
XLA Modules:
  0.0 533.9 jit_solution(9375839208722720337)
XLA Ops:
  19.8 7.3 %all-to-all-done = bf16[4,64,1280]{2,1,0:T(8,128)(2,1)S(1)} async-done(((bf16[4,64,1280]{2,1,0:T(8,128)(2,1)}), bf16[4,64,1280]{2,1,0:T(8,128)(2,1)S(1)}, u32[]{:S(2)}, u32[]{:S(2)}) %all-to-all-start) | async-done | bytes 655392 | tf_op jit(solution)/shard_map/all_to_all | solution.py:519
  46.7 20.0 %all-to-all-done.2 = bf16[32,32,128]{2,1,0:T(8,128)(2,1)S(1)} async-done(((bf16[32,32,128]{2,1,0:T(8,128)(2,1)}), bf16[32,32,128]{2,1,0:T(8,128)(2,1)S(1)}, u32[]{:S(2)}, u32[]{:S(2)}) %all-to-all-start.2) | async-done | bytes 262176 | tf_op jit(solution)/shard_map/all_to_all | solution.py:582
  82.7 7.2 %collective-permute-done.3 = bf16[256,1280]{1,0:T(8,128)(2,1)} collective-permute-done((bf16[256,1280]{1,0:T(8,128)(2,1)}, bf16[256,1280]{1,0:T(8,128)(2,1)}, u32[]{:S(2)}, u32[]{:S(2)}) %collective-permute-start.3) | collective-permute-done | bytes 655392 | tf_op jit(solution)/shard_map/ppermute | solution.py:468
  106.3 11.2 %collective-permute-done.11 = bf16[128,2048]{0,1:T(8,128)(2,1)S(1)} collective-permute-done((bf16[128,2048]{0,1:T(8,128)(2,1)S(1)}, bf16[128,2048]{0,1:T(8,128)(2,1)S(1)}, u32[]{:S(2)}, u32[]{:S(2)}) %collective-permute-start.11) | collective-permute-done | bytes 524320 | tf_op jit(solution)/shard_map/ppermute | solution.py:465
  137.5 9.9 %fusion.4.refs_0_ = bf16[1280,1024]{1,0:T(8,128)(2,1)} fusion(bf16[1024,2048]{0,1:T(8,128)(2,1)} %constant_dynamic-update-slice_fusion.33, bf16[2048,1296]{1,0:T(8,128)(2,1)} %constant_dynamic-update-slice_fusion.38), kind=kOutput, calls=%fused_computation.9 | convolution fusion | flops 5370019840 | bytes 12058624 | tf_op jit(solution)/shard_map/dot_general | solution.py:27
  153.9 10.3 %conv.1 = (bf16[1280,1024]{1,0:T(8,128)(2,1)}, bf16[1280,1024]{1,0:T(8,128)(2,1)}, bf16[4,1024,128]{2,1,0:T(8,128)(2,1)}) custom-call(s32[1]{0:T(128)} %constant.205.clone.1.place_ref, bf16[1280,1024]{1,0:T(8,128)(2,1)} %fusion.4.refs_0_, bf16[1280,128]{1,0:T(8,128)(2,1)S(1)} %fusion.11.refs_1_, f32[4,8,512]{2,1,0:T(8,128)S(1)} %select_maximum_fusion.refs_2_.refs_1_.refs_4_, ...), custom_call_target="tpu_custom_call" | custom-call | tf_op jit(solution)/shard_map/conv/pallas_call | solution.py:360
  186.0 9.6 %collective-permute-done.21 = bf16[256,1024]{1,0:T(8,128)(2,1)S(1)} collective-permute-done((bf16[256,1024]{1,0:T(8,128)(2,1)}, bf16[256,1024]{1,0:T(8,128)(2,1)S(1)}, u32[]{:S(2)}, u32[]{:S(2)}) %collective-permute-start.21) | collective-permute-done | bytes 524320 | tf_op jit(solution)/shard_map/ppermute | solution.py:468
  205.7 9.8 %fusion.69.refs_5_.refs_4_ = f32[1024,1024]{1,0:T(8,128)} fusion(bf16[2048,1024]{1,0:T(8,128)(2,1)S(1)} %constant_dynamic-update-slice_fusion.21, bf16[1024,2048]{0,1:T(8,128)(2,1)} %constant_dynamic-update-slice_fusion.33), kind=kOutput, calls=%fused_computation.229 | convolution fusion | flops 4294967296 | bytes 12582912 | tf_op jit(solution)/shard_map/dot_general | solution.py:27
  226.1 5.8 %convolution_convert_fusion.5.refs_6_.refs_5_ = bf16[1024,1024]{1,0:T(8,128)(2,1)} fusion(bf16[1024,2048]{1,0:T(8,128)(2,1)S(1)} %constant_dynamic-update-slice_fusion.13, bf16[1024,2048]{1,0:T(8,128)(2,1)S(1)} %constant_dynamic-update-slice_fusion.8), kind=kOutput, calls=%fused_computation.36 | convolution fusion | flops 4296015872 | bytes 10485760 | tf_op jit(solution)/shard_map/dot_general | solution.py:27
  236.1 6.8 %mix.1 = (bf16[1024,1024]{1,0:T(8,128)(2,1)S(1)}, f32[8,1024]{1,0:T(8,128)S(1)}) custom-call(s32[1]{0:T(128)} %constant.205.clone.1.place_ref, bf16[1280,1024]{1,0:T(8,128)(2,1)} %get-tuple-element.115.refs_0_, f32[4,8,512]{2,1,0:T(8,128)S(1)} %select_maximum_fusion.refs_2_.refs_1_.refs_4_, f32[16,1024]{1,0:T(8,128)S(1)} %reshape.687.refs_4_.refs_2_.refs_3_, ...), custom_call_target="tpu_custom_call" | custom-call | tf_op jit(solution)/shard_map/mix/pallas_call | solution.py:360
  250.9 8.3 %gate.1 = (bf16[1024,1024]{1,0:T(8,128)(2,1)S(1)}, bf16[1024,1024]{1,0:T(8,128)(2,1)}, bf16[1024,1024]{1,0:T(8,128)(2,1)}, bf16[4,1024,128]{2,1,0:T(8,128)(2,1)S(1)}) custom-call(s32[1]{0:T(128)} %constant.205.clone.1.place_ref, bf16[1280,1024]{1,0:T(8,128)(2,1)} %get-tuple-element.115.refs_0_, f32[4,8,512]{2,1,0:T(8,128)S(1)} %select_maximum_fusion.refs_2_.refs_1_.refs_4_, ...), custom_call_target="tpu_custom_call" | custom-call | tf_op jit(solution)/shard_map/gate/pallas_call | solution.py:360
  264.4 6.3 %convolution_convert_fusion.4 = bf16[1024,2048]{1,0:T(8,128)(2,1)} fusion(bf16[1024,1024]{1,0:T(8,128)(2,1)S(1)} %get-tuple-element.159, bf16[1024,2048]{1,0:T(8,128)(2,1)S(1)} %copy-done.32), kind=kOutput, calls=%fused_computation.13 | convolution fusion | flops 4297064448 | bytes 10485760 | tf_op jit(solution)/shard_map/dot_general | solution.py:27
  270.7 9.4 %convolution_convert_fusion.3 = bf16[2048,1024]{1,0:T(8,128)(2,1)} fusion(bf16[1024,2048]{0,1:T(8,128)(2,1)} %constant_dynamic-update-slice_fusion.33, bf16[1024,1024]{1,0:T(8,128)(2,1)} %get-tuple-element.160), kind=kOutput, calls=%fused_computation.12 | convolution fusion | flops 4297064448 | bytes 10485760 | tf_op jit(solution)/shard_map/dot_general | solution.py:27
  281.4 12.2 %within_back.1 = (f32[1024,1024]{1,0:T(8,128)}, f32[256,1024]{1,0:T(8,128)S(1)}, f32[48,1024]{1,0:T(8,128)S(1)}) custom-call(s32[1]{0:T(128)} %constant.205.clone.1.place_ref, bf16[1280,1024]{1,0:T(8,128)(2,1)} %get-tuple-element.115.refs_0_, f32[4,8,512]{2,1,0:T(8,128)S(1)} %select_maximum_fusion.refs_2_.refs_1_.refs_4_, ...), custom_call_target="tpu_custom_call" | custom-call | tf_op jit(solution)/shard_map/within_back/pallas_call | solution.py:360
  298.7 9.4 %convolution_convert_fusion.1 = bf16[1024,2048]{1,0:T(8,128)(2,1)} fusion(bf16[1024,1024]{1,0:T(8,128)(2,1)} %get-tuple-element.160, bf16[2048,1024]{1,0:T(8,128)(2,1)} %copy-done.30), kind=kOutput, calls=%fused_computation.10 | convolution fusion | flops 4297064448 | bytes 10485760 | tf_op jit(solution)/shard_map/dot_general | solution.py:27
  312.9 25.1 %collective-permute-done.42 = bf16[4,8,64,128]{3,2,1,0:T(8,128)(2,1)S(1)} collective-permute-done((bf16[4,8,64,128]{3,2,1,0:T(8,128)(2,1)}, bf16[4,8,64,128]{3,2,1,0:T(8,128)(2,1)S(1)}, u32[]{:S(2)}, u32[]{:S(2)}) %collective-permute-start.42) | collective-permute-done | bytes 524320 | tf_op jit(solution)/shard_map/ppermute | solution.py:468
  340.8 8.6 %state_back.1 = (bf16[1280,1024]{1,0:T(8,128)(2,1)}, f32[32,1024]{1,0:T(8,128)S(1)}, bf16[1280,128]{1,0:T(8,128)(2,1)}) custom-call(s32[1]{0:T(128)} %constant.205.clone.1.place_ref, bf16[1280,1024]{1,0:T(8,128)(2,1)} %get-tuple-element.115.refs_0_, bf16[1280,1024]{1,0:T(8,128)(2,1)} %get-tuple-element.156.refs_1_, ...), custom_call_target="tpu_custom_call" | custom-call | tf_op jit(solution)/shard_map/state_back/pallas_call | solution.py:360
  360.6 13.8 %conv_back.1 = (bf16[1280,1024]{1,0:T(8,128)(2,1)S(1)}, f32[5,1280,128]{2,1,0:T(8,128)}) custom-call(s32[1]{0:T(128)} %constant.205.clone.1.place_ref, bf16[1280,1024]{1,0:T(8,128)(2,1)} %fusion.4.refs_0_, bf16[1280,128]{1,0:T(8,128)(2,1)S(1)} %copy-done.6, bf16[1280,1024]{1,0:T(8,128)(2,1)} %get-tuple-element.166.refs_2_, bf16[1280,128]{1,0:T(8,128)(2,1)S(1)} %copy-done.9, ...), custom_call_target="tpu_custom_call" | custom-call | tf_op jit(solution)/shard_map/conv_back/pallas_call | solution.py:360
  379.8 10.0 %convolution_convert_fusion = bf16[2048,1296]{0,1:T(8,128)(2,1)} fusion(bf16[1024,2048]{0,1:T(8,128)(2,1)} %constant_dynamic-update-slice_fusion.33, bf16[16,1024]{1,0:T(8,128)(2,1)S(1)} %slice.333, bf16[1280,1024]{1,0:T(8,128)(2,1)S(1)} %get-tuple-element.169), kind=kOutput, calls=%fused_computation | convolution fusion | flops 5443780608 | bytes 12156928 | tf_op jit(solution)/shard_map/dot_general | solution.py:27
  394.5 7.3 %all-to-all-start.3 = ((f32[8,56,128]{2,1,0:T(8,128)}), f32[8,56,128]{2,1,0:T(8,128)S(1)}, u32[]{:S(2)}, u32[]{:S(2)}) async-start(f32[8,56,128]{2,1,0:T(8,128)} %broadcast_in_dim.111), calls=%async_computation.4 | async-start | bytes 458752 | tf_op jit(solution)/shard_map/all_to_all | solution.py:856
  414.4 8.0 %add_convert_fusion.1 = bf16[1024,1024]{1,0:T(8,128)(2,1)} fusion(bf16[1024,2048]{1,0:T(8,128)(2,1)} %convolution_convert_fusion.1, bf16[1296,1024]{1,0:T(8,128)(2,1)} %pad_maximum_fusion, bf16[2048,1296]{1,0:T(8,128)(2,1)} %constant_dynamic-update-slice_fusion.38), kind=kOutput, calls=%fused_computation.8 | convolution fusion | flops 2721054720 | bytes 9732096 | tf_op jit(solution)/shard_map/dot_general | solution.py:27
  436.4 8.1 %add_convert_fusion = bf16[1024,1024]{1,0:T(8,128)(2,1)} fusion(bf16[1024,2048]{1,0:T(8,128)(2,1)} %convolution_convert_fusion.1, bf16[1296,1024]{1,0:T(8,128)(2,1)} %pad_maximum_fusion, bf16[2048,1296]{1,0:T(8,128)(2,1)} %constant_dynamic-update-slice_fusion.38), kind=kOutput, calls=%fused_computation.6 | convolution fusion | flops 2721054720 | bytes 9732096 | tf_op jit(solution)/shard_map/dot_general | solution.py:27
  444.5 8.9 %all-to-all-done.4 = bf16[4,256,1024]{2,1,0:T(8,128)(2,1)} async-done(((bf16[4,256,1024]{2,1,0:T(8,128)(2,1)}), bf16[4,256,1024]{2,1,0:T(8,128)(2,1)}, u32[]{:S(2)}, u32[]{:S(2)}) %all-to-all-start.4) | async-done | bytes 2097184 | tf_op jit(solution)/shard_map/all_to_all | solution.py:778
  479.3 18.5 %collective-permute-done.51 = bf16[1,128,2048]{2,1,0:T(8,128)(2,1)S(1)} collective-permute-done((bf16[1,128,2048]{2,1,0:T(8,128)(2,1)}, bf16[1,128,2048]{2,1,0:T(8,128)(2,1)S(1)}, u32[]{:S(2)}, u32[]{:S(2)}) %collective-permute-start.51) | collective-permute-done | bytes 524320 | tf_op jit(solution)/shard_map/ppermute | solution.py:468
  (475 shorter events, 265.1 us)
Async XLA Ops:
  7.2 27.6 %collective-permute-start = (bf16[128,2048]{1,0:T(8,128)(2,1)}, bf16[128,2048]{1,0:T(8,128)(2,1)}, u32[]{:S(2)}, u32[]{:S(2)}) collective-permute-start(bf16[128,2048]{1,0:T(8,128)(2,1)} %param.16), channel_id=1, source_target_pairs={{0,2},{1,3},{2,4},{3,5},{4,6},{5,7},{6,0},{7,1},{8,10},{9,11},{10,... | collective-permute-start | bytes 1572872 | tf_op jit(solution)/shard_map/ppermute | solution.py:468
  39.8 26.9 %all-to-all-start.2 = ((bf16[32,32,128]{2,1,0:T(8,128)(2,1)}), bf16[32,32,128]{2,1,0:T(8,128)(2,1)S(1)}, u32[]{:S(2)}, u32[]{:S(2)}) async-start(bf16[32,32,128]{2,1,0:T(8,128)(2,1)} %bitcast.17), calls=%async_computation.2 | async-start | bytes 524288 | tf_op jit(solution)/shard_map/all_to_all | solution.py:582
  43.7 346.1 %reduce-scatter.6.cloned.1.call-start = ((), (), s32[]{:S(2)}) async-start(), calls=%async_computation.11 | async-start | bytes 4718592 | tf_op jit(solution)/shard_map/reduce_scatter | solution.py:785
  44.7 23.6 %collective-permute-start.2 = (bf16[256,1280]{1,0:T(8,128)(2,1)S(1)}, bf16[256,1280]{1,0:T(8,128)(2,1)}, u32[]{:S(2)}, u32[]{:S(2)}) collective-permute-start(bf16[256,1280]{1,0:T(8,128)(2,1)S(1)} %bitcast.193), channel_id=1, source_target_pairs={{0,1},{1,0},{2,3},{3,2},{4,5},{5,4},{6,7},{7,6},{8,9},{9,8},{10,11... | collective-permute-start | bytes 1966088 | tf_op jit(solution)/shard_map/ppermute | solution.py:468
  45.0 23.3 %collective-permute-start.1 = (bf16[256,1280]{1,0:T(8,128)(2,1)S(1)}, bf16[256,1280]{1,0:T(8,128)(2,1)}, u32[]{:S(2)}, u32[]{:S(2)}) collective-permute-start(bf16[256,1280]{1,0:T(8,128)(2,1)S(1)} %bitcast.194), channel_id=1, source_target_pairs={{0,2},{1,3},{2,4},{3,5},{4,6},{5,7},{6,0},{7,1},{8,10},{9,11},{10,... | collective-permute-start | bytes 1966088 | tf_op jit(solution)/shard_map/ppermute | solution.py:468
  68.3 28.5 %collective-permute-start.4 = (bf16[256,1280]{1,0:T(8,128)(2,1)}, bf16[256,1280]{1,0:T(8,128)(2,1)}, u32[]{:S(2)}, u32[]{:S(2)}) collective-permute-start(bf16[256,1280]{1,0:T(8,128)(2,1)} %collective-permute-done.1), channel_id=1, source_target_pairs={{0,1},{1,0},{2,3},{3,2},{4,5},{5,4},{6,7},{7,6},{8,9},{9,8},{10,11... | collective-permute-start | bytes 1966088 | tf_op jit(solution)/shard_map/ppermute | solution.py:468
  73.6 27.2 %collective-permute-start.6 = (bf16[256,2048]{0,1:T(8,128)(2,1)}, bf16[256,2048]{0,1:T(8,128)(2,1)S(1)}, u32[]{:S(2)}, u32[]{:S(2)}) collective-permute-start(bf16[256,2048]{0,1:T(8,128)(2,1)} %bitcast.22), channel_id=1, source_target_pairs={{0,16},{8,24},{16,0},{24,8},{1,17},{9,25},{17,1},{25,9},{2,18},{10... | collective-permute-start | bytes 3145736 | tf_op jit(solution)/shard_map/ppermute | solution.py:465
  74.6 26.2 %collective-permute-start.5 = (bf16[256,2048]{0,1:T(8,128)(2,1)}, bf16[256,2048]{0,1:T(8,128)(2,1)S(1)}, u32[]{:S(2)}, u32[]{:S(2)}) collective-permute-start(bf16[256,2048]{0,1:T(8,128)(2,1)} %bitcast.22), channel_id=1, source_target_pairs={{0,8},{8,0},{16,24},{24,16},{1,9},{9,1},{17,25},{25,17},{2,10},{10... | collective-permute-start | bytes 3145736 | tf_op jit(solution)/shard_map/ppermute | solution.py:465
  75.4 25.4 %collective-permute-start.7 = (bf16[128,2048]{1,0:T(8,128)(2,1)}, bf16[128,2048]{1,0:T(8,128)(2,1)}, u32[]{:S(2)}, u32[]{:S(2)}) collective-permute-start(bf16[128,2048]{1,0:T(8,128)(2,1)} %collective-permute-done), channel_id=1, source_target_pairs={{0,2},{1,3},{2,4},{3,5},{4,6},{5,7},{6,0},{7,1},{8,10},{9,11},{10,... | collective-permute-start | bytes 1572872 | tf_op jit(solution)/shard_map/ppermute | solution.py:468
  100.8 21.5 %collective-permute-start.9 = (bf16[256,1280]{1,0:T(8,128)(2,1)}, bf16[256,1280]{1,0:T(8,128)(2,1)}, u32[]{:S(2)}, u32[]{:S(2)}) collective-permute-start(bf16[256,1280]{1,0:T(8,128)(2,1)} %collective-permute-done.3), channel_id=1, source_target_pairs={{0,2},{1,3},{2,4},{3,5},{4,6},{5,7},{6,0},{7,1},{8,10},{9,11},{10,... | collective-permute-start | bytes 1966088 | tf_op jit(solution)/shard_map/ppermute | solution.py:468
  100.8 21.4 %collective-permute-start.8 = (bf16[256,1280]{1,0:T(8,128)(2,1)}, bf16[256,1280]{1,0:T(8,128)(2,1)}, u32[]{:S(2)}, u32[]{:S(2)}) collective-permute-start(bf16[256,1280]{1,0:T(8,128)(2,1)} %collective-permute-done.3), channel_id=1, source_target_pairs={{0,1},{1,0},{2,3},{3,2},{4,5},{5,4},{6,7},{7,6},{8,9},{9,8},{10,11... | collective-permute-start | bytes 1966088 | tf_op jit(solution)/shard_map/ppermute | solution.py:468
  118.0 29.3 %collective-permute-start.13 = (bf16[16,2048]{1,0:T(8,128)(2,1)S(1)}, bf16[16,2048]{1,0:T(8,128)(2,1)S(1)}, u32[]{:S(2)}, u32[]{:S(2)}) collective-permute-start(bf16[16,2048]{1,0:T(8,128)(2,1)S(1)} %reshape.685), channel_id=1, source_target_pairs={{0,1},{1,2},{2,3},{3,4},{4,5},{5,6},{6,7},{8,9},{9,10},{10,11},{11... | collective-permute-start | bytes 196616 | tf_op jit(solution)/shard_map/ppermute | solution.py:468
  126.0 39.0 %collective-permute-start.17 = (bf16[256,2048]{1,0:T(8,128)(2,1)}, bf16[256,2048]{1,0:T(8,128)(2,1)}, u32[]{:S(2)}, u32[]{:S(2)}) collective-permute-start(bf16[256,2048]{1,0:T(8,128)(2,1)} %param.25), channel_id=1, source_target_pairs={{0,16},{8,24},{16,0},{24,8},{1,17},{9,25},{17,1},{25,9},{2,18},{10... | collective-permute-start | bytes 3145736 | tf_op jit(solution)/shard_map/ppermute | solution.py:465
  127.3 37.7 %collective-permute-start.16 = (bf16[256,2048]{1,0:T(8,128)(2,1)}, bf16[256,2048]{1,0:T(8,128)(2,1)}, u32[]{:S(2)}, u32[]{:S(2)}) collective-permute-start(bf16[256,2048]{1,0:T(8,128)(2,1)} %param.25), channel_id=1, source_target_pairs={{0,8},{8,0},{16,24},{24,16},{1,9},{9,1},{17,25},{25,17},{2,10},{10... | collective-permute-start | bytes 3145736 | tf_op jit(solution)/shard_map/ppermute | solution.py:465
  174.8 20.8 %collective-permute-start.21 = (bf16[256,1024]{1,0:T(8,128)(2,1)}, bf16[256,1024]{1,0:T(8,128)(2,1)S(1)}, u32[]{:S(2)}, u32[]{:S(2)}) collective-permute-start(bf16[256,1024]{1,0:T(8,128)(2,1)} %collective-permute-done.15), channel_id=1, source_target_pairs={{0,2},{1,3},{2,4},{3,5},{4,6},{5,7},{6,0},{7,1},{8,10},{9,11},{10,... | collective-permute-start | bytes 1572872 | tf_op jit(solution)/shard_map/ppermute | solution.py:468
  174.8 20.7 %collective-permute-start.22 = (bf16[128,2048]{1,0:T(8,128)(2,1)S(1)}, bf16[128,2048]{1,0:T(8,128)(2,1)S(1)}, u32[]{:S(2)}, u32[]{:S(2)}) collective-permute-start(bf16[128,2048]{1,0:T(8,128)(2,1)S(1)} %slice.247), channel_id=1, source_target_pairs={{0,16},{8,24},{16,0},{24,8},{1,17},{9,25},{17,1},{25,9},{2,18},{10... | collective-permute-start | bytes 1572872 | tf_op jit(solution)/shard_map/ppermute | solution.py:465
  296.1 134.1 %reduce-scatter.4.cloned.1.call-start = ((), (), s32[]{:S(2)}) async-start(), calls=%async_computation.10 | async-start | bytes 5242880 | tf_op jit(solution)/shard_map/reduce_scatter | solution.py:790
  296.9 214.0 %reduce-scatter.8.cloned.1.call-start = ((), (), s32[]{:S(2)}) async-start(), calls=%async_computation.12 | async-start | bytes 5971968 | tf_op jit(solution)/shard_map/reduce_scatter | solution.py:785
  297.0 41.0 %collective-permute-start.42 = (bf16[4,8,64,128]{3,2,1,0:T(8,128)(2,1)}, bf16[4,8,64,128]{3,2,1,0:T(8,128)(2,1)S(1)}, u32[]{:S(2)}, u32[]{:S(2)}) collective-permute-start(bf16[4,8,64,128]{3,2,1,0:T(8,128)(2,1)} %add_convert_fusion.5), channel_id=1, source_target_pairs={{2,0},{3,1},{10,8},{11,9},{18,16},{19,17},{26,24},{27,25}} | collective-permute-start | bytes 1572872 | tf_op jit(solution)/shard_map/ppermute | solution.py:468
  358.4 20.6 %collective-permute-start.46 = (bf16[1,128,2048]{2,1,0:T(8,128)(2,1)S(1)}, bf16[1,128,2048]{2,1,0:T(8,128)(2,1)S(1)}, u32[]{:S(2)}, u32[]{:S(2)}) collective-permute-start(bf16[1,128,2048]{2,1,0:T(8,128)(2,1)S(1)} %fusion.40), channel_id=1, source_target_pairs={{2,0},{3,1},{4,2},{5,3},{6,4},{7,5},{0,6},{1,7},{10,8},{11,9},{12,... | collective-permute-start | bytes 1572872 | tf_op jit(solution)/shard_map/ppermute | solution.py:468
  423.8 29.6 %all-to-all-start.4 = ((bf16[4,256,1024]{2,1,0:T(8,128)(2,1)}), bf16[4,256,1024]{2,1,0:T(8,128)(2,1)}, u32[]{:S(2)}, u32[]{:S(2)}) async-start(bf16[4,256,1024]{2,1,0:T(8,128)(2,1)} %bitcast.198), calls=%async_computation.6 | async-start | bytes 4194304 | tf_op jit(solution)/shard_map/all_to_all | solution.py:778
  432.8 26.7 %collective-permute-start.50 = (bf16[1,128,2048]{2,1,0:T(8,128)(2,1)S(1)}, bf16[1,128,2048]{2,1,0:T(8,128)(2,1)S(1)}, u32[]{:S(2)}, u32[]{:S(2)}) collective-permute-start(bf16[1,128,2048]{2,1,0:T(8,128)(2,1)S(1)} %fusion.38), channel_id=1, source_target_pairs={{2,0},{3,1},{4,2},{5,3},{6,4},{7,5},{0,6},{1,7},{10,8},{11,9},{12,... | collective-permute-start | bytes 1572872 | tf_op jit(solution)/shard_map/ppermute | solution.py:468
  463.1 37.7 %all-to-all-start.5 = ((bf16[4,256,1024]{2,1,0:T(8,128)(2,1)}), bf16[4,256,1024]{2,1,0:T(8,128)(2,1)}, u32[]{:S(2)}, u32[]{:S(2)}) async-start(bf16[4,256,1024]{2,1,0:T(8,128)(2,1)} %bitcast.197), calls=%async_computation.7 | async-start | bytes 4194304 | tf_op jit(solution)/shard_map/all_to_all | solution.py:778
  470.3 27.5 %collective-permute-start.51 = (bf16[1,128,2048]{2,1,0:T(8,128)(2,1)}, bf16[1,128,2048]{2,1,0:T(8,128)(2,1)S(1)}, u32[]{:S(2)}, u32[]{:S(2)}) collective-permute-start(bf16[1,128,2048]{2,1,0:T(8,128)(2,1)} %fusion.35), channel_id=1, source_target_pairs={{2,0},{3,1},{4,2},{5,3},{6,4},{7,5},{0,6},{1,7},{10,8},{11,9},{12,... | collective-permute-start | bytes 1572872 | tf_op jit(solution)/shard_map/ppermute | solution.py:468
  (112 other events, 1532.9 us)
Sparse Core Ops, SparseCore 0:
  296.3 69.2 reduce-scatter.5
  368.5 56.6 reduce-scatter.3
  427.6 83.1 reduce-scatter.7

commit v3 on v2

--- a/solution.py
+++ b/solution.py
@@ -804,11 +804,8 @@
         return seen["back"][:1]
 
     def out_step():
-        seen["dgate_sum"] = over_planes(now(seen["dgate"]))
         seen["dout"] = mm(now(gated_hat), plane_cot, NN, bf16)
-        seen["gate_part"] = mm(now(dgate), gate_weight, CROSS, bf16)
-        seen["own"] = arranged(now(normed)), arranged(now(cotangent))
-        return (seen["dout"], seen["gate_part"]) + seen["own"]
+        return seen["dout"], seen["out"]
 
     local_dstate = local_dstate.reshape(by_head)
     other_dstate = sibling(local_dstate)
@@ -818,6 +815,7 @@
         [dgate_step, within_back_step, out_step], 1, other_dstate,
     )
     dx, dmatrix, row_sums = seen["back"]
+    seen["dgate_sum"] = over_planes(now(seen["dgate"]))
     output = (activations + seen["out"].astype(f32)).astype(bf16)
 
     grad_conv, dsteps, grad_starts = call(
@@ -837,7 +835,8 @@
     dout_mine = by_core(dout[:, :, 0], dout[:, :, 1])
     dout_other = sibling(by_core(dout[:, :, 1], dout[:, :, 0]))
     next_starts = over_heads(now(grad_starts), last_span)
-    until(next_starts, dout_other)
+    seen["gate_part"] = mm(now(dgate), gate_weight, CROSS, bf16)
+    until(next_starts, seen["gate_part"])
 
     def out_piece(i):
         at = (plane - i) % planes
@@ -865,48 +864,39 @@
         )
         return (seen["draw"],)
 
-    def second_half_step():
-        got = to_owner(seen["part"])
-        seen["part"] = grad_part(1)
-        return got, seen["part"]
-
-    def last_step():
-        got = to_owner(now(seen["part"]))
-        seen["others"] = [across_rows(now(params), m) for m in range(1, rows)]
-        return [got] + seen["others"]
-
     def grad_part(i):
         lanes = slice(i * half, (i + 1) * half)
         part = mm(now(seen["dmain"]), main_weight[lanes], CROSS)
         return (part + seen["gate_part"][:, lanes].astype(f32)).astype(bf16)
 
-    grad_parts = []
+    grad_parts, gate_rows = [], []
+    def next_sum(i, *since):
+        passed = over_heads(tie(running.astype(bf16), *since)[0], ring_down)
+        return passed, passed.astype(f32) + out_piece(i)
+
     running = out_piece(planes - 1)
-    for i, step in zip(
-        reversed(range(planes - 1)), (conv_back_step, second_half_step, last_step)
-    ):
-        passed = over_heads(now(running.astype(bf16)), ring_down)
-        found = step()
-        until(passed, *found)
-        running = passed.astype(f32) + out_piece(i)
-        if step is not conv_back_step:
-            grad_parts.append(found[0])
-            continue
-        dmain = jnp.concatenate([now(seen["draw"]), dsteps[:heads].astype(bf16)], axis=0)
-        product = rows_product(dmain)
-        dmain_sum = over_planes(tie(product, seen["dgate_sum"])[0])
-        params = head_exchange(now(seen["dtaps"]))
-        until(product, params)
-        seen["dmain"] = dmain
-        seen["part"] = grad_part(0)
-        sums = now(seen["dgate_sum"]).reshape(rows, span_rows, -1)
-        gate_rows = [
-            lax.dynamic_index_in_dim(sums, row ^ m, 0, keepdims=False) for m in range(rows)
-        ]
-        gate_rows[1:] = [across_rows(part, m) for m, part in enumerate(gate_rows) if m]
-        params = jnp.sum(now(params), axis=0)
-        until(seen["part"], *gate_rows)
-        seen["part"] = now(seen["part"])
+    passed, running = next_sum(planes - 2, next_starts)
+    until(*conv_back_step())
+    seen["dmain"] = jnp.concatenate([now(seen["draw"]), dsteps[:heads].astype(bf16)], axis=0)
+    product = rows_product(seen["dmain"])
+    dmain_sum = over_planes(tie(product, seen["dgate_sum"])[0])
+    until(product)
+    first_part = grad_part(0)
+    grad_parts.append(to_owner(first_part))
+    sums = tie(seen["dgate_sum"], product)[0].reshape(rows, span_rows, -1)
+    for m in range(rows):
+        part = lax.dynamic_index_in_dim(sums, row ^ m, 0, keepdims=False)
+        gate_rows.append(across_rows(part, m) if m else part)
+    second_part = grad_part(1)
+    for i in reversed(range(planes - 2)):
+        passed, running = next_sum(i, second_part if i else grad_parts[0])
+    params = jnp.sum(head_exchange(tie(seen["dtaps"], grad_parts[0], second_part)[0]), axis=0)
+    grad_parts.append(to_owner(tie(second_part, params)[0]))
+    seen["others"] = [across_rows(params, m) for m in range(1, rows)]
+    dmain_rows = tie(dmain_sum, grad_parts[1], *gate_rows, *seen["others"])[0]
+    dmain_rows = lax.all_to_all(
+        dmain_rows.reshape(rows, span_rows, -1), "row", 0, 0, tiled=True
+    )
     if groups > 1:
         running = lax.psum_scatter(
             running, "head", scatter_dimension=0, axis_index_groups=same_place, tiled=True
@@ -914,13 +904,12 @@
     out_weight_grad = running.reshape(out_rows, width_in)
     gate_gain_grad = jnp.sum(out_weight_grad * out_weight.astype(f32), axis=1) / gate_gain.astype(f32)
 
-    dmain_rows = lax.all_to_all(dmain_sum.reshape(rows, span_rows, -1), "row", 0, 0, tiled=True)
     every = jnp.zeros((rows, params.size), f32)
     for m, part in enumerate([params] + seen["others"]):
         every = lax.dynamic_update_slice(every, part.reshape(1, -1), (row ^ m, 0))
     total = every
 
-    normed_arranged, cot_arranged = seen["own"]
+    normed_arranged, cot_arranged = arranged(normed), arranged(cotangent)
     grad_normed = jnp.concatenate(grad_parts, axis=1) * gain_arranged
     grad_tokens = inverse * (
         grad_normed

time: 544 us -> 542 us (level)
  starting transfers between devices: 86.3 us -> 77.9 us
    ppermute x38, waiting for transfers between devices: 79.9 us -> 61 us  [over_heads(): return lax.ppermute(a, 'head', pairs)]
    ppermute x38, starting transfers between devices: 36.3 us -> 28.4 us  [over_heads(): return lax.ppermute(a, 'head', pairs)]
    all_to_all x1, waiting for transfers between devices: 1.11 us -> 7.95 us  [head_exchange(): return lax.all_to_all(packed, 'head', 0, 0, tiled=True)]
    all_to_all x2, waiting for transfers between devices: 8.93 us -> 15.6 us  [to_owner(): lax.all_to_all(partial_sum.reshape(rows, SPAN, -1), 'row', 0, 0, tiled=True)]
    reduce_scatter x2, waiting for transfers between devices: 3.05 us -> 9.3 us  [over_planes(): return lax.psum_scatter(product, 'head', scatter_dimension=0, tiled=True)]
    unnamed x152 -> x153, local copies, waits for them, and re-layouts: 9.48 us -> 11.1 us
  transfers between devices with their start and end apart: 65 -> 65, of which waited for: 26 -> 27; matrix products, arithmetic and copies ran while one was open for 38% -> 37% of each run, Pallas kernels for 9% -> 10%
where the time goes in v3:
time: 542 us; the launch traced here: 532 us
  waiting for transfers between devices  145 us (27%)
  matrix products  85.9 us (16%)
  local copies, waits for them, and re-layouts  85.6 us (16%)
  starting transfers between devices  77.9 us (14%)
  Pallas kernels  68.3 us (13%)
  other arithmetic  52 us (10%)
  between operations  16.9 us (3%)
    dot_general x12, matrix products, mm(): return lax.dot_general(a, b, dims, preferred_element_type=f32).astype(out)  85.6 us
    pallas_call x8, Pallas kernels, call(): pl.pallas_call(kernel if used else lambda place_ref, *refs: kernel(*refs)...  68.3 us
    ppermute x38, waiting for transfers between devices, over_heads(): return lax.ppermute(a, 'head', pairs)  61 us
    ppermute x38, starting transfers between devices, over_heads(): return lax.ppermute(a, 'head', pairs)  28.4 us
    dynamic_update_slice x24, local copies, waits for them, and re-layouts, place_parts(): whole = lax.dynamic_update_slice(whole, one, (place * size, 0))  21.2 us
    all_to_all x1, waiting for transfers between devices, shards(): table = lax.all_to_all(table, ('row', 'head'), 0, 0, tiled=True)  20.2 us
    ppermute x17, starting transfers between devices, across_rows(): return lax.ppermute(a, 'row', [(i, i ^ mask) for i in range(rows)])  18.9 us
    all_to_all x2, waiting for transfers between devices, to_owner(): lax.all_to_all(partial_sum.reshape(rows, SPAN, -1), 'row', 0, 0, tiled=True)  15.6 us
  transfers between devices with their start and end apart: 65, of which 27 were waited for; matrix products, arithmetic and copies ran while one was open for 37% of the time, Pallas kernels for 10%

profile of v3, /device:TPU:0, one launch (start us, length us, event | category | flops | bytes accessed | tf_op | source)
XLA Modules:
  0.0 531.5 jit_solution(10188727064414595544)
XLA Ops:
  46.5 20.2 %all-to-all-done.2 = bf16[32,32,128]{2,1,0:T(8,128)(2,1)S(1)} async-done(((bf16[32,32,128]{2,1,0:T(8,128)(2,1)}), bf16[32,32,128]{2,1,0:T(8,128)(2,1)S(1)}, u32[]{:S(2)}, u32[]{:S(2)}) %all-to-all-start.2) | async-done | bytes 262176 | tf_op jit(solution)/shard_map/all_to_all | solution.py:582
  82.6 10.0 %collective-permute-done.3 = bf16[256,1280]{1,0:T(8,128)(2,1)} collective-permute-done((bf16[256,1280]{1,0:T(8,128)(2,1)}, bf16[256,1280]{1,0:T(8,128)(2,1)}, u32[]{:S(2)}, u32[]{:S(2)}) %collective-permute-start.3) | collective-permute-done | bytes 655392 | tf_op jit(solution)/shard_map/ppermute | solution.py:468
  114.0 7.2 %collective-permute-done.11 = bf16[128,2048]{0,1:T(8,128)(2,1)S(1)} collective-permute-done((bf16[128,2048]{0,1:T(8,128)(2,1)}, bf16[128,2048]{0,1:T(8,128)(2,1)S(1)}, u32[]{:S(2)}, u32[]{:S(2)}) %collective-permute-start.11) | collective-permute-done | bytes 524320 | tf_op jit(solution)/shard_map/ppermute | solution.py:465
  138.6 9.9 %fusion.4.refs_0_ = bf16[1280,1024]{1,0:T(8,128)(2,1)} fusion(bf16[1024,2048]{0,1:T(8,128)(2,1)} %constant_dynamic-update-slice_fusion.33, bf16[2048,1296]{1,0:T(8,128)(2,1)} %constant_dynamic-update-slice_fusion.38), kind=kOutput, calls=%fused_computation.9 | convolution fusion | flops 5370019840 | bytes 12058624 | tf_op jit(solution)/shard_map/dot_general | solution.py:27
  157.2 10.3 %conv.1 = (bf16[1280,1024]{1,0:T(8,128)(2,1)}, bf16[1280,1024]{1,0:T(8,128)(2,1)}, bf16[4,1024,128]{2,1,0:T(8,128)(2,1)}) custom-call(s32[1]{0:T(128)} %constant.205.clone.1.place_ref, bf16[1280,1024]{1,0:T(8,128)(2,1)} %fusion.4.refs_0_, bf16[1280,128]{1,0:T(8,128)(2,1)S(1)} %fusion.11.refs_1_, f32[4,8,512]{2,1,0:T(8,128)S(1)} %select_maximum_fusion.refs_2_.refs_1_.refs_4_, ...), custom_call_target="tpu_custom_call" | custom-call | tf_op jit(solution)/shard_map/conv/pallas_call | solution.py:360
  189.3 9.6 %collective-permute-done.21 = bf16[256,1024]{1,0:T(8,128)(2,1)S(1)} collective-permute-done((bf16[256,1024]{1,0:T(8,128)(2,1)}, bf16[256,1024]{1,0:T(8,128)(2,1)S(1)}, u32[]{:S(2)}, u32[]{:S(2)}) %collective-permute-start.21) | collective-permute-done | bytes 524320 | tf_op jit(solution)/shard_map/ppermute | solution.py:468
  208.8 9.8 %fusion.69.refs_5_.refs_4_ = f32[1024,1024]{1,0:T(8,128)} fusion(bf16[2048,1024]{1,0:T(8,128)(2,1)S(1)} %constant_dynamic-update-slice_fusion.21, bf16[1024,2048]{0,1:T(8,128)(2,1)} %constant_dynamic-update-slice_fusion.33), kind=kOutput, calls=%fused_computation.229 | convolution fusion | flops 4294967296 | bytes 12582912 | tf_op jit(solution)/shard_map/dot_general | solution.py:27
  239.7 6.9 %mix.1 = (bf16[1024,1024]{1,0:T(8,128)(2,1)S(1)}, f32[8,1024]{1,0:T(8,128)S(1)}) custom-call(s32[1]{0:T(128)} %constant.205.clone.1.place_ref, bf16[1280,1024]{1,0:T(8,128)(2,1)} %get-tuple-element.109.refs_0_, f32[4,8,512]{2,1,0:T(8,128)S(1)} %select_maximum_fusion.refs_2_.refs_1_.refs_4_, f32[16,1024]{1,0:T(8,128)S(1)} %reshape.687.refs_4_.refs_2_.refs_3_, ...), custom_call_target="tpu_custom_call" | custom-call | tf_op jit(solution)/shard_map/mix/pallas_call | solution.py:360
  254.7 8.3 %gate.1 = (bf16[1024,1024]{1,0:T(8,128)(2,1)S(1)}, bf16[1024,1024]{1,0:T(8,128)(2,1)}, bf16[1024,1024]{1,0:T(8,128)(2,1)}, bf16[4,1024,128]{2,1,0:T(8,128)(2,1)S(1)}) custom-call(s32[1]{0:T(128)} %constant.205.clone.1.place_ref, bf16[1280,1024]{1,0:T(8,128)(2,1)} %get-tuple-element.109.refs_0_, f32[4,8,512]{2,1,0:T(8,128)S(1)} %select_maximum_fusion.refs_2_.refs_1_.refs_4_, ...), custom_call_target="tpu_custom_call" | custom-call | tf_op jit(solution)/shard_map/gate/pallas_call | solution.py:360
  267.0 6.3 %convolution_convert_fusion.4 = bf16[1024,2048]{1,0:T(8,128)(2,1)} fusion(bf16[1024,1024]{1,0:T(8,128)(2,1)S(1)} %get-tuple-element.152, bf16[1024,2048]{1,0:T(8,128)(2,1)S(1)} %copy-done.32), kind=kOutput, calls=%fused_computation.13 | convolution fusion | flops 4297064448 | bytes 10485760 | tf_op jit(solution)/shard_map/dot_general | solution.py:27
  274.3 9.5 %convolution_convert_fusion.3 = bf16[2048,1024]{1,0:T(8,128)(2,1)} fusion(bf16[1024,2048]{0,1:T(8,128)(2,1)} %constant_dynamic-update-slice_fusion.33, bf16[1024,1024]{1,0:T(8,128)(2,1)} %get-tuple-element.157), kind=kOutput, calls=%fused_computation.12 | convolution fusion | flops 4297064448 | bytes 10485760 | tf_op jit(solution)/shard_map/dot_general | solution.py:27
  285.1 12.3 %within_back.1 = (f32[1024,1024]{1,0:T(8,128)}, f32[256,1024]{1,0:T(8,128)S(1)}, f32[48,1024]{1,0:T(8,128)S(1)}) custom-call(s32[1]{0:T(128)} %constant.205.clone.1.place_ref, bf16[1280,1024]{1,0:T(8,128)(2,1)} %get-tuple-element.109.refs_0_, f32[4,8,512]{2,1,0:T(8,128)S(1)} %select_maximum_fusion.refs_2_.refs_1_.refs_4_, ...), custom_call_target="tpu_custom_call" | custom-call | tf_op jit(solution)/shard_map/within_back/pallas_call | solution.py:360
  300.4 6.1 %convolution_convert_fusion.2 = bf16[1024,2048]{1,0:T(8,128)(2,1)} fusion(bf16[1024,1024]{1,0:T(8,128)(2,1)S(1)} %copy-done.12, bf16[1024,2048]{1,0:T(8,128)(2,1)S(1)} %copy-done.34), kind=kOutput, calls=%fused_computation.11 | convolution fusion | flops 4297064448 | bytes 10485760 | tf_op jit(solution)/shard_map/dot_general | solution.py:27
  306.5 21.7 %collective-permute-done.42 = bf16[4,8,64,128]{3,2,1,0:T(8,128)(2,1)} collective-permute-done((bf16[4,8,64,128]{3,2,1,0:T(8,128)(2,1)S(1)}, bf16[4,8,64,128]{3,2,1,0:T(8,128)(2,1)}, u32[]{:S(2)}, u32[]{:S(2)}) %collective-permute-start.42) | collective-permute-done | bytes 524320 | tf_op jit(solution)/shard_map/ppermute | solution.py:468
  338.8 9.5 %state_back.1 = (bf16[1280,1024]{1,0:T(8,128)(2,1)}, f32[32,1024]{1,0:T(8,128)S(1)}, bf16[1280,128]{1,0:T(8,128)(2,1)S(1)}) custom-call(s32[1]{0:T(128)} %constant.205.clone.1.place_ref, bf16[1280,1024]{1,0:T(8,128)(2,1)} %get-tuple-element.109.refs_0_, bf16[1280,1024]{1,0:T(8,128)(2,1)} %get-tuple-element.142.refs_1_, ...), custom_call_target="tpu_custom_call" | custom-call | tf_op jit(solution)/shard_map/state_back/pallas_call | solution.py:360
  350.0 6.2 %convolution_convert_fusion.1 = bf16[1024,2048]{1,0:T(8,128)(2,1)} fusion(bf16[1024,1024]{1,0:T(8,128)(2,1)S(1)} %copy-done.60, bf16[2048,1024]{1,0:T(8,128)(2,1)S(1)} %copy-done.30), kind=kOutput, calls=%fused_computation.10 | convolution fusion | flops 4297064448 | bytes 10485760 | tf_op jit(solution)/shard_map/dot_general | solution.py:27
  356.2 13.8 %conv_back.1 = (bf16[1280,1024]{1,0:T(8,128)(2,1)S(1)}, f32[5,1280,128]{2,1,0:T(8,128)}) custom-call(s32[1]{0:T(128)} %constant.205.clone.1.place_ref, bf16[1280,1024]{1,0:T(8,128)(2,1)} %fusion.4.refs_0_, bf16[1280,128]{1,0:T(8,128)(2,1)S(1)} %copy-done.6, bf16[1280,1024]{1,0:T(8,128)(2,1)} %get-tuple-element.158.refs_2_, ...), custom_call_target="tpu_custom_call" | custom-call | tf_op jit(solution)/shard_map/conv_back/pallas_call | solution.py:360
  370.0 9.9 %convolution_convert_fusion = bf16[2048,1296]{0,1:T(8,128)(2,1)} fusion(bf16[1024,2048]{0,1:T(8,128)(2,1)} %constant_dynamic-update-slice_fusion.33, bf16[16,1024]{1,0:T(8,128)(2,1)S(1)} %slice.333, bf16[1280,1024]{1,0:T(8,128)(2,1)S(1)} %get-tuple-element.159), kind=kOutput, calls=%fused_computation | convolution fusion | flops 5443780608 | bytes 12156928 | tf_op jit(solution)/shard_map/dot_general | solution.py:27
  379.9 9.3 %reduce-scatter.6.cloned.1.call-done = bf16[256,1024]{1,0:T(8,128)(2,1)} async-done(((bf16[2048,1024]{1,0:T(8,128)(2,1)}), bf16[256,1024]{1,0:T(8,128)(2,1)}) %reduce-scatter.6.cloned.1.call-update) | async-done | bytes 524304 | tf_op jit(solution)/shard_map/reduce_scatter | solution.py:785
  396.0 7.6 %add_convert_fusion.1 = bf16[1024,1024]{1,0:T(8,128)(2,1)} fusion(bf16[1024,2048]{1,0:T(8,128)(2,1)S(1)} %copy-done.69, bf16[1296,1024]{1,0:T(8,128)(2,1)S(1)} %pad_maximum_fusion, bf16[2048,1296]{1,0:T(8,128)(2,1)} %constant_dynamic-update-slice_fusion.38), kind=kOutput, calls=%fused_computation.8 | convolution fusion | flops 2721054720 | bytes 9732096 | tf_op jit(solution)/shard_map/dot_general | solution.py:27
  409.3 6.9 %add_convert_fusion = bf16[1024,1024]{1,0:T(8,128)(2,1)} fusion(bf16[1024,2048]{1,0:T(8,128)(2,1)} %convolution_convert_fusion.1, bf16[1296,1024]{1,0:T(8,128)(2,1)S(1)} %copy-done.36, bf16[2048,1296]{1,0:T(8,128)(2,1)} %constant_dynamic-update-slice_fusion.38), kind=kOutput, calls=%fused_computation.6 | convolution fusion | flops 2721054720 | bytes 9732096 | tf_op jit(solution)/shard_map/dot_general | solution.py:27
  418.7 14.5 %all-to-all-done.3 = bf16[4,256,1024]{2,1,0:T(8,128)(2,1)} async-done(((bf16[4,256,1024]{2,1,0:T(8,128)(2,1)}), bf16[4,256,1024]{2,1,0:T(8,128)(2,1)}, u32[]{:S(2)}, u32[]{:S(2)}) %all-to-all-start.3) | async-done | bytes 2097184 | tf_op jit(solution)/shard_map/all_to_all | solution.py:778
  448.2 8.0 %all-to-all-done.4 = f32[8,56,128]{2,1,0:T(8,128)S(1)} async-done(((f32[8,56,128]{2,1,0:T(8,128)}), f32[8,56,128]{2,1,0:T(8,128)S(1)}, u32[]{:S(2)}, u32[]{:S(2)}) %all-to-all-start.4) | async-done | bytes 229408 | tf_op jit(solution)/shard_map/all_to_all | solution.py:855
  480.7 11.7 %collective-permute-done.54 = bf16[1,128,2048]{2,1,0:T(8,128)(2,1)S(1)} collective-permute-done((bf16[1,128,2048]{2,1,0:T(8,128)(2,1)S(1)}, bf16[1,128,2048]{2,1,0:T(8,128)(2,1)S(1)}, u32[]{:S(2)}, u32[]{:S(2)}) %collective-permute-start.54) | collective-permute-done | bytes 524320 | tf_op jit(solution)/shard_map/ppermute | solution.py:468
  (475 shorter events, 269.3 us)
Async XLA Ops:
  38.9 27.9 %all-to-all-start.2 = ((bf16[32,32,128]{2,1,0:T(8,128)(2,1)}), bf16[32,32,128]{2,1,0:T(8,128)(2,1)S(1)}, u32[]{:S(2)}, u32[]{:S(2)}) async-start(bf16[32,32,128]{2,1,0:T(8,128)(2,1)} %bitcast.17), calls=%async_computation.2 | async-start | bytes 524288 | tf_op jit(solution)/shard_map/all_to_all | solution.py:582
  43.8 289.5 %reduce-scatter.4.cloned.1.call-start = ((), (), s32[]{:S(2)}) async-start(), calls=%async_computation.10 | async-start | bytes 5242880 | tf_op jit(solution)/shard_map/reduce_scatter | solution.py:790
  44.7 23.6 %collective-permute-start.1 = (bf16[256,1280]{1,0:T(8,128)(2,1)S(1)}, bf16[256,1280]{1,0:T(8,128)(2,1)}, u32[]{:S(2)}, u32[]{:S(2)}) collective-permute-start(bf16[256,1280]{1,0:T(8,128)(2,1)S(1)} %bitcast.193), channel_id=1, source_target_pairs={{0,2},{1,3},{2,4},{3,5},{4,6},{5,7},{6,0},{7,1},{8,10},{9,11},{10,... | collective-permute-start | bytes 1966088 | tf_op jit(solution)/shard_map/ppermute | solution.py:468
  46.5 21.8 %collective-permute-start.2 = (bf16[256,1280]{1,0:T(8,128)(2,1)S(1)}, bf16[256,1280]{1,0:T(8,128)(2,1)}, u32[]{:S(2)}, u32[]{:S(2)}) collective-permute-start(bf16[256,1280]{1,0:T(8,128)(2,1)S(1)} %bitcast.194), channel_id=1, source_target_pairs={{0,1},{1,0},{2,3},{3,2},{4,5},{5,4},{6,7},{7,6},{8,9},{9,8},{10,11... | collective-permute-start | bytes 1966088 | tf_op jit(solution)/shard_map/ppermute | solution.py:468
  71.5 32.2 %collective-permute-start.5 = (bf16[256,2048]{0,1:T(8,128)(2,1)}, bf16[256,2048]{0,1:T(8,128)(2,1)S(1)}, u32[]{:S(2)}, u32[]{:S(2)}) collective-permute-start(bf16[256,2048]{0,1:T(8,128)(2,1)} %bitcast.22), channel_id=1, source_target_pairs={{0,8},{8,0},{16,24},{24,16},{1,9},{9,1},{17,25},{25,17},{2,10},{10... | collective-permute-start | bytes 3145736 | tf_op jit(solution)/shard_map/ppermute | solution.py:465
  71.5 32.2 %collective-permute-start.6 = (bf16[256,2048]{0,1:T(8,128)(2,1)}, bf16[256,2048]{0,1:T(8,128)(2,1)}, u32[]{:S(2)}, u32[]{:S(2)}) collective-permute-start(bf16[256,2048]{0,1:T(8,128)(2,1)} %bitcast.22), channel_id=1, source_target_pairs={{0,16},{8,24},{16,0},{24,8},{1,17},{9,25},{17,1},{25,9},{2,18},{10... | collective-permute-start | bytes 3145736 | tf_op jit(solution)/shard_map/ppermute | solution.py:465
  73.0 19.6 %collective-permute-start.3 = (bf16[256,1280]{1,0:T(8,128)(2,1)}, bf16[256,1280]{1,0:T(8,128)(2,1)}, u32[]{:S(2)}, u32[]{:S(2)}) collective-permute-start(bf16[256,1280]{1,0:T(8,128)(2,1)} %collective-permute-done.1), channel_id=1, source_target_pairs={{0,2},{1,3},{2,4},{3,5},{4,6},{5,7},{6,0},{7,1},{8,10},{9,11},{10,... | collective-permute-start | bytes 1966088 | tf_op jit(solution)/shard_map/ppermute | solution.py:468
  73.0 26.5 %collective-permute-start.4 = (bf16[256,1280]{1,0:T(8,128)(2,1)}, bf16[256,1280]{1,0:T(8,128)(2,1)}, u32[]{:S(2)}, u32[]{:S(2)}) collective-permute-start(bf16[256,1280]{1,0:T(8,128)(2,1)} %collective-permute-done.1), channel_id=1, source_target_pairs={{0,1},{1,0},{2,3},{3,2},{4,5},{5,4},{6,7},{7,6},{8,9},{9,8},{10,11... | collective-permute-start | bytes 1966088 | tf_op jit(solution)/shard_map/ppermute | solution.py:468
  74.5 29.2 %collective-permute-start.7 = (bf16[128,2048]{1,0:T(8,128)(2,1)}, bf16[128,2048]{1,0:T(8,128)(2,1)S(1)}, u32[]{:S(2)}, u32[]{:S(2)}) collective-permute-start(bf16[128,2048]{1,0:T(8,128)(2,1)} %collective-permute-done), channel_id=1, source_target_pairs={{0,2},{1,3},{2,4},{3,5},{4,6},{5,7},{6,0},{7,1},{8,10},{9,11},{10,... | collective-permute-start | bytes 1572872 | tf_op jit(solution)/shard_map/ppermute | solution.py:468
  103.7 22.1 %collective-permute-start.8 = (bf16[256,1280]{1,0:T(8,128)(2,1)}, bf16[256,1280]{1,0:T(8,128)(2,1)}, u32[]{:S(2)}, u32[]{:S(2)}) collective-permute-start(bf16[256,1280]{1,0:T(8,128)(2,1)} %collective-permute-done.3), channel_id=1, source_target_pairs={{0,1},{1,0},{2,3},{3,2},{4,5},{5,4},{6,7},{7,6},{8,9},{9,8},{10,11... | collective-permute-start | bytes 1966088 | tf_op jit(solution)/shard_map/ppermute | solution.py:468
  103.9 21.9 %collective-permute-start.9 = (bf16[256,1280]{1,0:T(8,128)(2,1)}, bf16[256,1280]{1,0:T(8,128)(2,1)}, u32[]{:S(2)}, u32[]{:S(2)}) collective-permute-start(bf16[256,1280]{1,0:T(8,128)(2,1)} %collective-permute-done.3), channel_id=1, source_target_pairs={{0,2},{1,3},{2,4},{3,5},{4,6},{5,7},{6,0},{7,1},{8,10},{9,11},{10,... | collective-permute-start | bytes 1966088 | tf_op jit(solution)/shard_map/ppermute | solution.py:468
  121.6 26.9 %collective-permute-start.13 = (bf16[16,2048]{1,0:T(8,128)(2,1)S(1)}, bf16[16,2048]{1,0:T(8,128)(2,1)S(1)}, u32[]{:S(2)}, u32[]{:S(2)}) collective-permute-start(bf16[16,2048]{1,0:T(8,128)(2,1)S(1)} %reshape.685), channel_id=1, source_target_pairs={{0,1},{1,2},{2,3},{3,4},{4,5},{5,6},{6,7},{8,9},{9,10},{10,11},{11... | collective-permute-start | bytes 196616 | tf_op jit(solution)/shard_map/ppermute | solution.py:468
  129.5 38.8 %collective-permute-start.16 = (bf16[256,2048]{1,0:T(8,128)(2,1)}, bf16[256,2048]{1,0:T(8,128)(2,1)}, u32[]{:S(2)}, u32[]{:S(2)}) collective-permute-start(bf16[256,2048]{1,0:T(8,128)(2,1)} %param.25), channel_id=1, source_target_pairs={{0,8},{8,0},{16,24},{24,16},{1,9},{9,1},{17,25},{25,17},{2,10},{10... | collective-permute-start | bytes 3145736 | tf_op jit(solution)/shard_map/ppermute | solution.py:465
  130.7 37.6 %collective-permute-start.17 = (bf16[256,2048]{1,0:T(8,128)(2,1)}, bf16[256,2048]{1,0:T(8,128)(2,1)}, u32[]{:S(2)}, u32[]{:S(2)}) collective-permute-start(bf16[256,2048]{1,0:T(8,128)(2,1)} %param.25), channel_id=1, source_target_pairs={{0,16},{8,24},{16,0},{24,8},{1,17},{9,25},{17,1},{25,9},{2,18},{10... | collective-permute-start | bytes 3145736 | tf_op jit(solution)/shard_map/ppermute | solution.py:465
  148.6 19.7 %collective-permute-start.15 = (bf16[256,1024]{1,0:T(8,128)(2,1)}, bf16[256,1024]{1,0:T(8,128)(2,1)}, u32[]{:S(2)}, u32[]{:S(2)}) collective-permute-start(bf16[256,1024]{1,0:T(8,128)(2,1)} %collective-permute-done.14), channel_id=1, source_target_pairs={{0,2},{1,3},{2,4},{3,5},{4,6},{5,7},{6,0},{7,1},{8,10},{9,11},{10,... | collective-permute-start | bytes 1572872 | tf_op jit(solution)/shard_map/ppermute | solution.py:468
  178.2 20.8 %collective-permute-start.21 = (bf16[256,1024]{1,0:T(8,128)(2,1)}, bf16[256,1024]{1,0:T(8,128)(2,1)S(1)}, u32[]{:S(2)}, u32[]{:S(2)}) collective-permute-start(bf16[256,1024]{1,0:T(8,128)(2,1)} %collective-permute-done.15), channel_id=1, source_target_pairs={{0,2},{1,3},{2,4},{3,5},{4,6},{5,7},{6,0},{7,1},{8,10},{9,11},{10,... | collective-permute-start | bytes 1572872 | tf_op jit(solution)/shard_map/ppermute | solution.py:468
  178.2 20.7 %collective-permute-start.22 = (bf16[128,2048]{1,0:T(8,128)(2,1)S(1)}, bf16[128,2048]{1,0:T(8,128)(2,1)S(1)}, u32[]{:S(2)}, u32[]{:S(2)}) collective-permute-start(bf16[128,2048]{1,0:T(8,128)(2,1)S(1)} %slice.247), channel_id=1, source_target_pairs={{0,16},{8,24},{16,0},{24,8},{1,17},{9,25},{17,1},{25,9},{2,18},{10... | collective-permute-start | bytes 1572872 | tf_op jit(solution)/shard_map/ppermute | solution.py:465
  273.4 115.8 %reduce-scatter.6.cloned.1.call-start = ((), (), s32[]{:S(2)}) async-start(), calls=%async_computation.11 | async-start | bytes 4718592 | tf_op jit(solution)/shard_map/reduce_scatter | solution.py:785
  299.1 29.1 %collective-permute-start.42 = (bf16[4,8,64,128]{3,2,1,0:T(8,128)(2,1)S(1)}, bf16[4,8,64,128]{3,2,1,0:T(8,128)(2,1)}, u32[]{:S(2)}, u32[]{:S(2)}) collective-permute-start(bf16[4,8,64,128]{3,2,1,0:T(8,128)(2,1)S(1)} %add_convert_fusion.5), channel_id=1, source_target_pairs={{2,0},{3,1},{10,8},{11,9},{18,16},{19,17},{26,24},{27,25}} | collective-permute-start | bytes 1572872 | tf_op jit(solution)/shard_map/ppermute | solution.py:468
  333.3 175.1 %reduce-scatter.8.cloned.1.call-start = ((), (), s32[]{:S(2)}) async-start(), calls=%async_computation.12 | async-start | bytes 5971968 | tf_op jit(solution)/shard_map/reduce_scatter | solution.py:785
  393.7 22.5 %collective-permute-start.51 = (bf16[1,4,128,2048]{3,2,1,0:T(8,128)(2,1)}, bf16[1,4,128,2048]{3,2,1,0:T(8,128)(2,1)}, u32[]{:S(2)}, u32[]{:S(2)}) collective-permute-start(bf16[1,4,128,2048]{3,2,1,0:T(8,128)(2,1)} %get-tuple-element.235), channel_id=1, source_target_pairs={{0,1},{1,0},{2,3},{3,2},{4,5},{5,4},{6,7},{7,6},{8,9},{9,8},{10,11... | collective-permute-start | bytes 6291464 | tf_op jit(solution)/shard_map/ppermute | solution.py:468
  403.6 29.6 %all-to-all-start.3 = ((bf16[4,256,1024]{2,1,0:T(8,128)(2,1)}), bf16[4,256,1024]{2,1,0:T(8,128)(2,1)}, u32[]{:S(2)}, u32[]{:S(2)}) async-start(bf16[4,256,1024]{2,1,0:T(8,128)(2,1)} %bitcast.198), calls=%async_computation.4 | async-start | bytes 4194304 | tf_op jit(solution)/shard_map/all_to_all | solution.py:778
  418.3 41.4 %collective-permute-start.52 = (bf16[1,128,2048]{2,1,0:T(8,128)(2,1)}, bf16[1,128,2048]{2,1,0:T(8,128)(2,1)}, u32[]{:S(2)}, u32[]{:S(2)}) collective-permute-start(bf16[1,128,2048]{2,1,0:T(8,128)(2,1)} %fusion.40), channel_id=1, source_target_pairs={{2,0},{3,1},{4,2},{5,3},{6,4},{7,5},{0,6},{1,7},{10,8},{11,9},{12,... | collective-permute-start | bytes 1572872 | tf_op jit(solution)/shard_map/ppermute | solution.py:468
  467.8 28.8 %all-to-all-start.5 = ((bf16[4,256,1024]{2,1,0:T(8,128)(2,1)}), bf16[4,256,1024]{2,1,0:T(8,128)(2,1)}, u32[]{:S(2)}, u32[]{:S(2)}) async-start(bf16[4,256,1024]{2,1,0:T(8,128)(2,1)} %bitcast.197), calls=%async_computation.6 | async-start | bytes 4194304 | tf_op jit(solution)/shard_map/all_to_all | solution.py:778
  (112 other events, 1507.7 us)
Sparse Core Ops, SparseCore 0:
  273.5 59.7 reduce-scatter.3
  335.7 53.4 reduce-scatter.5
  391.6 73.7 reduce-scatter.7
